TPU v7x, 32 devices: a whole 2x2x4 slice. The times are simulated.
32 devices in a mesh: rep: 4 (over y, core), grid: 8 (over z, x).
Axes of the slice: x: 2, y: 2, z: 4, core: 2. Of those that a mesh axis runs over, the one named last changes fastest.
Arguments:
- orbitals: bfloat16 [512, 256], P('rep'), may hold values from -6 to 6
- tiles: bfloat16 [4, 8, 6, 64, 4096], P('rep', 'grid'), may hold values from -0.75 to 0.75
- tile_block: int32 [4, 8, 6], P('rep', 'grid'), may hold values from 0 to 7, as said below
- tile_count: int32 [4, 8], P('rep', 'grid'), may hold values from 1 to 6, as said below
Outputs:
- exchange_action: float32 [512, 256], P('grid')
Inputs may be any that keep to these rules, and one draw needn't show every extreme that they name: `tile_block`: the live and empty slots of one (r, g) name distinct basis blocks. Slots at or after tile_count take no part.
All inputs are finite; a program needn't handle non-finite values.
Results may differ from a plain program's by a relative error of at most 0.00061.
Values may be sent and summed in bfloat16 or wider, within the bound.
No kernel may reach another device: no remote copies, remote signals or barrier semaphores. Data moves between devices by JAX's collectives and lax.ppermute only.
A program may use at most 64 MiB of HBM per device.

v0:
```python
import math

import jax
import jax.numpy as jnp
from jax import lax
from jax.sharding import PartitionSpec as P


def per_device(orbitals, tiles, tile_block, tile_count):
    full_orbitals = lax.all_gather(orbitals, "rep", axis=0, tiled=True)
    rep_size = lax.axis_size("rep")
    tile_width = tiles.shape[3]
    slot_total = tiles.shape[2]
    basis_rows = full_orbitals.shape[0]
    orb_count = full_orbitals.shape[1]
    fit_scale = 1.0 / math.sqrt(basis_rows)
    mix_scale = 0.25 / math.sqrt(tile_width * rep_size * orb_count)
    blocks = full_orbitals.reshape(basis_rows // tile_width, tile_width, orb_count)
    picked = jnp.take(blocks, tile_block[0, 0], axis=0)
    live_mask = (jnp.arange(slot_total, dtype=jnp.int32) < tile_count[0, 0]).astype(jnp.bfloat16)
    picked = picked * live_mask[:, None, None]
    intermed = jnp.einsum("tvk,tvj->kj", tiles[0, 0], picked, preferred_element_type=jnp.float32)
    local_rows = intermed.astype(jnp.bfloat16).reshape(tile_width, tile_width * orb_count)
    received = lax.all_to_all(local_rows, "grid", split_axis=1, concat_axis=0, tiled=True)
    fitted = fit_scale * lax.dot_general(
        received, full_orbitals, (((0,), (0,)), ((), ())), preferred_element_type=jnp.float32
    )
    fitted = fitted.astype(jnp.bfloat16)
    exchange_part = lax.psum_scatter(
        -mix_scale * jnp.dot(received, fitted, preferred_element_type=jnp.float32),
        "grid",
        scatter_dimension=0,
        tiled=True,
    )
    return lax.psum(exchange_part, "rep")


def solution(mesh):
    in_specs = (
        P("rep", None),
        P("rep", "grid", None, None, None),
        P("rep", "grid", None),
        P("rep", "grid"),
    )
    out_specs = P("grid", None)
    return jax.shard_map(
        per_device, mesh=mesh, in_specs=in_specs, out_specs=out_specs, check_vma=False
    )
```

profile of v0, /device:TPU:0, one launch (start us, length us, event | category | flops | bytes accessed | tf_op | source)
XLA Modules:
  0.0 193.6 jit_solution(1897112954188526)
XLA Ops:
  6.5 0.0 copy-start
  6.5 0.0 reduce-scatter.2.cloned.1.call-start
  7.3 0.8 fusion.10
  8.2 0.7 compare_convert_fusion
  8.8 7.4 %all_gather.3 = bf16[512,256]{1,0:T(8,128)(2,1)S(1)} all-gather(bf16[128,256]{1,0:T(8,128)(2,1)} %param.4), channel_id=1, replica_groups=mesh['rep'=4,'grid'=8] {'rep'}, dimensions={0}, use_global_device_ids=true | all-gather | bytes 327680 | tf_op jit(solution)/shard_map/all_gather | solution.py:10
  16.3 1.2 gather_fusion
  17.5 0.0 copy-done
  17.5 3.6 %fusion.1 = bf16[4096,256]{0,1:T(8,128)(2,1)} fusion(bf16[1,1,6,64,4096]{4,3,2,1,0:T(8,128)(2,1)S(1)} %copy-done, bf16[6,64,256]{2,1,0:T(8,128)(2,1)} %gather_fusion, pred[6]{0:T(512)(128)(4,1)S(1)} %get-tuple-element.6, bf16[6]{0:T(256)(128)(2,1)S(1)} %get-tuple-element.5), kind=kOutput, calls=%fused_computation.3 | convolution fusion | flops 806551552 | bytes 5439506 | tf_op jit(solution)/shard_map/tvk,tvj->kj/dot_general | solution.py:22
  21.1 4.1 %copy.7 = bf16[4096,256]{1,0:T(8,128)(2,1)} copy(bf16[4096,256]{0,1:T(8,128)(2,1)} %fusion.1) | data formatting | bytes 4194304 | tf_op jit(solution)/shard_map/convert_element_type | solution.py:23
  25.2 4.2 %all_to_all.14 = bf16[64,8,2048]{2,1,0:T(8,128)(2,1)} reshape(bf16[4096,256]{1,0:T(8,128)(2,1)} %copy.7) | data formatting | bytes 4194304 | tf_op jit(solution)/shard_map/all_to_all | solution.py:24
  29.4 2.7 %copy.8 = bf16[64,8,2048]{2,0,1:T(8,128)(2,1)S(1)} copy(bf16[64,8,2048]{2,1,0:T(8,128)(2,1)} %all_to_all.14) | data formatting | bytes 4194304 | tf_op jit(solution)/shard_map/all_to_all | solution.py:24
  32.1 54.4 %all_to_all.19 = bf16[64,8,2048]{2,0,1:T(8,128)(2,1)} all-to-all(bf16[64,8,2048]{2,0,1:T(8,128)(2,1)S(1)} %copy.8), channel_id=1, replica_groups=mesh['rep'=4,'grid'=8] {'grid'}, dimensions={1} | all-to-all | bytes 4194304 | tf_op jit(solution)/shard_map/all_to_all | solution.py:24
  86.6 5.0 %convolution_multiply_fusion.1 = f32[512,256]{1,0:T(8,128)} fusion(bf16[512,2048]{1,0:T(8,128)(2,1)} %bitcast.26, bf16[512,256]{1,0:T(8,128)(2,1)S(1)} %all_gather.3), kind=kOutput, calls=%fused_computation.7 | convolution fusion | flops 1074921472 | bytes 2883584 | tf_op jit(solution)/shard_map/dot_general | solution.py:30
  91.6 0.0 reduce-scatter.2.cloned.1.call-update
  91.6 0.0 all-reduce.2.cloned.1.call-start
  91.6 61.1 %reduce-scatter.2.cloned.1.call-done = f32[64,256]{1,0:T(8,128)} async-done(((f32[512,256]{1,0:T(8,128)}), f32[64,256]{1,0:T(8,128)}) %reduce-scatter.2.cloned.1.call-update) | async-done | bytes 65552 | tf_op jit(solution)/shard_map/reduce_scatter | solution.py:29
  152.8 0.0 all-reduce.2.cloned.1.call-update
  152.8 32.5 %all-reduce.2.cloned.1.call-done = f32[64,256]{1,0:T(8,128)} async-done(((f32[64,256]{1,0:T(8,128)}), f32[64,256]{1,0:T(8,128)}) %all-reduce.2.cloned.1.call-update) | async-done | bytes 65552 | tf_op jit(solution)/shard_map/psum | solution.py:35
  185.3 1.5 copy.11
  (1 shorter events, 0.0 us)
Async XLA Ops:
  6.5 11.0 %copy-start = (bf16[1,1,6,64,4096]{4,3,2,1,0:T(8,128)(2,1)S(1)}, bf16[1,1,6,64,4096]{4,3,2,1,0:T(8,128)(2,1)}, u32[]{:S(2)}) copy-start(bf16[1,1,6,64,4096]{4,3,2,1,0:T(8,128)(2,1)} %param.5) | copy-start | bytes 9437188
  6.5 146.2 %reduce-scatter.2.cloned.1.call-start = ((), (), s32[]{:S(2)}) async-start(), calls=%async_computation.2 | async-start | bytes 589824 | tf_op jit(solution)/shard_map/reduce_scatter | solution.py:29
  91.6 93.7 %all-reduce.2.cloned.1.call-start = ((), (), s32[]{:S(2)}) async-start(), calls=%async_computation.3 | async-start | bytes 131072 | tf_op jit(solution)/shard_map/psum | solution.py:35
Sparse Core Ops, SparseCore 0:
  91.7 61.0 reduce-scatter.1
  155.2 30.0 all-reduce.1
where the time goes:
time: 194 us
  waiting for transfers between devices  93.6 us (48%)
  blocking collectives  61.9 us (32%)
  between operations  14.2 us (7%)
  local copies, waits for them, and re-layouts  13.7 us (7%)
  matrix products  8.61 us (4%)
    reduce_scatter x1, waiting for transfers between devices, per_device(): lax.psum_scatter(-mix_scale * jnp.dot(received, fitted, preferred_element...  61.1 us
    all_to_all x1, blocking collectives, per_device(): lax.all_to_all(local_rows, 'grid', split_axis=1, concat_axis=0, tiled=True)  54.4 us
    psum x1, waiting for transfers between devices, per_device(): return lax.psum(exchange_part, 'rep')  32.5 us
    all_gather x1, blocking collectives, per_device(): full_orbitals = lax.all_gather(orbitals, 'rep', axis=0, tiled=True)  7.43 us
    all_to_all x2, local copies, waits for them, and re-layouts, per_device(): lax.all_to_all(local_rows, 'grid', split_axis=1, concat_axis=0, tiled=True)  6.94 us
    dot_general x1, matrix products, per_device(): jnp.dot(received, fitted, preferred_element_type=jnp.float32)  5 us
    convert_element_type x1, local copies, waits for them, and re-layouts, per_device(): intermed.astype(jnp.bfloat16).reshape(tile_width, tile_width * orb_count)  4.07 us
  transfers between devices with their start and end apart: 2, of which 2 were waited for; matrix products, arithmetic and copies ran while one was open for 0% of the time, Pallas kernels for 0%

commit v1 on v0

v1 whole, which is shorter than its diff:
```python
import functools
import math

import jax
import jax.numpy as jnp
from jax import lax
from jax.experimental import pallas as pl
from jax.experimental.pallas import tpu as pltpu
from jax.sharding import PartitionSpec as P

LANES = 128
SUB = 16


def contract_kernel(count_ref, block_ref, orb_ref, swap_ref, tiles_ref, out_ref, buf, picked, sems):
    slots, width, extent = tiles_ref.shape
    norb = orb_ref.shape[1]
    half = norb // 2
    parts = out_ref.shape[0]
    per_part = half // parts
    step = SUB * width
    chunks = extent // step

    def copy(at):
        lanes = pl.ds(at * step, step)
        return pltpu.make_async_copy(tiles_ref.at[:, :, lanes], buf.at[:, :, lanes], sems.at[at])

    for at in range(chunks):
        copy(at).start()
    for t in range(slots):
        row = pl.multiple_of(block_ref[0, 0, t] * width, width)
        rows = orb_ref[pl.ds(row, width), :]
        picked[t * width:(t + 1) * width, :] = jnp.where(t < count_ref[0, 0], rows, jnp.zeros_like(rows))
    lhs = picked[...].T
    swap = swap_ref[...]
    low = lax.broadcasted_iota(jnp.int32, (half, LANES), 1) < width
    for at in range(chunks):
        copy(at).wait()
        lanes = slice(at * step, (at + 1) * step)
        rhs = buf[:, :, lanes].reshape(slots * width, step)
        acc = jnp.dot(lhs, rhs, preferred_element_type=jnp.float32)
        per_mu = []
        for q in range(step // LANES):
            a = acc[:half, q * LANES:(q + 1) * LANES]
            b = acc[half:, q * LANES:(q + 1) * LANES]
            per_mu.append(jnp.where(low, a, pltpu.roll(b, width, 1)).astype(jnp.bfloat16))
            per_mu.append(jnp.where(low, pltpu.roll(a, width, 1), b).astype(jnp.bfloat16))
        for s in range(half // (2 * SUB)):
            r0 = 2 * s * SUB
            left = jnp.concatenate([m[r0:r0 + SUB] for m in per_mu], axis=0)
            right = jnp.concatenate([m[r0 + SUB:r0 + 2 * SUB] for m in per_mu], axis=0)
            moved = jnp.dot(swap, jnp.concatenate([left, right], axis=1), preferred_element_type=jnp.float32)
            moved = moved.astype(jnp.bfloat16)
            for side in range(2):
                for k in range(SUB):
                    i_lo = r0 + side * SUB + k
                    h, l = divmod(i_lo, per_part)
                    out_ref[h, at * SUB:(at + 1) * SUB, l * LANES:(l + 1) * LANES] = moved[
                        k * SUB:(k + 1) * SUB, side * LANES:(side + 1) * LANES
                    ]


def contract(count, block, orbitals, tiles, parts):
    slots, width, extent = tiles.shape
    norb = orbitals.shape[1]
    pos = jnp.arange(SUB * SUB, dtype=jnp.int32)
    swap = (pos[None, :] == ((pos % SUB) * SUB + pos // SUB)[:, None]).astype(jnp.bfloat16)
    cols = width * norb // parts
    return pl.pallas_call(
        contract_kernel,
        out_shape=jax.ShapeDtypeStruct((parts, width, cols), jnp.bfloat16),
        in_specs=[
            pl.BlockSpec(memory_space=pltpu.SMEM),
            pl.BlockSpec(memory_space=pltpu.SMEM),
            pl.BlockSpec(memory_space=pltpu.VMEM),
            pl.BlockSpec(memory_space=pltpu.VMEM),
            pl.BlockSpec(memory_space=pl.ANY),
        ],
        out_specs=pl.BlockSpec(memory_space=pltpu.VMEM),
        scratch_shapes=[
            pltpu.VMEM((slots, width, extent), jnp.bfloat16),
            pltpu.VMEM((slots * width, norb), jnp.bfloat16),
            pltpu.SemaphoreType.DMA((extent // (SUB * width),)),
        ],
        compiler_params=pltpu.CompilerParams(vmem_limit_bytes=32 * 1024 * 1024),
        cost_estimate=pl.CostEstimate(
            flops=2 * slots * width * extent * norb, bytes_accessed=2 * slots * width * extent, transcendentals=0
        ),
    )(count, block, orbitals, swap, tiles)


def action_kernel(fit_scale, mix_scale, step, orb_ref, rows_ref, out_ref):
    orb_t = orb_ref[...].T
    for at in range(rows_ref.shape[1] // step):
        part = rows_ref[:, at * step:(at + 1) * step]
        fitted = (fit_scale * jnp.dot(orb_t, part, preferred_element_type=jnp.float32)).astype(jnp.bfloat16)
        term = lax.dot_general(part, fitted, (((1,), (1,)), ((), ())), preferred_element_type=jnp.float32)
        term = -mix_scale * term
        if at == 0:
            out_ref[...] = term
        else:
            out_ref[...] += term


def action(orbitals, rows, fit_scale, mix_scale):
    step = min(512, rows.shape[1])
    return pl.pallas_call(
        functools.partial(action_kernel, fit_scale, mix_scale, step),
        out_shape=jax.ShapeDtypeStruct(orbitals.shape, jnp.float32),
        in_specs=[pl.BlockSpec(memory_space=pltpu.VMEM)] * 2,
        out_specs=pl.BlockSpec(memory_space=pltpu.VMEM),
        compiler_params=pltpu.CompilerParams(vmem_limit_bytes=32 * 1024 * 1024),
        cost_estimate=pl.CostEstimate(
            flops=4 * rows.shape[0] * rows.shape[1] * orbitals.shape[1],
            bytes_accessed=2 * rows.shape[0] * rows.shape[1],
            transcendentals=0,
        ),
    )(orbitals, rows)


def per_device(orbitals, tiles, tile_block, tile_count):
    rep_size = lax.axis_size("rep")
    grid_size = lax.axis_size("grid")
    width = tiles.shape[3]
    norb = orbitals.shape[1]
    full = lax.all_gather(orbitals, "rep", axis=0, tiled=True)
    basis_rows = full.shape[0]
    fit_scale = 1.0 / math.sqrt(basis_rows)
    mix_scale = 0.25 / math.sqrt(width * rep_size * norb)
    local = contract(tile_count, tile_block, full, tiles[0, 0], grid_size)
    received = lax.all_to_all(local, "grid", split_axis=0, concat_axis=0, tiled=True)
    part = action(full, received.reshape(basis_rows, -1), fit_scale, mix_scale)
    shares = lax.all_to_all(part.reshape(grid_size, width, norb), "grid", split_axis=0, concat_axis=0, tiled=True)
    mine = jnp.sum(shares, axis=0)
    every = lax.all_gather(mine, "rep", axis=0, tiled=False)
    return jnp.sum(every, axis=0)


def solution(mesh):
    in_specs = (
        P("rep", None),
        P("rep", "grid", None, None, None),
        P("rep", "grid", None),
        P("rep", "grid"),
    )
    return jax.shard_map(
        per_device, mesh=mesh, in_specs=in_specs, out_specs=P("grid", None), check_vma=False
    )
```

time: 194 us -> 95.7 us (0.49)
  waiting for transfers between devices: 93.6 us -> 0 us
  blocking collectives: 61.9 us -> 85.6 us
  between operations: 14.2 us -> 0.68 us
  local copies, waits for them, and re-layouts: 13.7 us -> 2.54 us
  matrix products: 8.61 us -> 0 us
  Pallas kernels: 0 us -> 5.87 us
    reduce_scatter x1 -> x0, waiting for transfers between devices: 61.1 us -> none  [per_device(): lax.psum_scatter(-mix_scale * jnp.dot(received, fitted, preferred_element...]
    psum x1 -> x0, waiting for transfers between devices: 32.5 us -> none  [per_device(): return lax.psum(exchange_part, 'rep')]
    all_to_all x1 -> x2, blocking collectives: 54.4 us -> 72.3 us  [the longest x1 54.3 us: per_device(): lax.all_to_all(local, 'grid', split_axis=0, concat_axis=0, tiled=True)]
    dot_general x2 -> x0, matrix products: 8.61 us -> none  [the longest x1 5 us: per_device(): jnp.dot(received, fitted, preferred_element_type=jnp.float32)]
    all_to_all x2 -> x0, local copies, waits for them, and re-layouts: 6.94 us -> none  [per_device(): lax.all_to_all(local_rows, 'grid', split_axis=1, concat_axis=0, tiled=True)]
    pallas_call x0 -> x2, Pallas kernels: none -> 5.87 us  [the longest x1 4.2 us: contract(): pl.pallas_call(contract_kernel, out_shape=jax.ShapeDtypeStruct((parts, wi...]
    all_gather x1 -> x2, blocking collectives: 7.43 us -> 13.2 us  [the longest x1 7.43 us: per_device(): full = lax.all_gather(orbitals, 'rep', axis=0, tiled=True)]
    convert_element_type x1 -> x0, local copies, waits for them, and re-layouts: 4.07 us -> none  [per_device(): intermed.astype(jnp.bfloat16).reshape(tile_width, tile_width * orb_count)]
  transfers between devices with their start and end apart: 2 -> 0, of which waited for: 2 -> 0; matrix products, arithmetic and copies ran while one was open for 0% -> 0% of each run, Pallas kernels for 0% -> 0%
where the time goes in v1:
time: 95.7 us; the launch traced here: 95.5 us
  blocking collectives  85.6 us (89%)
  Pallas kernels  5.87 us (6%)
  local copies, waits for them, and re-layouts  2.54 us (3%)
    all_to_all x1, blocking collectives, per_device(): lax.all_to_all(local, 'grid', split_axis=0, concat_axis=0, tiled=True)  54.3 us
    all_to_all x1, blocking collectives, per_device(): lax.all_to_all(part.reshape(grid_size, width, norb), 'grid', split_axis=0...  18 us
    all_gather x1, blocking collectives, per_device(): full = lax.all_gather(orbitals, 'rep', axis=0, tiled=True)  7.43 us
    all_gather x1, blocking collectives, per_device(): every = lax.all_gather(mine, 'rep', axis=0, tiled=False)  5.79 us
    pallas_call x1, Pallas kernels, contract(): pl.pallas_call(contract_kernel, out_shape=jax.ShapeDtypeStruct((parts, wi...  4.2 us
    unnamed x4, local copies, waits for them, and re-layouts  2.54 us

profile of v1, /device:TPU:0, one launch (start us, length us, event | category | flops | bytes accessed | tf_op | source)
XLA Modules:
  0.0 95.5 jit_solution(9407782330714311251)
XLA Ops:
  0.7 0.1 fusion.swap_ref
  0.8 7.4 %all_gather.9.orb_ref = bf16[512,256]{1,0:T(8,128)(2,1)S(1)} all-gather(bf16[128,256]{1,0:T(8,128)(2,1)} %param.4), channel_id=1, replica_groups=mesh['rep'=4,'grid'=8] {'rep'}, dimensions={0}, use_global_device_ids=true | all-gather | bytes 327680 | tf_op jit(solution)/shard_map/all_gather | solution.py:126
  8.2 0.0 copy-start
  8.2 1.9 %copy-done = bf16[1,1,6,64,4096]{4,3,2,1,0:T(8,128)(2,1)S(1)} copy-done((bf16[1,1,6,64,4096]{4,3,2,1,0:T(8,128)(2,1)S(1)}, bf16[1,1,6,64,4096]{4,3,2,1,0:T(8,128)(2,1)}, u32[]{:S(2)}) %copy-start) | copy-done | bytes 3145752
  10.1 0.0 copy-start.1
  10.1 0.7 copy-done.1
  10.7 4.2 %shard_map.46 = bf16[8,64,2048]{2,1,0:T(8,128)(2,1)S(1)} custom-call(s32[1,1]{1,0:T(1,128)S(6)} %copy.5.count_ref, s32[1,1,6]{2,1,0:T(1,128)S(1)} %copy-done.1, bf16[512,256]{1,0:T(8,128)(2,1)S(1)} %all_gather.9.orb_ref, bf16[256,256]{1,0:T(8,128)(2,1)S(1)} %fusion.swap_ref, bf16[6,64,4096]{2,1,0:T(8,128)(2,1)S(1)} %bitcast.4), custom_call_target="tpu_custom_call" | custom-call | flops 805306368 | bytes 3145728 | tf_op jit(solution)/shard_map/pallas_call | solution.py:69
  15.0 54.3 %all_to_all.10 = bf16[8,64,2048]{2,1,0:T(8,128)(2,1)S(1)} all-to-all(bf16[8,64,2048]{2,1,0:T(8,128)(2,1)S(1)} %shard_map.46), channel_id=1, replica_groups=mesh['rep'=4,'grid'=8] {'grid'}, dimensions={0} | all-to-all | bytes 4194304 | tf_op jit(solution)/shard_map/all_to_all | solution.py:131
  69.3 1.7 %shard_map.47 = f32[512,256]{1,0:T(8,128)S(1)} custom-call(bf16[512,256]{1,0:T(8,128)(2,1)S(1)} %all_gather.9.orb_ref, bf16[512,2048]{1,0:T(8,128)(2,1)S(1)} %bitcast.5), custom_call_target="tpu_custom_call" | custom-call | flops 1073741824 | bytes 2097152 | tf_op jit(solution)/shard_map/pallas_call | solution.py:107
  70.9 18.0 %all_to_all.11 = f32[8,64,256]{2,1,0:T(8,128)S(1)} all-to-all(f32[8,64,256]{2,1,0:T(8,128)S(1)} %bitcast.6), channel_id=1, replica_groups=mesh['rep'=4,'grid'=8] {'grid'}, dimensions={0} | all-to-all | bytes 1048576 | tf_op jit(solution)/shard_map/all_to_all | solution.py:133
  89.0 5.8 %all-gather = f32[256,256]{1,0:T(8,128)S(1)} all-gather(f32[64,256]{1,0:T(8,128)S(1)} %reduce_sum.18), channel_id=2, replica_groups=mesh['rep'=4,'grid'=8] {'rep'}, dimensions={0}, use_global_device_ids=true | all-gather | bytes 327680 | tf_op jit(solution)/shard_map/all_gather | solution.py:135
  94.8 0.6 reduce_sum.19
  (2 shorter events, 0.0 us)
Async XLA Ops:
  8.2 1.9 %copy-start = (bf16[1,1,6,64,4096]{4,3,2,1,0:T(8,128)(2,1)S(1)}, bf16[1,1,6,64,4096]{4,3,2,1,0:T(8,128)(2,1)}, u32[]{:S(2)}) copy-start(bf16[1,1,6,64,4096]{4,3,2,1,0:T(8,128)(2,1)} %param.5) | copy-start | bytes 9437188
  10.1 0.7 copy-start.1

commit v2 on v1

v2 whole, which is shorter than its diff:
```python
import functools
import math

import jax
import jax.numpy as jnp
from jax import lax
from jax.experimental import pallas as pl
from jax.experimental.pallas import tpu as pltpu
from jax.sharding import PartitionSpec as P

LANES = 128
SUB = 16
VMEM_LIMIT = 24 * 1024 * 1024


def contract_kernel(group_starts, place, skip, count, block_hbm, orb_ref, tiles_hbm, *refs):
    outs, (buf, picked, turned, block, sems, block_sem) = refs[skip:-6], refs[-6:]
    slots, width, extent = tiles_hbm.shape[2:]
    half = orb_ref.shape[1] // 2
    step = SUB * width
    chunks = extent // step


    def copy(at):
        lanes = pl.ds(at * step, step)
        return pltpu.make_async_copy(tiles_hbm.at[0, 0, :, :, lanes], buf.at[:, :, lanes], sems.at[at])

    block_copy = pltpu.make_async_copy(block_hbm, block, block_sem.at[0])
    block_copy.start()
    for at in range(chunks):
        copy(at).start()
    row_at = lax.broadcasted_iota(jnp.int32, (SUB * SUB, SUB * SUB), 0)
    col_at = lax.broadcasted_iota(jnp.int32, (SUB * SUB, SUB * SUB), 1)
    swap = (col_at == (row_at % SUB) * SUB + row_at // SUB).astype(jnp.bfloat16)
    low = lax.broadcasted_iota(jnp.int32, (SUB, LANES), 1) < width
    block_copy.wait()
    for t in range(slots):
        row = pl.multiple_of(block[0, 0, t] * width, width)
        rows = orb_ref[pl.ds(row, width), :]
        picked[t * width:(t + 1) * width, :] = jnp.where(t < count[0, 0], rows, jnp.zeros_like(rows))
    turned[...] = picked[...].T
    starts = group_starts()
    groups = len(starts)
    lhs = jnp.concatenate(
        [turned[pl.ds(pl.multiple_of(at, SUB), SUB), :] for at in starts]
        + [turned[pl.ds(pl.multiple_of(half + at, SUB), SUB), :] for at in starts],
        axis=0,
    )
    for at in range(chunks):
        copy(at).wait()
        rhs = buf[:, :, at * step:(at + 1) * step].reshape(slots * width, step)
        acc = jnp.dot(lhs, rhs, preferred_element_type=jnp.float32)
        for s in range(0, groups, 2):
            sides = []
            for g in (s, s + 1):
                per_mu = []
                for q in range(step // LANES):
                    a = acc[g * SUB:(g + 1) * SUB, q * LANES:(q + 1) * LANES]
                    b = acc[(groups + g) * SUB:(groups + g + 1) * SUB, q * LANES:(q + 1) * LANES]
                    per_mu.append(jnp.where(low, a, pltpu.roll(b, width, 1)).astype(jnp.bfloat16))
                    per_mu.append(jnp.where(low, pltpu.roll(a, width, 1), b).astype(jnp.bfloat16))
                sides.append(jnp.concatenate(per_mu, axis=0))
            moved = jnp.dot(swap, jnp.concatenate(sides, axis=1), preferred_element_type=jnp.float32)
            moved = moved.astype(jnp.bfloat16)
            for side in range(2):
                for k in range(SUB):
                    which, part, col = place(s + side, k)
                    outs[which][part, at * SUB:(at + 1) * SUB, col * LANES:(col + 1) * LANES] = moved[
                        k * SUB:(k + 1) * SUB, side * LANES:(side + 1) * LANES
                    ]


def in_hbm(x):
    return pltpu.with_memory_space_constraint(x, pltpu.HBM)


def contract(group_starts, place, out_shapes, count, block, orbitals, tiles, after=None):
    later = [] if after is None else [after]
    slots, width, extent = tiles.shape[2:]
    norb = orbitals.shape[1]
    made = sum(math.prod(shape) for shape in out_shapes)
    return pl.pallas_call(
        functools.partial(contract_kernel, group_starts, place, len(later)),
        out_shape=[jax.ShapeDtypeStruct(shape, jnp.bfloat16) for shape in out_shapes],
        in_specs=[
            pl.BlockSpec(memory_space=pltpu.SMEM),
            pl.BlockSpec(memory_space=pltpu.HBM),
            pl.BlockSpec(memory_space=pltpu.VMEM),
            pl.BlockSpec(memory_space=pltpu.HBM),
        ]
        + [pl.BlockSpec(memory_space=pl.ANY)] * len(later),
        out_specs=[pl.BlockSpec(memory_space=pltpu.VMEM)] * len(out_shapes),
        scratch_shapes=[
            pltpu.VMEM((slots, width, extent), jnp.bfloat16),
            pltpu.VMEM((slots * width, norb), jnp.bfloat16),
            pltpu.VMEM((norb, slots * width), jnp.bfloat16),
            pltpu.SMEM(block.shape, jnp.int32),
            pltpu.SemaphoreType.DMA((extent // (SUB * width),)),
            pltpu.SemaphoreType.DMA((1,)),
        ],
        compiler_params=pltpu.CompilerParams(vmem_limit_bytes=VMEM_LIMIT),
        cost_estimate=pl.CostEstimate(
            flops=2 * slots * width * made, bytes_accessed=2 * slots * width * extent + 2 * made, transcendentals=0
        ),
    )(count, in_hbm(block), orbitals, in_hbm(tiles), *later)


def orbital_rows(orb_ref, width, ids):
    rows = [orb_ref[pl.ds(pl.multiple_of(b * width, width), width), :] for b in ids]
    return jnp.concatenate(rows, axis=0).T


def joined(refs, lanes=slice(None)):
    return jnp.concatenate([ref[:, :, lanes].reshape(-1, ref[:, :, lanes].shape[2]) for ref in refs], axis=0)


def fit_kernel(step, ids, orb_ref, *refs):
    rows, out_ref = refs[:-1], refs[-1]
    turned = orbital_rows(orb_ref, rows[0].shape[1], ids())
    for at in range(out_ref.shape[1] // step):
        lanes = slice(at * step, (at + 1) * step)
        out_ref[:, lanes] = jnp.dot(turned, joined(rows, lanes), preferred_element_type=jnp.float32)


def fit(orbitals, rows, ids):
    width, cols = rows[0].shape[1:]
    number = sum(each.shape[0] for each in rows)
    norb = orbitals.shape[1]
    return pl.pallas_call(
        functools.partial(fit_kernel, min(512, cols), ids),
        out_shape=jax.ShapeDtypeStruct((norb, cols), jnp.float32),
        in_specs=[pl.BlockSpec(memory_space=pltpu.VMEM)] * (1 + len(rows)),
        out_specs=pl.BlockSpec(memory_space=pltpu.VMEM),
        compiler_params=pltpu.CompilerParams(vmem_limit_bytes=VMEM_LIMIT),
        cost_estimate=pl.CostEstimate(
            flops=2 * number * width * cols * norb,
            bytes_accessed=2 * number * width * cols + 4 * norb * cols,
            transcendentals=0,
        ),
    )(orbitals, *rows)


def action_kernel(fit_scale, mix_scale, step, early_ids, late_ids, n_early, fitted_ref, orb_ref, *refs):
    early, late, (keep_ref, send_ref, fitted) = refs[:n_early], refs[n_early:-3], refs[-3:]
    width, cols = early[0].shape[1:]
    norb = orb_ref.shape[1]
    upper = lax.axis_index("rep") % 2 == 1
    if late:
        turned = orbital_rows(orb_ref, width, late_ids())
    for at in range(cols // step):
        lanes = slice(at * step, (at + 1) * step)
        total = fitted_ref[:, lanes]
        if late:
            total = total + jnp.dot(turned, joined(late, lanes), preferred_element_type=jnp.float32)
        fitted[:, lanes] = (fit_scale * total).astype(jnp.bfloat16)
    parts = [(early_ids(), early)]
    if late:
        parts.append((late_ids(), late))
    for ids, rows in parts:
        term = lax.dot_general(joined(rows), fitted[...], (((1,), (1,)), ((), ())), preferred_element_type=jnp.float32)
        term = (-mix_scale * term).reshape(len(ids), 2, width // 2, norb)
        keep = jnp.where(upper, term[:, 1], term[:, 0])
        send = jnp.where(upper, term[:, 0], term[:, 1])
        for k, b in enumerate(ids):
            keep_ref[b] = keep[k]
            send_ref[b] = send[k]


def action(orbitals, fitted, early, late, early_ids, late_ids, fit_scale, mix_scale):
    width, cols = early[0].shape[1:]
    blocks = orbitals.shape[0] // width
    norb = orbitals.shape[1]
    shape = jax.ShapeDtypeStruct((blocks, width // 2, norb), jnp.float32)
    return pl.pallas_call(
        functools.partial(action_kernel, fit_scale, mix_scale, min(512, cols), early_ids, late_ids, len(early)),
        out_shape=[shape, shape],
        in_specs=[pl.BlockSpec(memory_space=pltpu.VMEM)] * (2 + len(early) + len(late)),
        out_specs=[pl.BlockSpec(memory_space=pltpu.VMEM)] * 2,
        scratch_shapes=[pltpu.VMEM((norb, cols), jnp.bfloat16)],
        compiler_params=pltpu.CompilerParams(vmem_limit_bytes=VMEM_LIMIT),
        cost_estimate=pl.CostEstimate(
            flops=4 * blocks * width * cols * norb, bytes_accessed=2 * blocks * width * cols, transcendentals=0
        ),
    )(fitted, orbitals, *early, *late)


def per_device(orbitals, tiles, tile_block, tile_count):
    rep_size = lax.axis_size("rep")
    grid_size = lax.axis_size("grid")
    width = tiles.shape[3]
    norb = orbitals.shape[1]
    half = norb // 2
    cols = width * norb // grid_size
    full = lax.all_gather(orbitals, "rep", axis=0, tiled=True)
    fit_scale = 1.0 / math.sqrt(full.shape[0])
    mix_scale = 0.25 / math.sqrt(width * rep_size * norb)
    args = (tile_count, tile_block, full, tiles)
    per_part = half // grid_size
    if per_part == SUB and grid_size % 4 == 0 and grid_size & (grid_size - 1) == 0:
        near_size = grid_size // 2

        def far_blocks():
            me = lax.axis_index("grid")
            return [me ^ (near_size + k) for k in range(near_size)]

        def near_blocks():
            me = lax.axis_index("grid")
            return [me ^ k for k in range(near_size)]

        sent_far = contract(
            lambda: [b * SUB for b in far_blocks()], lambda s, k: (s, 0, k), [(1, width, cols)] * near_size, *args
        )
        far = [
            lax.ppermute(sent, "grid", [(i, i ^ (near_size + k)) for i in range(grid_size)])
            for k, sent in enumerate(sent_far)
        ]
        sent_near = contract(
            lambda: [b * SUB for b in near_blocks()], lambda s, k: (s, 0, k), [(1, width, cols)] * near_size, *args,
            after=sent_far[0],
        )
        near = [sent_near[0]] + [
            lax.ppermute(sent, "grid", [(i, i ^ k) for i in range(grid_size)])
            for k, sent in enumerate(sent_near) if k
        ]
        early, late, early_ids, late_ids = far, near, far_blocks, near_blocks
    else:
        def place(s, k):
            part, col = divmod(s * SUB + k, per_part)
            return 0, part, col

        (sent,) = contract(
            lambda: list(range(0, half, SUB)), place, [(grid_size, width, cols)], *args
        )
        early, late = [lax.all_to_all(sent, "grid", 0, 0, tiled=True)], []

        def early_ids():
            return list(range(grid_size))

        late_ids = None
    fitted = fit(full, early, early_ids)
    part_keep, part_send = action(full, fitted, early, late, early_ids, late_ids, fit_scale, mix_scale)
    pair = part_keep + lax.ppermute(part_send, "rep", [(i, i ^ 1) for i in range(rep_size)])
    mine = jnp.sum(lax.all_to_all(pair, "grid", 0, 0, tiled=True), axis=0)
    every = lax.all_gather(mine, "rep", axis=0, tiled=False)
    return jnp.sum(every.reshape(rep_size // 2, 2, width // 2, norb), axis=0).reshape(width, norb)


def solution(mesh):
    in_specs = (
        P("rep", None),
        P("rep", "grid", None, None, None),
        P("rep", "grid", None),
        P("rep", "grid"),
    )
    return jax.shard_map(
        per_device, mesh=mesh, in_specs=in_specs, out_specs=P("grid", None), check_vma=False
    )
```

time: 95.7 us -> 87.7 us (0.916)
  blocking collectives: 85.6 us -> 27.2 us
  waiting for transfers between devices: 0 us -> 35.2 us
  starting transfers between devices: 0 us -> 15.2 us
  Pallas kernels: 5.87 us -> 8.57 us
  local copies, waits for them, and re-layouts: 2.54 us -> 0 us
    all_to_all x2 -> x1, blocking collectives: 72.3 us -> 14.3 us  [per_device(): mine = jnp.sum(lax.all_to_all(pair, 'grid', 0, 0, tiled=True), axis=0)]
    ppermute x0 -> x8, waiting for transfers between devices: none -> 35.2 us  [the longest x4 32.5 us: per_device(): lax.ppermute(sent, 'grid', [(i, i ^ near_size + k) for i in range(grid_si...]
    ppermute x0 -> x8, starting transfers between devices: none -> 15.2 us  [the longest x3 7.72 us: per_device(): lax.ppermute(sent, 'grid', [(i, i ^ k) for i in range(grid_size)])]
    pallas_call x2 -> x4, Pallas kernels: 5.87 us -> 8.57 us  [the longest x2 7.09 us: contract(): pl.pallas_call(functools.partial(contract_kernel, group_starts, place, le...]
    unnamed x4 -> x0, local copies, waits for them, and re-layouts: 2.54 us -> none
  transfers between devices with their start and end apart: 0 -> 8, of which waited for: 0 -> 4; matrix products, arithmetic and copies ran while one was open for 0% -> 0% of each run, Pallas kernels for 0% -> 5%
where the time goes in v2:
time: 87.7 us; the launch traced here: 87.5 us
  waiting for transfers between devices  35.2 us (40%)
  blocking collectives  27.2 us (31%)
  starting transfers between devices  15.2 us (17%)
  Pallas kernels  8.57 us (10%)
    ppermute x4, waiting for transfers between devices, per_device(): lax.ppermute(sent, 'grid', [(i, i ^ near_size + k) for i in range(grid_si...  32.5 us
    all_to_all x1, blocking collectives, per_device(): mine = jnp.sum(lax.all_to_all(pair, 'grid', 0, 0, tiled=True), axis=0)  14.3 us
    ppermute x3, starting transfers between devices, per_device(): lax.ppermute(sent, 'grid', [(i, i ^ k) for i in range(grid_size)])  7.72 us
    all_gather x1, blocking collectives, per_device(): full = lax.all_gather(orbitals, 'rep', axis=0, tiled=True)  7.43 us
    ppermute x4, starting transfers between devices, per_device(): lax.ppermute(sent, 'grid', [(i, i ^ near_size + k) for i in range(grid_si...  7.4 us
    pallas_call x2, Pallas kernels, contract(): pl.pallas_call(functools.partial(contract_kernel, group_starts, place, le...  7.09 us
    all_gather x1, blocking collectives, per_device(): every = lax.all_gather(mine, 'rep', axis=0, tiled=False)  5.43 us
  transfers between devices with their start and end apart: 8, of which 4 were waited for; matrix products, arithmetic and copies ran while one was open for 0% of the time, Pallas kernels for 5%

profile of v2, /device:TPU:0, one launch (start us, length us, event | category | flops | bytes accessed | tf_op | source)
XLA Modules:
  0.0 87.5 jit_solution(8049329558716476152)
XLA Ops:
  0.7 7.4 %all_gather.9.orb_ref = bf16[512,256]{1,0:T(8,128)(2,1)S(1)} all-gather(bf16[128,256]{1,0:T(8,128)(2,1)} %param.4), channel_id=1, replica_groups=mesh['rep'=4,'grid'=8] {'rep'}, dimensions={0}, use_global_device_ids=true | all-gather | bytes 327680 | tf_op jit(solution)/shard_map/all_gather | solution.py:194
  8.1 3.5 %shard_map.46 = (bf16[1,64,2048]{2,1,0:T(8,128)(2,1)S(1)}, bf16[1,64,2048]{2,1,0:T(8,128)(2,1)S(1)}, bf16[1,64,2048]{2,1,0:T(8,128)(2,1)S(1)}, bf16[1,64,2048]{2,1,0:T(8,128)(2,1)S(1)}) custom-call(s32[1,1]{1,0:T(1,128)S(6)} %copy.5.count, s32[1,1,6]{2,1,0:T(1,128)} %block_hbm.3, bf16[512,256]{1,0:T(8,128)(2,1)S(1)} %all_gather.9.orb_ref, ...), custom_call_target="tpu_custom_call" | custom-call | flops 402653184 | bytes 4194304 | tf_op jit(solution)/shard_map/pallas_call | solution.py:82
  11.6 3.6 %collective-permute-start.1 = (bf16[1,64,2048]{2,1,0:T(8,128)(2,1)S(1)}, bf16[1,64,2048]{2,1,0:T(8,128)(2,1)S(1)}, u32[]{:S(2)}, u32[]{:S(2)}) collective-permute-start(bf16[1,64,2048]{2,1,0:T(8,128)(2,1)S(1)} %get-tuple-element.16), channel_id=1, source_target_pairs={{0,5},{1,4},{2,7},{3,6},{4,1},{5,0},{6,3},{7,2},{8,13},{9,12},{10,... | collective-permute-start | bytes 786440 | tf_op jit(solution)/shard_map/ppermute | solution.py:214
  15.2 1.4 %collective-permute-start.2 = (bf16[1,64,2048]{2,1,0:T(8,128)(2,1)S(1)}, bf16[1,64,2048]{2,1,0:T(8,128)(2,1)S(1)}, u32[]{:S(2)}, u32[]{:S(2)}) collective-permute-start(bf16[1,64,2048]{2,1,0:T(8,128)(2,1)S(1)} %get-tuple-element.17), channel_id=1, source_target_pairs={{0,6},{1,7},{2,4},{3,5},{4,2},{5,3},{6,0},{7,1},{8,14},{9,15},{10,... | collective-permute-start | bytes 786440 | tf_op jit(solution)/shard_map/ppermute | solution.py:214
  16.6 2.5 %collective-permute-start.3 = (bf16[1,64,2048]{2,1,0:T(8,128)(2,1)S(1)}, bf16[1,64,2048]{2,1,0:T(8,128)(2,1)S(1)}, u32[]{:S(2)}, u32[]{:S(2)}) collective-permute-start(bf16[1,64,2048]{2,1,0:T(8,128)(2,1)S(1)} %get-tuple-element.18), channel_id=1, source_target_pairs={{0,7},{1,6},{2,5},{3,4},{4,3},{5,2},{6,1},{7,0},{8,15},{9,14},{10,... | collective-permute-start | bytes 786440 | tf_op jit(solution)/shard_map/ppermute | solution.py:214
  19.0 0.0 collective-permute-start
  19.0 3.5 %shard_map.48 = (bf16[1,64,2048]{2,1,0:T(8,128)(2,1)S(1)}, bf16[1,64,2048]{2,1,0:T(8,128)(2,1)S(1)}, bf16[1,64,2048]{2,1,0:T(8,128)(2,1)S(1)}, bf16[1,64,2048]{2,1,0:T(8,128)(2,1)S(1)}) custom-call(s32[1,1]{1,0:T(1,128)S(6)} %copy.5.count, s32[1,1,6]{2,1,0:T(1,128)} %block_hbm.3, bf16[512,256]{1,0:T(8,128)(2,1)S(1)} %all_gather.9.orb_ref, ...), custom_call_target="tpu_custom_call" | custom-call | flops 402653184 | bytes 4194304 | tf_op jit(solution)/shard_map/pallas_call | solution.py:82
  22.6 1.5 %collective-permute-start.4 = (bf16[1,64,2048]{2,1,0:T(8,128)(2,1)S(1)}, bf16[1,64,2048]{2,1,0:T(8,128)(2,1)S(1)}, u32[]{:S(2)}, u32[]{:S(2)}) collective-permute-start(bf16[1,64,2048]{2,1,0:T(8,128)(2,1)S(1)} %get-tuple-element.20), channel_id=1, source_target_pairs={{0,1},{1,0},{2,3},{3,2},{4,5},{5,4},{6,7},{7,6},{8,9},{9,8},{10,11... | collective-permute-start | bytes 786440 | tf_op jit(solution)/shard_map/ppermute | solution.py:222
  24.1 21.0 %collective-permute-done.1.refs_1_ = bf16[1,64,2048]{2,1,0:T(8,128)(2,1)S(1)} collective-permute-done((bf16[1,64,2048]{2,1,0:T(8,128)(2,1)S(1)}, bf16[1,64,2048]{2,1,0:T(8,128)(2,1)S(1)}, u32[]{:S(2)}, u32[]{:S(2)}) %collective-permute-start.1) | collective-permute-done | bytes 262176 | tf_op jit(solution)/shard_map/ppermute | solution.py:214
  45.1 0.2 collective-permute-start.5
  45.3 0.0 collective-permute-done.2.refs_2_
  45.3 6.0 %collective-permute-start.6 = (bf16[1,64,2048]{2,1,0:T(8,128)(2,1)S(1)}, bf16[1,64,2048]{2,1,0:T(8,128)(2,1)S(1)}, u32[]{:S(2)}, u32[]{:S(2)}) collective-permute-start(bf16[1,64,2048]{2,1,0:T(8,128)(2,1)S(1)} %get-tuple-element.22), channel_id=1, source_target_pairs={{0,3},{1,2},{2,1},{3,0},{4,7},{5,6},{6,5},{7,4},{8,11},{9,10},{10,... | collective-permute-start | bytes 786440 | tf_op jit(solution)/shard_map/ppermute | solution.py:222
  51.3 0.0 collective-permute-done.3.refs_3_
  51.3 11.5 %collective-permute-done.refs_0_ = bf16[1,64,2048]{2,1,0:T(8,128)(2,1)S(1)} collective-permute-done((bf16[1,64,2048]{2,1,0:T(8,128)(2,1)S(1)}, bf16[1,64,2048]{2,1,0:T(8,128)(2,1)S(1)}, u32[]{:S(2)}, u32[]{:S(2)}) %collective-permute-start) | collective-permute-done | bytes 262176 | tf_op jit(solution)/shard_map/ppermute | solution.py:214
  62.8 0.5 shard_map.47.fitted_ref
  63.2 0.0 collective-permute-done.4.refs_5_
  63.3 0.0 collective-permute-done.5.refs_6_
  63.3 1.2 %collective-permute-done.6.refs_7_ = bf16[1,64,2048]{2,1,0:T(8,128)(2,1)S(1)} collective-permute-done((bf16[1,64,2048]{2,1,0:T(8,128)(2,1)S(1)}, bf16[1,64,2048]{2,1,0:T(8,128)(2,1)S(1)}, u32[]{:S(2)}, u32[]{:S(2)}) %collective-permute-start.6) | collective-permute-done | bytes 262176 | tf_op jit(solution)/shard_map/ppermute | solution.py:222
  64.4 1.0 %shard_map.49 = (f32[8,32,256]{2,1,0:T(8,128)S(1)}, f32[8,32,256]{2,1,0:T(8,128)S(1)}) custom-call(f32[256,2048]{1,0:T(8,128)S(1)} %shard_map.47.fitted_ref, bf16[512,256]{1,0:T(8,128)(2,1)S(1)} %all_gather.9.orb_ref, bf16[1,64,2048]{2,1,0:T(8,128)(2,1)S(1)} %collective-permute-done.refs_0_, bf16[1,64,2048]{2,1,0:T(8,128)(2,1)S(1)} %collective-permute-done.1.refs_1_, ...), custom_call_target="tpu_custom_call" | custom-call | flops 1073741824 | bytes 2097152 | tf_op jit(solution)/shard_map/pallas_call | solution.py:174
  65.5 0.1 collective-permute-start.7
  65.6 1.5 %collective-permute-done.7 = f32[8,32,256]{2,1,0:T(8,128)S(1)} collective-permute-done((f32[8,32,256]{2,1,0:T(8,128)S(1)}, f32[8,32,256]{2,1,0:T(8,128)S(1)}, u32[]{:S(2)}, u32[]{:S(2)}) %collective-permute-start.7) | collective-permute-done | bytes 262176 | tf_op jit(solution)/shard_map/ppermute | solution.py:242
  67.1 14.3 %all_to_all.5 = f32[8,32,256]{2,1,0:T(8,128)S(1)} all-to-all(f32[8,32,256]{2,1,0:T(8,128)S(1)} %add.3), channel_id=1, replica_groups=mesh['rep'=4,'grid'=8] {'grid'}, dimensions={0} | all-to-all | bytes 524288 | tf_op jit(solution)/shard_map/all_to_all | solution.py:243
  81.5 5.4 %all-gather = f32[128,256]{1,0:T(8,128)S(1)} all-gather(f32[32,256]{1,0:T(8,128)S(1)} %reduce_sum.18), channel_id=2, replica_groups=mesh['rep'=4,'grid'=8] {'rep'}, dimensions={0}, use_global_device_ids=true | all-gather | bytes 163840 | tf_op jit(solution)/shard_map/all_gather | solution.py:244
  86.9 0.6 reduce_sum.19
  (2 shorter events, 0.1 us)
Async XLA Ops:
  11.6 33.5 %collective-permute-start.1 = (bf16[1,64,2048]{2,1,0:T(8,128)(2,1)S(1)}, bf16[1,64,2048]{2,1,0:T(8,128)(2,1)S(1)}, u32[]{:S(2)}, u32[]{:S(2)}) collective-permute-start(bf16[1,64,2048]{2,1,0:T(8,128)(2,1)S(1)} %get-tuple-element.16), channel_id=1, source_target_pairs={{0,5},{1,4},{2,7},{3,6},{4,1},{5,0},{6,3},{7,2},{8,13},{9,12},{10,... | collective-permute-start | bytes 786440 | tf_op jit(solution)/shard_map/ppermute | solution.py:214
  15.2 30.1 %collective-permute-start.2 = (bf16[1,64,2048]{2,1,0:T(8,128)(2,1)S(1)}, bf16[1,64,2048]{2,1,0:T(8,128)(2,1)S(1)}, u32[]{:S(2)}, u32[]{:S(2)}) collective-permute-start(bf16[1,64,2048]{2,1,0:T(8,128)(2,1)S(1)} %get-tuple-element.17), channel_id=1, source_target_pairs={{0,6},{1,7},{2,4},{3,5},{4,2},{5,3},{6,0},{7,1},{8,14},{9,15},{10,... | collective-permute-start | bytes 786440 | tf_op jit(solution)/shard_map/ppermute | solution.py:214
  16.6 34.7 %collective-permute-start.3 = (bf16[1,64,2048]{2,1,0:T(8,128)(2,1)S(1)}, bf16[1,64,2048]{2,1,0:T(8,128)(2,1)S(1)}, u32[]{:S(2)}, u32[]{:S(2)}) collective-permute-start(bf16[1,64,2048]{2,1,0:T(8,128)(2,1)S(1)} %get-tuple-element.18), channel_id=1, source_target_pairs={{0,7},{1,6},{2,5},{3,4},{4,3},{5,2},{6,1},{7,0},{8,15},{9,14},{10,... | collective-permute-start | bytes 786440 | tf_op jit(solution)/shard_map/ppermute | solution.py:214
  19.0 43.7 %collective-permute-start = (bf16[1,64,2048]{2,1,0:T(8,128)(2,1)S(1)}, bf16[1,64,2048]{2,1,0:T(8,128)(2,1)S(1)}, u32[]{:S(2)}, u32[]{:S(2)}) collective-permute-start(bf16[1,64,2048]{2,1,0:T(8,128)(2,1)S(1)} %get-tuple-element.15.refs_0_), channel_id=1, source_target_pairs={{0,4},{1,5},{2,6},{3,7},{4,0},{5,1},{6,2},{7,3},{8,12},{9,13},{10,... | collective-permute-start | bytes 786440 | tf_op jit(solution)/shard_map/ppermute | solution.py:214
  22.6 40.7 %collective-permute-start.4 = (bf16[1,64,2048]{2,1,0:T(8,128)(2,1)S(1)}, bf16[1,64,2048]{2,1,0:T(8,128)(2,1)S(1)}, u32[]{:S(2)}, u32[]{:S(2)}) collective-permute-start(bf16[1,64,2048]{2,1,0:T(8,128)(2,1)S(1)} %get-tuple-element.20), channel_id=1, source_target_pairs={{0,1},{1,0},{2,3},{3,2},{4,5},{5,4},{6,7},{7,6},{8,9},{9,8},{10,11... | collective-permute-start | bytes 786440 | tf_op jit(solution)/shard_map/ppermute | solution.py:222
  45.1 18.2 %collective-permute-start.5 = (bf16[1,64,2048]{2,1,0:T(8,128)(2,1)S(1)}, bf16[1,64,2048]{2,1,0:T(8,128)(2,1)S(1)}, u32[]{:S(2)}, u32[]{:S(2)}) collective-permute-start(bf16[1,64,2048]{2,1,0:T(8,128)(2,1)S(1)} %get-tuple-element.21), channel_id=1, source_target_pairs={{0,2},{1,3},{2,0},{3,1},{4,6},{5,7},{6,4},{7,5},{8,10},{9,11},{10,... | collective-permute-start | bytes 786440 | tf_op jit(solution)/shard_map/ppermute | solution.py:222
  45.3 19.1 %collective-permute-start.6 = (bf16[1,64,2048]{2,1,0:T(8,128)(2,1)S(1)}, bf16[1,64,2048]{2,1,0:T(8,128)(2,1)S(1)}, u32[]{:S(2)}, u32[]{:S(2)}) collective-permute-start(bf16[1,64,2048]{2,1,0:T(8,128)(2,1)S(1)} %get-tuple-element.22), channel_id=1, source_target_pairs={{0,3},{1,2},{2,1},{3,0},{4,7},{5,6},{6,5},{7,4},{8,11},{9,10},{10,... | collective-permute-start | bytes 786440 | tf_op jit(solution)/shard_map/ppermute | solution.py:222
  65.5 1.6 %collective-permute-start.7 = (f32[8,32,256]{2,1,0:T(8,128)S(1)}, f32[8,32,256]{2,1,0:T(8,128)S(1)}, u32[]{:S(2)}, u32[]{:S(2)}) collective-permute-start(f32[8,32,256]{2,1,0:T(8,128)S(1)} %get-tuple-element.24), channel_id=1, source_target_pairs={{0,8},{8,0},{16,24},{24,16},{1,9},{9,1},{17,25},{25,17},{2,10},{10... | collective-permute-start | bytes 786440 | tf_op jit(solution)/shard_map/ppermute | solution.py:242

commit v3 on v2

v3 whole, which is shorter than its diff:
```python
import functools
import math

import jax
import jax.numpy as jnp
from jax import lax
from jax.experimental import pallas as pl
from jax.experimental.pallas import tpu as pltpu
from jax.sharding import PartitionSpec as P

LANES = 128
SUB = 16
VMEM_LIMIT = 24 * 1024 * 1024


def load_kernel(count_ref, block_hbm, tiles_hbm, out_ref, live_ref, block, sems, block_sem):
    chunks = sems.shape[0]
    step = out_ref.shape[2] // chunks
    copies = [
        pltpu.make_async_copy(
            tiles_hbm.at[0, 0, :, :, pl.ds(at * step, step)], out_ref.at[:, :, pl.ds(at * step, step)], sems.at[at]
        )
        for at in range(chunks)
    ]
    block_copy = pltpu.make_async_copy(block_hbm, block, block_sem.at[0])
    block_copy.start()
    for each in copies:
        each.start()
    block_copy.wait()
    slot = lax.broadcasted_iota(jnp.int32, live_ref.shape, 1)
    live_ref[...] = jnp.where(slot < count_ref[0, 0], block[0], -1)
    for each in copies:
        each.wait()


def in_hbm(x):
    return pltpu.with_memory_space_constraint(x, pltpu.HBM)


def load(tiles, count, block):
    return pl.pallas_call(
        load_kernel,
        out_shape=[
            jax.ShapeDtypeStruct(tiles.shape[2:], tiles.dtype),
            jax.ShapeDtypeStruct(block.shape[1:], block.dtype),
        ],
        in_specs=[
            pl.BlockSpec(memory_space=pltpu.SMEM),
            pl.BlockSpec(memory_space=pltpu.HBM),
            pl.BlockSpec(memory_space=pltpu.HBM),
        ],
        out_specs=[pl.BlockSpec(memory_space=pltpu.VMEM)] * 2,
        scratch_shapes=[
            pltpu.VMEM(block.shape, block.dtype),
            pltpu.SemaphoreType.DMA((4,)),
            pltpu.SemaphoreType.DMA((1,)),
        ],
        compiler_params=pltpu.CompilerParams(vmem_limit_bytes=VMEM_LIMIT),
        cost_estimate=pl.CostEstimate(flops=0, bytes_accessed=2 * math.prod(tiles.shape), transcendentals=0),
    )(count, in_hbm(block), in_hbm(tiles))


def multiply(turned_ref, tiles_ref, group_starts, place, outs):
    slots, width, extent = tiles_ref.shape
    half = turned_ref.shape[0] // 2
    step = SUB * width
    row_at = lax.broadcasted_iota(jnp.int32, (SUB * SUB, SUB * SUB), 0)
    col_at = lax.broadcasted_iota(jnp.int32, (SUB * SUB, SUB * SUB), 1)
    bits = SUB.bit_length() - 1
    swap = (col_at == ((row_at & (SUB - 1)) << bits) + (row_at >> bits)).astype(jnp.bfloat16)
    low = lax.broadcasted_iota(jnp.int32, (SUB, LANES), 1) < width
    groups = len(group_starts)
    lhs = jnp.concatenate(
        [
            turned_ref[pl.ds(pl.multiple_of(first + at, SUB), SUB), :]
            for first in (0, half)
            for at in group_starts
        ],
        axis=0,
    )
    chunks = extent // step
    sides = []
    for at in range(chunks):
        rhs = tiles_ref[:, :, at * step:(at + 1) * step].reshape(slots * width, step)
        acc = jnp.dot(lhs, rhs, preferred_element_type=jnp.float32)
        for s in range(groups):
            per_mu = []
            for q in range(step // LANES):
                a = acc[s * SUB:(s + 1) * SUB, q * LANES:(q + 1) * LANES]
                b = acc[(groups + s) * SUB:(groups + s + 1) * SUB, q * LANES:(q + 1) * LANES]
                per_mu.append(jnp.where(low, a, pltpu.roll(b, width, 1)).astype(jnp.bfloat16))
                per_mu.append(jnp.where(low, pltpu.roll(a, width, 1), b).astype(jnp.bfloat16))
            sides.append((at, s, jnp.concatenate(per_mu, axis=0)))
    moved = jnp.dot(
        swap, jnp.concatenate([side for _, _, side in sides], axis=1), preferred_element_type=jnp.float32
    ).astype(jnp.bfloat16)
    for n, (at, s, _) in enumerate(sides):
        for k in range(SUB):
            which, part, col = place(s, k)
            outs[which][part, at * SUB:(at + 1) * SUB, col * LANES:(col + 1) * LANES] = moved[
                k * SUB:(k + 1) * SUB, n * LANES:(n + 1) * LANES
            ]


def first_kernel(group_starts, place, n_parts, block_ref, tiles_ref, *refs):
    parts, (full_ref, turned_ref, *outs), picked = refs[:n_parts], refs[n_parts:-1], refs[-1]
    slots, width, _ = tiles_ref.shape
    depth = parts[0].shape[0]
    me = lax.axis_index("rep") if n_parts > 1 else 0
    for k in range(n_parts):
        full_ref[pl.ds(pl.multiple_of((me ^ k) * depth, depth), depth), :] = parts[k][...]
    for t in range(slots):
        row = pl.multiple_of(jnp.maximum(block_ref[0, t], 0) * width, width)
        rows = full_ref[pl.ds(row, width), :]
        picked[t * width:(t + 1) * width, :] = jnp.where(block_ref[0, t] >= 0, rows, jnp.zeros_like(rows))
    turned_ref[...] = picked[...].T
    multiply(turned_ref, tiles_ref, group_starts(), place, outs)


def next_kernel(group_starts, place, turned_ref, tiles_ref, skipped, *outs):
    multiply(turned_ref, tiles_ref, group_starts(), place, outs)


def contract_cost(tiles, norb, out_shapes):
    slots, width, extent = tiles.shape
    made = sum(math.prod(shape) for shape in out_shapes)
    return pl.CostEstimate(
        flops=2 * slots * width * made, bytes_accessed=2 * slots * width * extent + 2 * made, transcendentals=0
    )


def contract_first(group_starts, place, out_shapes, block, tiles, parts):
    slots, width, _ = tiles.shape
    depth, norb = parts[0].shape
    shapes = [(depth * len(parts), norb), (norb, slots * width)] + out_shapes
    full, turned, *made = pl.pallas_call(
        functools.partial(first_kernel, group_starts, place, len(parts)),
        out_shape=[jax.ShapeDtypeStruct(shape, jnp.bfloat16) for shape in shapes],
        in_specs=[pl.BlockSpec(memory_space=pltpu.SMEM)]
        + [pl.BlockSpec(memory_space=pltpu.VMEM)] * (1 + len(parts)),
        out_specs=[pl.BlockSpec(memory_space=pltpu.VMEM)] * len(shapes),
        scratch_shapes=[pltpu.VMEM((slots * width, norb), jnp.bfloat16)],
        compiler_params=pltpu.CompilerParams(vmem_limit_bytes=VMEM_LIMIT),
        cost_estimate=contract_cost(tiles, norb, out_shapes),
    )(block, tiles, *parts)
    return full, turned, made


def contract_next(group_starts, place, out_shapes, turned, tiles, after):
    return pl.pallas_call(
        functools.partial(next_kernel, group_starts, place),
        out_shape=[jax.ShapeDtypeStruct(shape, jnp.bfloat16) for shape in out_shapes],
        in_specs=[pl.BlockSpec(memory_space=pltpu.VMEM)] * 2 + [pl.BlockSpec(memory_space=pl.ANY)],
        out_specs=[pl.BlockSpec(memory_space=pltpu.VMEM)] * len(out_shapes),
        compiler_params=pltpu.CompilerParams(vmem_limit_bytes=VMEM_LIMIT),
        cost_estimate=contract_cost(tiles, turned.shape[0], out_shapes),
    )(turned, tiles, after)


def orbital_rows(orb_ref, width, ids):
    rows = [orb_ref[pl.ds(pl.multiple_of(b * width, width), width), :] for b in ids]
    return jnp.concatenate(rows, axis=0).T


def joined(refs, lanes=slice(None)):
    return jnp.concatenate([ref[:, :, lanes].reshape(-1, ref[:, :, lanes].shape[2]) for ref in refs], axis=0)


def fit_kernel(step, ids, orb_ref, *refs):
    rows, out_ref = refs[:-1], refs[-1]
    turned = orbital_rows(orb_ref, rows[0].shape[1], ids())
    for at in range(out_ref.shape[1] // step):
        lanes = slice(at * step, (at + 1) * step)
        out_ref[:, lanes] = jnp.dot(turned, joined(rows, lanes), preferred_element_type=jnp.float32)


def fit(orbitals, rows, ids):
    width, cols = rows[0].shape[1:]
    number = sum(each.shape[0] for each in rows)
    norb = orbitals.shape[1]
    return pl.pallas_call(
        functools.partial(fit_kernel, min(512, cols), ids),
        out_shape=jax.ShapeDtypeStruct((norb, cols), jnp.float32),
        in_specs=[pl.BlockSpec(memory_space=pltpu.VMEM)] * (1 + len(rows)),
        out_specs=pl.BlockSpec(memory_space=pltpu.VMEM),
        compiler_params=pltpu.CompilerParams(vmem_limit_bytes=VMEM_LIMIT),
        cost_estimate=pl.CostEstimate(
            flops=2 * number * width * cols * norb,
            bytes_accessed=2 * number * width * cols + 4 * norb * cols,
            transcendentals=0,
        ),
    )(orbitals, *rows)


def action_kernel(fit_scale, mix_scale, step, early_ids, late_ids, n_early, fitted_ref, orb_ref, *refs):
    early, late, (keep_ref, send_ref, fitted) = refs[:n_early], refs[n_early:-3], refs[-3:]
    width, cols = early[0].shape[1:]
    norb = orb_ref.shape[1]
    upper = lax.axis_index("rep") % 2 == 1
    if late:
        turned = orbital_rows(orb_ref, width, late_ids())
    for at in range(cols // step):
        lanes = slice(at * step, (at + 1) * step)
        total = fitted_ref[:, lanes]
        if late:
            total = total + jnp.dot(turned, joined(late, lanes), preferred_element_type=jnp.float32)
        fitted[:, lanes] = (fit_scale * total).astype(jnp.bfloat16)
    parts = [(early_ids(), early)]
    if late:
        parts.append((late_ids(), late))
    for ids, rows in parts:
        term = lax.dot_general(joined(rows), fitted[...], (((1,), (1,)), ((), ())), preferred_element_type=jnp.float32)
        term = (-mix_scale * term).reshape(len(ids), 2, width // 2, norb)
        keep = jnp.where(upper, term[:, 1], term[:, 0])
        send = jnp.where(upper, term[:, 0], term[:, 1])
        for k, b in enumerate(ids):
            keep_ref[b] = keep[k]
            send_ref[b] = send[k]


def action(orbitals, fitted, early, late, early_ids, late_ids, fit_scale, mix_scale):
    width, cols = early[0].shape[1:]
    blocks = orbitals.shape[0] // width
    norb = orbitals.shape[1]
    shape = jax.ShapeDtypeStruct((blocks, width // 2, norb), jnp.float32)
    return pl.pallas_call(
        functools.partial(action_kernel, fit_scale, mix_scale, min(512, cols), early_ids, late_ids, len(early)),
        out_shape=[shape, shape],
        in_specs=[pl.BlockSpec(memory_space=pltpu.VMEM)] * (2 + len(early) + len(late)),
        out_specs=[pl.BlockSpec(memory_space=pltpu.VMEM)] * 2,
        scratch_shapes=[pltpu.VMEM((norb, cols), jnp.bfloat16)],
        compiler_params=pltpu.CompilerParams(vmem_limit_bytes=VMEM_LIMIT),
        cost_estimate=pl.CostEstimate(
            flops=4 * blocks * width * cols * norb, bytes_accessed=2 * blocks * width * cols, transcendentals=0
        ),
    )(fitted, orbitals, *early, *late)


def swapped(x, axis, k):
    return lax.ppermute(x, axis, [(i, i ^ k) for i in range(lax.axis_size(axis))])


def per_device(orbitals, tiles, tile_block, tile_count):
    rep_size = lax.axis_size("rep")
    grid_size = lax.axis_size("grid")
    width = tiles.shape[3]
    depth, norb = orbitals.shape
    half = norb // 2
    cols = width * norb // grid_size
    basis_rows = depth * rep_size
    fit_scale = 1.0 / math.sqrt(basis_rows)
    mix_scale = 0.25 / math.sqrt(width * rep_size * norb)
    inside, block = load(tiles, tile_count, tile_block)
    per_part = half // grid_size
    if per_part == SUB and grid_size == 8 and rep_size == 4:
        near_size = grid_size // 2
        parts = [orbitals] + [swapped(orbitals, "rep", k) for k in range(1, rep_size)]

        def ids(ks):
            def blocks():
                me = lax.axis_index("grid")
                return [me ^ k for k in ks]

            return blocks

        def starts(ks):
            return lambda: [b * SUB for b in ids(ks)()]

        def own_output(s, k):
            return s, 0, k

        def shapes(ks):
            return [(1, width, cols)] * len(ks)

        waves, late_ks = [[4], [0, 1, 2, 3], [5, 6, 7]], [5, 6, 7]
        full, turned, made = contract_first(
            starts(waves[0]), own_output, shapes(waves[0]), block, inside, parts
        )
        sent = dict(zip(waves[0], made))
        for wave in waves[1:]:
            made = contract_next(starts(wave), own_output, shapes(wave), turned, inside, made[0])
            sent.update(zip(wave, made))
        received = {k: swapped(sent[k], "grid", k) if k else sent[k] for wave in waves for k in wave}
        early_ks = [k for wave in waves for k in wave if k not in late_ks]
        early, late = [received[k] for k in early_ks], [received[k] for k in late_ks]
        early_ids, late_ids = ids(early_ks), ids(late_ks)
    else:
        def place(s, k):
            part, col = divmod(s * SUB + k, per_part)
            return 0, part, col

        parts = [lax.all_gather(orbitals, "rep", axis=0, tiled=True)]
        full, _, (sent,) = contract_first(
            lambda: list(range(0, half, SUB)), place, [(grid_size, width, cols)], block, inside, parts
        )
        early, late = [lax.all_to_all(sent, "grid", 0, 0, tiled=True)], []

        def early_ids():
            return list(range(grid_size))

        late_ids = None
    fitted = fit(full, early, early_ids)
    part_keep, part_send = action(full, fitted, early, late, early_ids, late_ids, fit_scale, mix_scale)
    pair = part_keep + swapped(part_send, "rep", 1)
    mine = jnp.sum(lax.all_to_all(pair, "grid", 0, 0, tiled=True), axis=0)
    if rep_size == 4:
        other, across = swapped(mine, "rep", 2), swapped(mine, "rep", 3)
        beside = swapped(mine, "rep", 1)
        own, theirs = mine + other, beside + across
        upper = lax.axis_index("rep") % 2 == 1
        return jnp.concatenate([jnp.where(upper, theirs, own), jnp.where(upper, own, theirs)], axis=0)
    every = lax.all_gather(mine, "rep", axis=0, tiled=False)
    return jnp.sum(every.reshape(rep_size // 2, 2, width // 2, norb), axis=0).reshape(width, norb)


def solution(mesh):
    in_specs = (
        P("rep", None),
        P("rep", "grid", None, None, None),
        P("rep", "grid", None),
        P("rep", "grid"),
    )
    return jax.shard_map(
        per_device, mesh=mesh, in_specs=in_specs, out_specs=P("grid", None), check_vma=False
    )
```

time: 87.7 us -> 79.7 us (0.909)
  blocking collectives: 27.2 us -> 21.7 us
  waiting for transfers between devices: 35.2 us -> 31.1 us
  starting transfers between devices: 15.2 us -> 17.7 us
  Pallas kernels: 8.57 us -> 7.53 us
    all_gather x2 -> x0, blocking collectives: 12.9 us -> none  [the longest x1 7.43 us: per_device(): full = lax.all_gather(orbitals, 'rep', axis=0, tiled=True)]
    all_to_all x1, blocking collectives: 14.3 us -> 21.7 us  [per_device(): mine = jnp.sum(lax.all_to_all(pair, 'grid', 0, 0, tiled=True), axis=0)]
    ppermute x8 -> x14, waiting for transfers between devices: 35.2 us -> 31.1 us  [swapped(): lax.ppermute(x, axis, [(i, i ^ k) for i in range(lax.axis_size(axis))])]
    ppermute x8 -> x14, starting transfers between devices: 15.2 us -> 17.7 us  [swapped(): lax.ppermute(x, axis, [(i, i ^ k) for i in range(lax.axis_size(axis))])]
    pallas_call x2 -> x4, Pallas kernels: 7.09 us -> 5.59 us  [the longest x2 2.1 us: contract_next(): pl.pallas_call(functools.partial(next_kernel, group_starts, place), out_s...]
  transfers between devices with their start and end apart: 8 -> 14, of which waited for: 4 -> 7; matrix products, arithmetic and copies ran while one was open for 0% -> 0% of each run, Pallas kernels for 5% -> 6%
where the time goes in v3:
time: 79.7 us; the launch traced here: 79.5 us
  waiting for transfers between devices  31.1 us (39%)
  blocking collectives  21.7 us (27%)
  starting transfers between devices  17.7 us (22%)
  Pallas kernels  7.53 us (9%)
    ppermute x14, waiting for transfers between devices, swapped(): lax.ppermute(x, axis, [(i, i ^ k) for i in range(lax.axis_size(axis))])  31.1 us
    all_to_all x1, blocking collectives, per_device(): mine = jnp.sum(lax.all_to_all(pair, 'grid', 0, 0, tiled=True), axis=0)  21.7 us
    ppermute x14, starting transfers between devices, swapped(): lax.ppermute(x, axis, [(i, i ^ k) for i in range(lax.axis_size(axis))])  17.7 us
    pallas_call x2, Pallas kernels, contract_next(): pl.pallas_call(functools.partial(next_kernel, group_starts, place), out_s...  2.1 us
    pallas_call x1, Pallas kernels, load(): pl.pallas_call(load_kernel, out_shape=[jax.ShapeDtypeStruct(tiles.shape[2...  1.91 us
  transfers between devices with their start and end apart: 14, of which 7 were waited for; matrix products, arithmetic and copies ran while one was open for 0% of the time, Pallas kernels for 6%

profile of v3, /device:TPU:0, one launch (start us, length us, event | category | flops | bytes accessed | tf_op | source)
XLA Modules:
  0.0 79.5 jit_solution(6441676583271063050)
XLA Ops:
  0.0 0.0 copy-start
  0.0 3.0 %collective-permute-start.1 = (bf16[128,256]{1,0:T(8,128)(2,1)}, bf16[128,256]{1,0:T(8,128)(2,1)S(1)}, u32[]{:S(2)}, u32[]{:S(2)}) collective-permute-start(bf16[128,256]{1,0:T(8,128)(2,1)} %refs_0_.1), channel_id=1, source_target_pairs={{0,16},{8,24},{16,0},{24,8},{1,17},{9,25},{17,1},{25,9},{2,18},{10... | collective-permute-start | bytes 196616 | tf_op jit(solution)/shard_map/ppermute | solution.py:240
  3.0 0.0 collective-permute-start
  3.0 0.2 collective-permute-start.2
  3.8 1.9 %shard_map.46 = (bf16[6,64,4096]{2,1,0:T(8,128)(2,1)S(1)}, s32[1,6]{1,0:T(1,128)S(1)}) custom-call(s32[1,1]{1,0:T(1,128)S(6)} %copy.5.count_ref, s32[1,1,6]{2,1,0:T(1,128)} %block_hbm.1, bf16[1,1,6,64,4096]{4,3,2,1,0:T(8,128)(2,1)} %tiles_hbm.1), custom_call_target="tpu_custom_call" | custom-call | bytes 3145728 | tf_op jit(solution)/shard_map/pallas_call | solution.py:41
  5.7 0.0 collective-permute-done.1.refs_2_
  5.7 0.0 collective-permute-done.refs_1_
  5.8 1.2 %collective-permute-done.2.refs_3_ = bf16[128,256]{1,0:T(8,128)(2,1)S(1)} collective-permute-done((bf16[128,256]{1,0:T(8,128)(2,1)}, bf16[128,256]{1,0:T(8,128)(2,1)S(1)}, u32[]{:S(2)}, u32[]{:S(2)}) %collective-permute-start.2) | collective-permute-done | bytes 65568 | tf_op jit(solution)/shard_map/ppermute | solution.py:240
  6.9 0.0 copy-done
  6.9 1.6 %shard_map.47 = (bf16[512,256]{1,0:T(8,128)(2,1)S(1)}, bf16[256,384]{1,0:T(8,128)(2,1)S(1)}, bf16[1,64,2048]{2,1,0:T(8,128)(2,1)S(1)}) custom-call(s32[1,6]{1,0:T(1,128)S(1)} %get-tuple-element.19.block_ref, bf16[6,64,4096]{2,1,0:T(8,128)(2,1)S(1)} %get-tuple-element.20.tiles_ref, bf16[128,256]{1,0:T(8,128)(2,1)S(1)} %copy-done, ...), custom_call_target="tpu_custom_call" | custom-call | flops 100663296 | bytes 3407872 | tf_op jit(solution)/shard_map/pallas_call | solution.py:136
  8.5 2.7 %collective-permute-start.3 = (bf16[1,64,2048]{2,1,0:T(8,128)(2,1)S(1)}, bf16[1,64,2048]{2,1,0:T(8,128)(2,1)S(1)}, u32[]{:S(2)}, u32[]{:S(2)}) collective-permute-start(bf16[1,64,2048]{2,1,0:T(8,128)(2,1)S(1)} %get-tuple-element.22.skipped), channel_id=1, source_target_pairs={{0,4},{1,5},{2,6},{3,7},{4,0},{5,1},{6,2},{7,3},{8,12},{9,13},{10,... | collective-permute-start | bytes 786440 | tf_op jit(solution)/shard_map/ppermute | solution.py:240
  11.2 1.1 %shard_map.48 = (bf16[1,64,2048]{2,1,0:T(8,128)(2,1)S(1)}, bf16[1,64,2048]{2,1,0:T(8,128)(2,1)S(1)}, bf16[1,64,2048]{2,1,0:T(8,128)(2,1)S(1)}, bf16[1,64,2048]{2,1,0:T(8,128)(2,1)S(1)}) custom-call(bf16[256,384]{1,0:T(8,128)(2,1)S(1)} %get-tuple-element.23.turned_ref, bf16[6,64,4096]{2,1,0:T(8,128)(2,1)S(1)} %get-tuple-element.20.tiles_ref, ...), custom_call_target="tpu_custom_call" | custom-call | flops 402653184 | bytes 4194304 | tf_op jit(solution)/shard_map/pallas_call | solution.py:150
  12.2 1.6 %collective-permute-start.4 = (bf16[1,64,2048]{2,1,0:T(8,128)(2,1)S(1)}, bf16[1,64,2048]{2,1,0:T(8,128)(2,1)S(1)}, u32[]{:S(2)}, u32[]{:S(2)}) collective-permute-start(bf16[1,64,2048]{2,1,0:T(8,128)(2,1)S(1)} %get-tuple-element.25), channel_id=1, source_target_pairs={{0,1},{1,0},{2,3},{3,2},{4,5},{5,4},{6,7},{7,6},{8,9},{9,8},{10,11... | collective-permute-start | bytes 786440 | tf_op jit(solution)/shard_map/ppermute | solution.py:240
  13.8 1.6 %collective-permute-start.5 = (bf16[1,64,2048]{2,1,0:T(8,128)(2,1)S(1)}, bf16[1,64,2048]{2,1,0:T(8,128)(2,1)S(1)}, u32[]{:S(2)}, u32[]{:S(2)}) collective-permute-start(bf16[1,64,2048]{2,1,0:T(8,128)(2,1)S(1)} %get-tuple-element.26), channel_id=1, source_target_pairs={{0,2},{1,3},{2,0},{3,1},{4,6},{5,7},{6,4},{7,5},{8,10},{9,11},{10,... | collective-permute-start | bytes 786440 | tf_op jit(solution)/shard_map/ppermute | solution.py:240
  15.4 0.4 collective-permute-start.6
  15.8 1.1 %shard_map.50 = (bf16[1,64,2048]{2,1,0:T(8,128)(2,1)S(1)}, bf16[1,64,2048]{2,1,0:T(8,128)(2,1)S(1)}, bf16[1,64,2048]{2,1,0:T(8,128)(2,1)S(1)}) custom-call(bf16[256,384]{1,0:T(8,128)(2,1)S(1)} %get-tuple-element.23.turned_ref, bf16[6,64,4096]{2,1,0:T(8,128)(2,1)S(1)} %get-tuple-element.20.tiles_ref, bf16[1,64,2048]{2,1,0:T(8,128)(2,1)S(1)} %get-tuple-element.24.refs_1_.skipped), custom_call_target="tpu_custom_call" | custom-call | flops 301989888 | bytes 3932160 | tf_op jit(solution)/shard_map/pallas_call | solution.py:150
  16.8 1.3 %collective-permute-start.7 = (bf16[1,64,2048]{2,1,0:T(8,128)(2,1)S(1)}, bf16[1,64,2048]{2,1,0:T(8,128)(2,1)S(1)}, u32[]{:S(2)}, u32[]{:S(2)}) collective-permute-start(bf16[1,64,2048]{2,1,0:T(8,128)(2,1)S(1)} %get-tuple-element.28), channel_id=1, source_target_pairs={{0,5},{1,4},{2,7},{3,6},{4,1},{5,0},{6,3},{7,2},{8,13},{9,12},{10,... | collective-permute-start | bytes 786440 | tf_op jit(solution)/shard_map/ppermute | solution.py:240
  18.2 6.1 %collective-permute-done.3.refs_0_ = bf16[1,64,2048]{2,1,0:T(8,128)(2,1)S(1)} collective-permute-done((bf16[1,64,2048]{2,1,0:T(8,128)(2,1)S(1)}, bf16[1,64,2048]{2,1,0:T(8,128)(2,1)S(1)}, u32[]{:S(2)}, u32[]{:S(2)}) %collective-permute-start.3) | collective-permute-done | bytes 262176 | tf_op jit(solution)/shard_map/ppermute | solution.py:240
  24.3 3.1 %collective-permute-start.8 = (bf16[1,64,2048]{2,1,0:T(8,128)(2,1)S(1)}, bf16[1,64,2048]{2,1,0:T(8,128)(2,1)S(1)}, u32[]{:S(2)}, u32[]{:S(2)}) collective-permute-start(bf16[1,64,2048]{2,1,0:T(8,128)(2,1)S(1)} %get-tuple-element.29), channel_id=1, source_target_pairs={{0,6},{1,7},{2,4},{3,5},{4,2},{5,3},{6,0},{7,1},{8,14},{9,15},{10,... | collective-permute-start | bytes 786440 | tf_op jit(solution)/shard_map/ppermute | solution.py:240
  27.4 0.0 collective-permute-done.4.refs_2_
  27.4 1.7 %collective-permute-start.9 = (bf16[1,64,2048]{2,1,0:T(8,128)(2,1)S(1)}, bf16[1,64,2048]{2,1,0:T(8,128)(2,1)S(1)}, u32[]{:S(2)}, u32[]{:S(2)}) collective-permute-start(bf16[1,64,2048]{2,1,0:T(8,128)(2,1)S(1)} %get-tuple-element.30), channel_id=1, source_target_pairs={{0,7},{1,6},{2,5},{3,4},{4,3},{5,2},{6,1},{7,0},{8,15},{9,14},{10,... | collective-permute-start | bytes 786440 | tf_op jit(solution)/shard_map/ppermute | solution.py:240
  29.1 4.0 %collective-permute-done.5.refs_3_ = bf16[1,64,2048]{2,1,0:T(8,128)(2,1)S(1)} collective-permute-done((bf16[1,64,2048]{2,1,0:T(8,128)(2,1)S(1)}, bf16[1,64,2048]{2,1,0:T(8,128)(2,1)S(1)}, u32[]{:S(2)}, u32[]{:S(2)}) %collective-permute-start.5) | collective-permute-done | bytes 262176 | tf_op jit(solution)/shard_map/ppermute | solution.py:240
  33.1 15.8 %collective-permute-done.6.refs_4_ = bf16[1,64,2048]{2,1,0:T(8,128)(2,1)S(1)} collective-permute-done((bf16[1,64,2048]{2,1,0:T(8,128)(2,1)S(1)}, bf16[1,64,2048]{2,1,0:T(8,128)(2,1)S(1)}, u32[]{:S(2)}, u32[]{:S(2)}) %collective-permute-start.6) | collective-permute-done | bytes 262176 | tf_op jit(solution)/shard_map/ppermute | solution.py:240
  48.8 0.7 shard_map.49.fitted_ref
  49.6 0.0 collective-permute-done.7.refs_5_
  49.6 0.0 collective-permute-done.8.refs_6_
  49.6 0.0 collective-permute-done.9.refs_7_
  49.6 1.2 %shard_map.51 = (f32[8,32,256]{2,1,0:T(8,128)S(1)}, f32[8,32,256]{2,1,0:T(8,128)S(1)}) custom-call(f32[256,2048]{1,0:T(8,128)S(1)} %shard_map.49.fitted_ref, bf16[512,256]{1,0:T(8,128)(2,1)S(1)} %get-tuple-element.21.orb_ref, bf16[1,64,2048]{2,1,0:T(8,128)(2,1)S(1)} %collective-permute-done.3.refs_0_, ...), custom_call_target="tpu_custom_call" | custom-call | flops 1073741824 | bytes 2097152 | tf_op jit(solution)/shard_map/pallas_call | solution.py:226
  50.8 0.1 collective-permute-start.10
  50.9 1.5 %collective-permute-done.10 = f32[8,32,256]{2,1,0:T(8,128)S(1)} collective-permute-done((f32[8,32,256]{2,1,0:T(8,128)S(1)}, f32[8,32,256]{2,1,0:T(8,128)S(1)}, u32[]{:S(2)}, u32[]{:S(2)}) %collective-permute-start.10) | collective-permute-done | bytes 262176 | tf_op jit(solution)/shard_map/ppermute | solution.py:240
  52.5 21.7 %all_to_all.5 = f32[8,32,256]{2,1,0:T(8,128)S(1)} all-to-all(f32[8,32,256]{2,1,0:T(8,128)S(1)} %add.14), channel_id=1, replica_groups=mesh['rep'=4,'grid'=8] {'grid'}, dimensions={0} | all-to-all | bytes 524288 | tf_op jit(solution)/shard_map/all_to_all | solution.py:305
  74.2 1.3 %collective-permute-start.13 = (f32[32,256]{1,0:T(8,128)S(1)}, f32[32,256]{1,0:T(8,128)S(1)}, u32[]{:S(2)}, u32[]{:S(2)}) collective-permute-start(f32[32,256]{1,0:T(8,128)S(1)} %reduce_sum.9), channel_id=1, source_target_pairs={{0,16},{8,24},{16,0},{24,8},{1,17},{9,25},{17,1},{25,9},{2,18},{10... | collective-permute-start | bytes 98312 | tf_op jit(solution)/shard_map/ppermute | solution.py:240
  75.5 0.0 collective-permute-start.12
  75.5 0.9 %collective-permute-start.11 = (f32[32,256]{1,0:T(8,128)S(1)}, f32[32,256]{1,0:T(8,128)S(1)}, u32[]{:S(2)}, u32[]{:S(2)}) collective-permute-start(f32[32,256]{1,0:T(8,128)S(1)} %reduce_sum.9), channel_id=1, source_target_pairs={{0,8},{8,0},{16,24},{24,16},{1,9},{9,1},{17,25},{25,17},{2,10},{10... | collective-permute-start | bytes 98312 | tf_op jit(solution)/shard_map/ppermute | solution.py:240
  76.4 1.8 %collective-permute-done.13 = f32[32,256]{1,0:T(8,128)S(1)} collective-permute-done((f32[32,256]{1,0:T(8,128)S(1)}, f32[32,256]{1,0:T(8,128)S(1)}, u32[]{:S(2)}, u32[]{:S(2)}) %collective-permute-start.13) | collective-permute-done | bytes 32800 | tf_op jit(solution)/shard_map/ppermute | solution.py:240
  78.2 0.7 collective-permute-done.12
  78.9 0.0 collective-permute-done.11
  78.9 0.6 pad_maximum_fusion
  (3 shorter events, 0.1 us)
Async XLA Ops:
  0.0 6.9 %copy-start = (bf16[128,256]{1,0:T(8,128)(2,1)S(1)}, bf16[128,256]{1,0:T(8,128)(2,1)}, u32[]{:S(2)}) copy-start(bf16[128,256]{1,0:T(8,128)(2,1)} %refs_0_.1) | copy-start | bytes 196612
  0.0 5.7 %collective-permute-start.1 = (bf16[128,256]{1,0:T(8,128)(2,1)}, bf16[128,256]{1,0:T(8,128)(2,1)S(1)}, u32[]{:S(2)}, u32[]{:S(2)}) collective-permute-start(bf16[128,256]{1,0:T(8,128)(2,1)} %refs_0_.1), channel_id=1, source_target_pairs={{0,16},{8,24},{16,0},{24,8},{1,17},{9,25},{17,1},{25,9},{2,18},{10... | collective-permute-start | bytes 196616 | tf_op jit(solution)/shard_map/ppermute | solution.py:240
  3.0 2.8 %collective-permute-start = (bf16[128,256]{1,0:T(8,128)(2,1)}, bf16[128,256]{1,0:T(8,128)(2,1)S(1)}, u32[]{:S(2)}, u32[]{:S(2)}) collective-permute-start(bf16[128,256]{1,0:T(8,128)(2,1)} %refs_0_.1), channel_id=1, source_target_pairs={{0,8},{8,0},{16,24},{24,16},{1,9},{9,1},{17,25},{25,17},{2,10},{10... | collective-permute-start | bytes 196616 | tf_op jit(solution)/shard_map/ppermute | solution.py:240
  3.0 4.0 %collective-permute-start.2 = (bf16[128,256]{1,0:T(8,128)(2,1)}, bf16[128,256]{1,0:T(8,128)(2,1)S(1)}, u32[]{:S(2)}, u32[]{:S(2)}) collective-permute-start(bf16[128,256]{1,0:T(8,128)(2,1)} %refs_0_.1), channel_id=1, source_target_pairs={{0,24},{8,16},{16,8},{24,0},{1,25},{9,17},{17,9},{25,1},{2,26},{10... | collective-permute-start | bytes 196616 | tf_op jit(solution)/shard_map/ppermute | solution.py:240
  8.5 15.8 %collective-permute-start.3 = (bf16[1,64,2048]{2,1,0:T(8,128)(2,1)S(1)}, bf16[1,64,2048]{2,1,0:T(8,128)(2,1)S(1)}, u32[]{:S(2)}, u32[]{:S(2)}) collective-permute-start(bf16[1,64,2048]{2,1,0:T(8,128)(2,1)S(1)} %get-tuple-element.22.skipped), channel_id=1, source_target_pairs={{0,4},{1,5},{2,6},{3,7},{4,0},{5,1},{6,2},{7,3},{8,12},{9,13},{10,... | collective-permute-start | bytes 786440 | tf_op jit(solution)/shard_map/ppermute | solution.py:240
  12.2 15.2 %collective-permute-start.4 = (bf16[1,64,2048]{2,1,0:T(8,128)(2,1)S(1)}, bf16[1,64,2048]{2,1,0:T(8,128)(2,1)S(1)}, u32[]{:S(2)}, u32[]{:S(2)}) collective-permute-start(bf16[1,64,2048]{2,1,0:T(8,128)(2,1)S(1)} %get-tuple-element.25), channel_id=1, source_target_pairs={{0,1},{1,0},{2,3},{3,2},{4,5},{5,4},{6,7},{7,6},{8,9},{9,8},{10,11... | collective-permute-start | bytes 786440 | tf_op jit(solution)/shard_map/ppermute | solution.py:240
  13.8 19.3 %collective-permute-start.5 = (bf16[1,64,2048]{2,1,0:T(8,128)(2,1)S(1)}, bf16[1,64,2048]{2,1,0:T(8,128)(2,1)S(1)}, u32[]{:S(2)}, u32[]{:S(2)}) collective-permute-start(bf16[1,64,2048]{2,1,0:T(8,128)(2,1)S(1)} %get-tuple-element.26), channel_id=1, source_target_pairs={{0,2},{1,3},{2,0},{3,1},{4,6},{5,7},{6,4},{7,5},{8,10},{9,11},{10,... | collective-permute-start | bytes 786440 | tf_op jit(solution)/shard_map/ppermute | solution.py:240
  15.4 33.5 %collective-permute-start.6 = (bf16[1,64,2048]{2,1,0:T(8,128)(2,1)S(1)}, bf16[1,64,2048]{2,1,0:T(8,128)(2,1)S(1)}, u32[]{:S(2)}, u32[]{:S(2)}) collective-permute-start(bf16[1,64,2048]{2,1,0:T(8,128)(2,1)S(1)} %get-tuple-element.27), channel_id=1, source_target_pairs={{0,3},{1,2},{2,1},{3,0},{4,7},{5,6},{6,5},{7,4},{8,11},{9,10},{10,... | collective-permute-start | bytes 786440 | tf_op jit(solution)/shard_map/ppermute | solution.py:240
  16.8 32.8 %collective-permute-start.7 = (bf16[1,64,2048]{2,1,0:T(8,128)(2,1)S(1)}, bf16[1,64,2048]{2,1,0:T(8,128)(2,1)S(1)}, u32[]{:S(2)}, u32[]{:S(2)}) collective-permute-start(bf16[1,64,2048]{2,1,0:T(8,128)(2,1)S(1)} %get-tuple-element.28), channel_id=1, source_target_pairs={{0,5},{1,4},{2,7},{3,6},{4,1},{5,0},{6,3},{7,2},{8,13},{9,12},{10,... | collective-permute-start | bytes 786440 | tf_op jit(solution)/shard_map/ppermute | solution.py:240
  24.3 25.3 %collective-permute-start.8 = (bf16[1,64,2048]{2,1,0:T(8,128)(2,1)S(1)}, bf16[1,64,2048]{2,1,0:T(8,128)(2,1)S(1)}, u32[]{:S(2)}, u32[]{:S(2)}) collective-permute-start(bf16[1,64,2048]{2,1,0:T(8,128)(2,1)S(1)} %get-tuple-element.29), channel_id=1, source_target_pairs={{0,6},{1,7},{2,4},{3,5},{4,2},{5,3},{6,0},{7,1},{8,14},{9,15},{10,... | collective-permute-start | bytes 786440 | tf_op jit(solution)/shard_map/ppermute | solution.py:240
  27.4 22.2 %collective-permute-start.9 = (bf16[1,64,2048]{2,1,0:T(8,128)(2,1)S(1)}, bf16[1,64,2048]{2,1,0:T(8,128)(2,1)S(1)}, u32[]{:S(2)}, u32[]{:S(2)}) collective-permute-start(bf16[1,64,2048]{2,1,0:T(8,128)(2,1)S(1)} %get-tuple-element.30), channel_id=1, source_target_pairs={{0,7},{1,6},{2,5},{3,4},{4,3},{5,2},{6,1},{7,0},{8,15},{9,14},{10,... | collective-permute-start | bytes 786440 | tf_op jit(solution)/shard_map/ppermute | solution.py:240
  50.8 1.6 %collective-permute-start.10 = (f32[8,32,256]{2,1,0:T(8,128)S(1)}, f32[8,32,256]{2,1,0:T(8,128)S(1)}, u32[]{:S(2)}, u32[]{:S(2)}) collective-permute-start(f32[8,32,256]{2,1,0:T(8,128)S(1)} %get-tuple-element.32), channel_id=1, source_target_pairs={{0,8},{8,0},{16,24},{24,16},{1,9},{9,1},{17,25},{25,17},{2,10},{10... | collective-permute-start | bytes 786440 | tf_op jit(solution)/shard_map/ppermute | solution.py:240
  74.2 4.0 %collective-permute-start.13 = (f32[32,256]{1,0:T(8,128)S(1)}, f32[32,256]{1,0:T(8,128)S(1)}, u32[]{:S(2)}, u32[]{:S(2)}) collective-permute-start(f32[32,256]{1,0:T(8,128)S(1)} %reduce_sum.9), channel_id=1, source_target_pairs={{0,16},{8,24},{16,0},{24,8},{1,17},{9,25},{17,1},{25,9},{2,18},{10... | collective-permute-start | bytes 98312 | tf_op jit(solution)/shard_map/ppermute | solution.py:240
  75.5 3.4 %collective-permute-start.12 = (f32[32,256]{1,0:T(8,128)S(1)}, f32[32,256]{1,0:T(8,128)S(1)}, u32[]{:S(2)}, u32[]{:S(2)}) collective-permute-start(f32[32,256]{1,0:T(8,128)S(1)} %reduce_sum.9), channel_id=1, source_target_pairs={{0,24},{8,16},{16,8},{24,0},{1,25},{9,17},{17,9},{25,1},{2,26},{10... | collective-permute-start | bytes 98312 | tf_op jit(solution)/shard_map/ppermute | solution.py:240
  75.5 3.4 %collective-permute-start.11 = (f32[32,256]{1,0:T(8,128)S(1)}, f32[32,256]{1,0:T(8,128)S(1)}, u32[]{:S(2)}, u32[]{:S(2)}) collective-permute-start(f32[32,256]{1,0:T(8,128)S(1)} %reduce_sum.9), channel_id=1, source_target_pairs={{0,8},{8,0},{16,24},{24,16},{1,9},{9,1},{17,25},{25,17},{2,10},{10... | collective-permute-start | bytes 98312 | tf_op jit(solution)/shard_map/ppermute | solution.py:240

commit v4 on v3

--- a/solution.py
+++ b/solution.py
@@ -136,8 +136,7 @@
     full, turned, *made = pl.pallas_call(
         functools.partial(first_kernel, group_starts, place, len(parts)),
         out_shape=[jax.ShapeDtypeStruct(shape, jnp.bfloat16) for shape in shapes],
-        in_specs=[pl.BlockSpec(memory_space=pltpu.SMEM)]
-        + [pl.BlockSpec(memory_space=pltpu.VMEM)] * (1 + len(parts)),
+        in_specs=[pl.BlockSpec(memory_space=pltpu.VMEM)] * (2 + len(parts)),
         out_specs=[pl.BlockSpec(memory_space=pltpu.VMEM)] * len(shapes),
         scratch_shapes=[pltpu.VMEM((slots * width, norb), jnp.bfloat16)],
         compiler_params=pltpu.CompilerParams(vmem_limit_bytes=VMEM_LIMIT),
@@ -166,74 +165,79 @@
     return jnp.concatenate([ref[:, :, lanes].reshape(-1, ref[:, :, lanes].shape[2]) for ref in refs], axis=0)
 
 
-def fit_kernel(step, ids, orb_ref, *refs):
-    rows, out_ref = refs[:-1], refs[-1]
-    turned = orbital_rows(orb_ref, rows[0].shape[1], ids())
+def fit_kernel(step, width, early_ids, late_ids, orb_ref, *refs):
+    rows, (out_ref, *late_ref) = refs[:-1 - bool(late_ids)], refs[-1 - bool(late_ids):]
+    turned = orbital_rows(orb_ref, width, early_ids())
     for at in range(out_ref.shape[1] // step):
         lanes = slice(at * step, (at + 1) * step)
         out_ref[:, lanes] = jnp.dot(turned, joined(rows, lanes), preferred_element_type=jnp.float32)
-
-
-def fit(orbitals, rows, ids):
-    width, cols = rows[0].shape[1:]
-    number = sum(each.shape[0] for each in rows)
+    if late_ids:
+        late_ref[0][...] = orbital_rows(orb_ref, width, late_ids())
+
+
+def fit(orbitals, early, n_late, early_ids, late_ids):
+    width, cols = early[0].shape[1:]
+    number = sum(each.shape[0] for each in early)
     norb = orbitals.shape[1]
+    shapes = [jax.ShapeDtypeStruct((norb, cols), jnp.float32)]
+    if n_late:
+        shapes.append(jax.ShapeDtypeStruct((norb, n_late * width), jnp.bfloat16))
     return pl.pallas_call(
-        functools.partial(fit_kernel, min(512, cols), ids),
-        out_shape=jax.ShapeDtypeStruct((norb, cols), jnp.float32),
-        in_specs=[pl.BlockSpec(memory_space=pltpu.VMEM)] * (1 + len(rows)),
-        out_specs=pl.BlockSpec(memory_space=pltpu.VMEM),
+        functools.partial(fit_kernel, min(512, cols), width, early_ids, late_ids),
+        out_shape=shapes,
+        in_specs=[pl.BlockSpec(memory_space=pltpu.VMEM)] * (1 + len(early)),
+        out_specs=[pl.BlockSpec(memory_space=pltpu.VMEM)] * len(shapes),
         compiler_params=pltpu.CompilerParams(vmem_limit_bytes=VMEM_LIMIT),
         cost_estimate=pl.CostEstimate(
             flops=2 * number * width * cols * norb,
             bytes_accessed=2 * number * width * cols + 4 * norb * cols,
             transcendentals=0,
         ),
-    )(orbitals, *rows)
-
-
-def action_kernel(fit_scale, mix_scale, step, early_ids, late_ids, n_early, fitted_ref, orb_ref, *refs):
-    early, late, (keep_ref, send_ref, fitted) = refs[:n_early], refs[n_early:-3], refs[-3:]
-    width, cols = early[0].shape[1:]
-    norb = orb_ref.shape[1]
+    )(orbitals, *early)
+
+
+def action_kernel(fit_scale, mix_scale, step, width, ids, n_early, n_late, fitted_ref, *refs):
+    early, late, (keep_ref, send_ref, fitted) = refs[:n_early], refs[n_early:n_early + n_late], refs[-3:]
+    norb, cols = fitted_ref.shape
     upper = lax.axis_index("rep") % 2 == 1
     if late:
-        turned = orbital_rows(orb_ref, width, late_ids())
+        turned = refs[n_early + n_late][...]
     for at in range(cols // step):
         lanes = slice(at * step, (at + 1) * step)
         total = fitted_ref[:, lanes]
         if late:
             total = total + jnp.dot(turned, joined(late, lanes), preferred_element_type=jnp.float32)
         fitted[:, lanes] = (fit_scale * total).astype(jnp.bfloat16)
-    parts = [(early_ids(), early)]
-    if late:
-        parts.append((late_ids(), late))
-    for ids, rows in parts:
-        term = lax.dot_general(joined(rows), fitted[...], (((1,), (1,)), ((), ())), preferred_element_type=jnp.float32)
-        term = (-mix_scale * term).reshape(len(ids), 2, width // 2, norb)
-        keep = jnp.where(upper, term[:, 1], term[:, 0])
-        send = jnp.where(upper, term[:, 0], term[:, 1])
-        for k, b in enumerate(ids):
-            keep_ref[b] = keep[k]
-            send_ref[b] = send[k]
-
-
-def action(orbitals, fitted, early, late, early_ids, late_ids, fit_scale, mix_scale):
-    width, cols = early[0].shape[1:]
-    blocks = orbitals.shape[0] // width
-    norb = orbitals.shape[1]
+    term = lax.dot_general(
+        joined(early + late), fitted[...], (((1,), (1,)), ((), ())), preferred_element_type=jnp.float32
+    )
+    blocks = ids()
+    term = (-mix_scale * term).reshape(len(blocks), 2, width // 2, norb)
+    keep = jnp.where(upper, term[:, 1], term[:, 0])
+    send = jnp.where(upper, term[:, 0], term[:, 1])
+    for k, b in enumerate(blocks):
+        keep_ref[b] = keep[k]
+        send_ref[b] = send[k]
+
+
+def action(fitted, early, late, ids, basis_rows, fit_scale, mix_scale):
+    norb, cols = fitted[0].shape
+    width = early[0].shape[1]
+    blocks = basis_rows // width
     shape = jax.ShapeDtypeStruct((blocks, width // 2, norb), jnp.float32)
     return pl.pallas_call(
-        functools.partial(action_kernel, fit_scale, mix_scale, min(512, cols), early_ids, late_ids, len(early)),
+        functools.partial(
+            action_kernel, fit_scale, mix_scale, min(512, cols), width, ids, len(early), len(late)
+        ),
         out_shape=[shape, shape],
-        in_specs=[pl.BlockSpec(memory_space=pltpu.VMEM)] * (2 + len(early) + len(late)),
+        in_specs=[pl.BlockSpec(memory_space=pltpu.VMEM)] * (len(fitted) + len(early) + len(late)),
         out_specs=[pl.BlockSpec(memory_space=pltpu.VMEM)] * 2,
         scratch_shapes=[pltpu.VMEM((norb, cols), jnp.bfloat16)],
         compiler_params=pltpu.CompilerParams(vmem_limit_bytes=VMEM_LIMIT),
         cost_estimate=pl.CostEstimate(
             flops=4 * blocks * width * cols * norb, bytes_accessed=2 * blocks * width * cols, transcendentals=0
         ),
-    )(fitted, orbitals, *early, *late)
+    )(fitted[0], *early, *late, *fitted[1:])
 
 
 def swapped(x, axis, k):
@@ -272,7 +276,7 @@
         def shapes(ks):
             return [(1, width, cols)] * len(ks)
 
-        waves, late_ks = [[4], [0, 1, 2, 3], [5, 6, 7]], [5, 6, 7]
+        waves, late_ks = [[6], [0, 1, 2, 3], [4, 5, 7]], [4, 5, 7]
         full, turned, made = contract_first(
             starts(waves[0]), own_output, shapes(waves[0]), block, inside, parts
         )
@@ -283,7 +287,7 @@
         received = {k: swapped(sent[k], "grid", k) if k else sent[k] for wave in waves for k in wave}
         early_ks = [k for wave in waves for k in wave if k not in late_ks]
         early, late = [received[k] for k in early_ks], [received[k] for k in late_ks]
-        early_ids, late_ids = ids(early_ks), ids(late_ks)
+        early_ids, late_ids, all_ids = ids(early_ks), ids(late_ks), ids(early_ks + late_ks)
     else:
         def place(s, k):
             part, col = divmod(s * SUB + k, per_part)
@@ -298,9 +302,9 @@
         def early_ids():
             return list(range(grid_size))
 
-        late_ids = None
-    fitted = fit(full, early, early_ids)
-    part_keep, part_send = action(full, fitted, early, late, early_ids, late_ids, fit_scale, mix_scale)
+        late_ids, all_ids = None, early_ids
+    fitted = fit(full, early, len(late), early_ids, late_ids)
+    part_keep, part_send = action(fitted, early, late, all_ids, basis_rows, fit_scale, mix_scale)
     pair = part_keep + swapped(part_send, "rep", 1)
     mine = jnp.sum(lax.all_to_all(pair, "grid", 0, 0, tiled=True), axis=0)
     if rep_size == 4:

time: 79.7 us -> 78.2 us (0.981)
  blocking collectives: 21.7 us -> 17.1 us
  starting transfers between devices: 17.7 us -> 21.4 us
    all_to_all x1, blocking collectives: 21.7 us -> 17.1 us  [per_device(): mine = jnp.sum(lax.all_to_all(pair, 'grid', 0, 0, tiled=True), axis=0)]
    ppermute x14, starting transfers between devices: 17.7 us -> 21.4 us  [swapped(): lax.ppermute(x, axis, [(i, i ^ k) for i in range(lax.axis_size(axis))])]
  transfers between devices with their start and end apart: 14 -> 14, of which waited for: 7 -> 8; matrix products, arithmetic and copies ran while one was open for 0% -> 0% of each run, Pallas kernels for 6% -> 6%
where the time goes in v4:
time: 78.2 us; the launch traced here: 78 us
  waiting for transfers between devices  31.3 us (40%)
  starting transfers between devices  21.4 us (27%)
  blocking collectives  17.1 us (22%)
  Pallas kernels  6.87 us (9%)
    ppermute x14, waiting for transfers between devices, swapped(): lax.ppermute(x, axis, [(i, i ^ k) for i in range(lax.axis_size(axis))])  31.3 us
    ppermute x14, starting transfers between devices, swapped(): lax.ppermute(x, axis, [(i, i ^ k) for i in range(lax.axis_size(axis))])  21.4 us
    all_to_all x1, blocking collectives, per_device(): mine = jnp.sum(lax.all_to_all(pair, 'grid', 0, 0, tiled=True), axis=0)  17.1 us
    pallas_call x2, Pallas kernels, contract_next(): pl.pallas_call(functools.partial(next_kernel, group_starts, place), out_s...  2.09 us
    pallas_call x1, Pallas kernels, load(): pl.pallas_call(load_kernel, out_shape=[jax.ShapeDtypeStruct(tiles.shape[2...  1.91 us
  transfers between devices with their start and end apart: 14, of which 8 were waited for; matrix products, arithmetic and copies ran while one was open for 0% of the time, Pallas kernels for 6%

profile of v4, /device:TPU:0, one launch (start us, length us, event | category | flops | bytes accessed | tf_op | source)
XLA Modules:
  0.0 78.0 jit_solution(16296497833667858806)
XLA Ops:
  0.0 0.0 copy-start
  0.0 3.0 %collective-permute-start.1 = (bf16[128,256]{1,0:T(8,128)(2,1)}, bf16[128,256]{1,0:T(8,128)(2,1)S(1)}, u32[]{:S(2)}, u32[]{:S(2)}) collective-permute-start(bf16[128,256]{1,0:T(8,128)(2,1)} %refs_0_.1), channel_id=1, source_target_pairs={{0,16},{8,24},{16,0},{24,8},{1,17},{9,25},{17,1},{25,9},{2,18},{10... | collective-permute-start | bytes 196616 | tf_op jit(solution)/shard_map/ppermute | solution.py:244
  3.0 0.0 collective-permute-start
  3.0 0.2 collective-permute-start.2
  3.8 1.9 %shard_map.46 = (bf16[6,64,4096]{2,1,0:T(8,128)(2,1)S(1)}, s32[1,6]{1,0:T(1,128)S(1)}) custom-call(s32[1,1]{1,0:T(1,128)S(6)} %copy.5.count_ref, s32[1,1,6]{2,1,0:T(1,128)} %block_hbm.1, bf16[1,1,6,64,4096]{4,3,2,1,0:T(8,128)(2,1)} %tiles_hbm.1), custom_call_target="tpu_custom_call" | custom-call | bytes 3145728 | tf_op jit(solution)/shard_map/pallas_call | solution.py:41
  5.7 0.0 collective-permute-done.1.refs_2_
  5.7 0.0 collective-permute-done.refs_1_
  5.8 1.2 %collective-permute-done.2.refs_3_ = bf16[128,256]{1,0:T(8,128)(2,1)S(1)} collective-permute-done((bf16[128,256]{1,0:T(8,128)(2,1)}, bf16[128,256]{1,0:T(8,128)(2,1)S(1)}, u32[]{:S(2)}, u32[]{:S(2)}) %collective-permute-start.2) | collective-permute-done | bytes 65568 | tf_op jit(solution)/shard_map/ppermute | solution.py:244
  6.9 0.0 copy-done
  6.9 1.1 %shard_map.47 = (bf16[512,256]{1,0:T(8,128)(2,1)S(1)}, bf16[256,384]{1,0:T(8,128)(2,1)S(1)}, bf16[1,64,2048]{2,1,0:T(8,128)(2,1)S(1)}) custom-call(s32[1,6]{1,0:T(1,128)S(1)} %get-tuple-element.21.block_ref, bf16[6,64,4096]{2,1,0:T(8,128)(2,1)S(1)} %get-tuple-element.22.tiles_ref, bf16[128,256]{1,0:T(8,128)(2,1)S(1)} %copy-done, ...), custom_call_target="tpu_custom_call" | custom-call | flops 100663296 | bytes 3407872 | tf_op jit(solution)/shard_map/pallas_call | solution.py:136
  8.0 3.7 %collective-permute-start.3 = (bf16[1,64,2048]{2,1,0:T(8,128)(2,1)S(1)}, bf16[1,64,2048]{2,1,0:T(8,128)(2,1)S(1)}, u32[]{:S(2)}, u32[]{:S(2)}) collective-permute-start(bf16[1,64,2048]{2,1,0:T(8,128)(2,1)S(1)} %get-tuple-element.24.skipped), channel_id=1, source_target_pairs={{0,6},{1,7},{2,4},{3,5},{4,2},{5,3},{6,0},{7,1},{8,14},{9,15},{10,... | collective-permute-start | bytes 786440 | tf_op jit(solution)/shard_map/ppermute | solution.py:244
  11.7 1.1 %shard_map.48 = (bf16[1,64,2048]{2,1,0:T(8,128)(2,1)S(1)}, bf16[1,64,2048]{2,1,0:T(8,128)(2,1)S(1)}, bf16[1,64,2048]{2,1,0:T(8,128)(2,1)S(1)}, bf16[1,64,2048]{2,1,0:T(8,128)(2,1)S(1)}) custom-call(bf16[256,384]{1,0:T(8,128)(2,1)S(1)} %get-tuple-element.25.turned_ref, bf16[6,64,4096]{2,1,0:T(8,128)(2,1)S(1)} %get-tuple-element.22.tiles_ref, ...), custom_call_target="tpu_custom_call" | custom-call | flops 402653184 | bytes 4194304 | tf_op jit(solution)/shard_map/pallas_call | solution.py:149
  12.8 1.6 %collective-permute-start.4 = (bf16[1,64,2048]{2,1,0:T(8,128)(2,1)S(1)}, bf16[1,64,2048]{2,1,0:T(8,128)(2,1)S(1)}, u32[]{:S(2)}, u32[]{:S(2)}) collective-permute-start(bf16[1,64,2048]{2,1,0:T(8,128)(2,1)S(1)} %get-tuple-element.27), channel_id=1, source_target_pairs={{0,1},{1,0},{2,3},{3,2},{4,5},{5,4},{6,7},{7,6},{8,9},{9,8},{10,11... | collective-permute-start | bytes 786440 | tf_op jit(solution)/shard_map/ppermute | solution.py:244
  14.3 0.0 collective-permute-start.5
  14.3 2.0 %collective-permute-start.6 = (bf16[1,64,2048]{2,1,0:T(8,128)(2,1)S(1)}, bf16[1,64,2048]{2,1,0:T(8,128)(2,1)S(1)}, u32[]{:S(2)}, u32[]{:S(2)}) collective-permute-start(bf16[1,64,2048]{2,1,0:T(8,128)(2,1)S(1)} %get-tuple-element.29), channel_id=1, source_target_pairs={{0,3},{1,2},{2,1},{3,0},{4,7},{5,6},{6,5},{7,4},{8,11},{9,10},{10,... | collective-permute-start | bytes 786440 | tf_op jit(solution)/shard_map/ppermute | solution.py:244
  16.3 1.0 %shard_map.50 = (bf16[1,64,2048]{2,1,0:T(8,128)(2,1)S(1)}, bf16[1,64,2048]{2,1,0:T(8,128)(2,1)S(1)}, bf16[1,64,2048]{2,1,0:T(8,128)(2,1)S(1)}) custom-call(bf16[256,384]{1,0:T(8,128)(2,1)S(1)} %get-tuple-element.25.turned_ref, bf16[6,64,4096]{2,1,0:T(8,128)(2,1)S(1)} %get-tuple-element.22.tiles_ref, bf16[1,64,2048]{2,1,0:T(8,128)(2,1)S(1)} %get-tuple-element.26.refs_1_.skipped), custom_call_target="tpu_custom_call" | custom-call | flops 301989888 | bytes 3932160 | tf_op jit(solution)/shard_map/pallas_call | solution.py:149
  17.4 0.1 collective-permute-start.7
  17.5 1.6 %collective-permute-done.3.refs_0_ = bf16[1,64,2048]{2,1,0:T(8,128)(2,1)S(1)} collective-permute-done((bf16[1,64,2048]{2,1,0:T(8,128)(2,1)S(1)}, bf16[1,64,2048]{2,1,0:T(8,128)(2,1)S(1)}, u32[]{:S(2)}, u32[]{:S(2)}) %collective-permute-start.3) | collective-permute-done | bytes 262176 | tf_op jit(solution)/shard_map/ppermute | solution.py:244
  19.0 7.3 %collective-permute-start.8 = (bf16[1,64,2048]{2,1,0:T(8,128)(2,1)S(1)}, bf16[1,64,2048]{2,1,0:T(8,128)(2,1)S(1)}, u32[]{:S(2)}, u32[]{:S(2)}) collective-permute-start(bf16[1,64,2048]{2,1,0:T(8,128)(2,1)S(1)} %get-tuple-element.32), channel_id=1, source_target_pairs={{0,5},{1,4},{2,7},{3,6},{4,1},{5,0},{6,3},{7,2},{8,13},{9,12},{10,... | collective-permute-start | bytes 786440 | tf_op jit(solution)/shard_map/ppermute | solution.py:244
  26.4 0.0 collective-permute-done.4.refs_2_
  26.4 1.3 %collective-permute-start.9 = (bf16[1,64,2048]{2,1,0:T(8,128)(2,1)S(1)}, bf16[1,64,2048]{2,1,0:T(8,128)(2,1)S(1)}, u32[]{:S(2)}, u32[]{:S(2)}) collective-permute-start(bf16[1,64,2048]{2,1,0:T(8,128)(2,1)S(1)} %get-tuple-element.33), channel_id=1, source_target_pairs={{0,7},{1,6},{2,5},{3,4},{4,3},{5,2},{6,1},{7,0},{8,15},{9,14},{10,... | collective-permute-start | bytes 786440 | tf_op jit(solution)/shard_map/ppermute | solution.py:244
  27.7 3.4 %collective-permute-done.5.refs_3_ = bf16[1,64,2048]{2,1,0:T(8,128)(2,1)S(1)} collective-permute-done((bf16[1,64,2048]{2,1,0:T(8,128)(2,1)S(1)}, bf16[1,64,2048]{2,1,0:T(8,128)(2,1)S(1)}, u32[]{:S(2)}, u32[]{:S(2)}) %collective-permute-start.5) | collective-permute-done | bytes 262176 | tf_op jit(solution)/shard_map/ppermute | solution.py:244
  31.0 6.5 %collective-permute-done.6.refs_4_ = bf16[1,64,2048]{2,1,0:T(8,128)(2,1)S(1)} collective-permute-done((bf16[1,64,2048]{2,1,0:T(8,128)(2,1)S(1)}, bf16[1,64,2048]{2,1,0:T(8,128)(2,1)S(1)}, u32[]{:S(2)}, u32[]{:S(2)}) %collective-permute-start.6) | collective-permute-done | bytes 262176 | tf_op jit(solution)/shard_map/ppermute | solution.py:244
  37.5 0.7 shard_map.49
  38.2 0.0 collective-permute-done.7.refs_5_
  38.2 14.7 %collective-permute-done.8.refs_6_ = bf16[1,64,2048]{2,1,0:T(8,128)(2,1)S(1)} collective-permute-done((bf16[1,64,2048]{2,1,0:T(8,128)(2,1)S(1)}, bf16[1,64,2048]{2,1,0:T(8,128)(2,1)S(1)}, u32[]{:S(2)}, u32[]{:S(2)}) %collective-permute-start.8) | collective-permute-done | bytes 262176 | tf_op jit(solution)/shard_map/ppermute | solution.py:244
  52.9 0.0 collective-permute-done.9.refs_7_
  52.9 1.0 %shard_map.51 = (f32[8,32,256]{2,1,0:T(8,128)S(1)}, f32[8,32,256]{2,1,0:T(8,128)S(1)}) custom-call(f32[256,2048]{1,0:T(8,128)S(1)} %get-tuple-element.30.fitted_ref, bf16[1,64,2048]{2,1,0:T(8,128)(2,1)S(1)} %collective-permute-done.3.refs_0_, bf16[1,64,2048]{2,1,0:T(8,128)(2,1)S(1)} %get-tuple-element.26.refs_1_.skipped, ...), custom_call_target="tpu_custom_call" | custom-call | flops 1073741824 | bytes 2097152 | tf_op jit(solution)/shard_map/pallas_call | solution.py:228
  53.9 0.1 collective-permute-start.10
  54.0 1.5 %collective-permute-done.10 = f32[8,32,256]{2,1,0:T(8,128)S(1)} collective-permute-done((f32[8,32,256]{2,1,0:T(8,128)S(1)}, f32[8,32,256]{2,1,0:T(8,128)S(1)}, u32[]{:S(2)}, u32[]{:S(2)}) %collective-permute-start.10) | collective-permute-done | bytes 262176 | tf_op jit(solution)/shard_map/ppermute | solution.py:244
  55.6 17.1 %all_to_all.5 = f32[8,32,256]{2,1,0:T(8,128)S(1)} all-to-all(f32[8,32,256]{2,1,0:T(8,128)S(1)} %add.14), channel_id=1, replica_groups=mesh['rep'=4,'grid'=8] {'grid'}, dimensions={0} | all-to-all | bytes 524288 | tf_op jit(solution)/shard_map/all_to_all | solution.py:309
  72.7 1.3 %collective-permute-start.13 = (f32[32,256]{1,0:T(8,128)S(1)}, f32[32,256]{1,0:T(8,128)S(1)}, u32[]{:S(2)}, u32[]{:S(2)}) collective-permute-start(f32[32,256]{1,0:T(8,128)S(1)} %reduce_sum.9), channel_id=1, source_target_pairs={{0,16},{8,24},{16,0},{24,8},{1,17},{9,25},{17,1},{25,9},{2,18},{10... | collective-permute-start | bytes 98312 | tf_op jit(solution)/shard_map/ppermute | solution.py:244
  73.9 0.0 collective-permute-start.12
  73.9 0.9 %collective-permute-start.11 = (f32[32,256]{1,0:T(8,128)S(1)}, f32[32,256]{1,0:T(8,128)S(1)}, u32[]{:S(2)}, u32[]{:S(2)}) collective-permute-start(f32[32,256]{1,0:T(8,128)S(1)} %reduce_sum.9), channel_id=1, source_target_pairs={{0,8},{8,0},{16,24},{24,16},{1,9},{9,1},{17,25},{25,17},{2,10},{10... | collective-permute-start | bytes 98312 | tf_op jit(solution)/shard_map/ppermute | solution.py:244
  74.9 1.8 %collective-permute-done.13 = f32[32,256]{1,0:T(8,128)S(1)} collective-permute-done((f32[32,256]{1,0:T(8,128)S(1)}, f32[32,256]{1,0:T(8,128)S(1)}, u32[]{:S(2)}, u32[]{:S(2)}) %collective-permute-start.13) | collective-permute-done | bytes 32800 | tf_op jit(solution)/shard_map/ppermute | solution.py:244
  76.6 0.7 collective-permute-done.12
  77.3 0.0 collective-permute-done.11
  77.4 0.6 pad_maximum_fusion
  (3 shorter events, 0.1 us)
Async XLA Ops:
  0.0 6.9 %copy-start = (bf16[128,256]{1,0:T(8,128)(2,1)S(1)}, bf16[128,256]{1,0:T(8,128)(2,1)}, u32[]{:S(2)}) copy-start(bf16[128,256]{1,0:T(8,128)(2,1)} %refs_0_.1) | copy-start | bytes 196612
  0.0 5.7 %collective-permute-start.1 = (bf16[128,256]{1,0:T(8,128)(2,1)}, bf16[128,256]{1,0:T(8,128)(2,1)S(1)}, u32[]{:S(2)}, u32[]{:S(2)}) collective-permute-start(bf16[128,256]{1,0:T(8,128)(2,1)} %refs_0_.1), channel_id=1, source_target_pairs={{0,16},{8,24},{16,0},{24,8},{1,17},{9,25},{17,1},{25,9},{2,18},{10... | collective-permute-start | bytes 196616 | tf_op jit(solution)/shard_map/ppermute | solution.py:244
  3.0 2.8 %collective-permute-start = (bf16[128,256]{1,0:T(8,128)(2,1)}, bf16[128,256]{1,0:T(8,128)(2,1)S(1)}, u32[]{:S(2)}, u32[]{:S(2)}) collective-permute-start(bf16[128,256]{1,0:T(8,128)(2,1)} %refs_0_.1), channel_id=1, source_target_pairs={{0,8},{8,0},{16,24},{24,16},{1,9},{9,1},{17,25},{25,17},{2,10},{10... | collective-permute-start | bytes 196616 | tf_op jit(solution)/shard_map/ppermute | solution.py:244
  3.0 4.0 %collective-permute-start.2 = (bf16[128,256]{1,0:T(8,128)(2,1)}, bf16[128,256]{1,0:T(8,128)(2,1)S(1)}, u32[]{:S(2)}, u32[]{:S(2)}) collective-permute-start(bf16[128,256]{1,0:T(8,128)(2,1)} %refs_0_.1), channel_id=1, source_target_pairs={{0,24},{8,16},{16,8},{24,0},{1,25},{9,17},{17,9},{25,1},{2,26},{10... | collective-permute-start | bytes 196616 | tf_op jit(solution)/shard_map/ppermute | solution.py:244
  8.0 11.0 %collective-permute-start.3 = (bf16[1,64,2048]{2,1,0:T(8,128)(2,1)S(1)}, bf16[1,64,2048]{2,1,0:T(8,128)(2,1)S(1)}, u32[]{:S(2)}, u32[]{:S(2)}) collective-permute-start(bf16[1,64,2048]{2,1,0:T(8,128)(2,1)S(1)} %get-tuple-element.24.skipped), channel_id=1, source_target_pairs={{0,6},{1,7},{2,4},{3,5},{4,2},{5,3},{6,0},{7,1},{8,14},{9,15},{10,... | collective-permute-start | bytes 786440 | tf_op jit(solution)/shard_map/ppermute | solution.py:244
  12.8 13.6 %collective-permute-start.4 = (bf16[1,64,2048]{2,1,0:T(8,128)(2,1)S(1)}, bf16[1,64,2048]{2,1,0:T(8,128)(2,1)S(1)}, u32[]{:S(2)}, u32[]{:S(2)}) collective-permute-start(bf16[1,64,2048]{2,1,0:T(8,128)(2,1)S(1)} %get-tuple-element.27), channel_id=1, source_target_pairs={{0,1},{1,0},{2,3},{3,2},{4,5},{5,4},{6,7},{7,6},{8,9},{9,8},{10,11... | collective-permute-start | bytes 786440 | tf_op jit(solution)/shard_map/ppermute | solution.py:244
  14.3 16.7 %collective-permute-start.5 = (bf16[1,64,2048]{2,1,0:T(8,128)(2,1)S(1)}, bf16[1,64,2048]{2,1,0:T(8,128)(2,1)S(1)}, u32[]{:S(2)}, u32[]{:S(2)}) collective-permute-start(bf16[1,64,2048]{2,1,0:T(8,128)(2,1)S(1)} %get-tuple-element.28), channel_id=1, source_target_pairs={{0,2},{1,3},{2,0},{3,1},{4,6},{5,7},{6,4},{7,5},{8,10},{9,11},{10,... | collective-permute-start | bytes 786440 | tf_op jit(solution)/shard_map/ppermute | solution.py:244
  14.3 23.2 %collective-permute-start.6 = (bf16[1,64,2048]{2,1,0:T(8,128)(2,1)S(1)}, bf16[1,64,2048]{2,1,0:T(8,128)(2,1)S(1)}, u32[]{:S(2)}, u32[]{:S(2)}) collective-permute-start(bf16[1,64,2048]{2,1,0:T(8,128)(2,1)S(1)} %get-tuple-element.29), channel_id=1, source_target_pairs={{0,3},{1,2},{2,1},{3,0},{4,7},{5,6},{6,5},{7,4},{8,11},{9,10},{10,... | collective-permute-start | bytes 786440 | tf_op jit(solution)/shard_map/ppermute | solution.py:244
  17.4 20.9 %collective-permute-start.7 = (bf16[1,64,2048]{2,1,0:T(8,128)(2,1)S(1)}, bf16[1,64,2048]{2,1,0:T(8,128)(2,1)S(1)}, u32[]{:S(2)}, u32[]{:S(2)}) collective-permute-start(bf16[1,64,2048]{2,1,0:T(8,128)(2,1)S(1)} %get-tuple-element.31), channel_id=1, source_target_pairs={{0,4},{1,5},{2,6},{3,7},{4,0},{5,1},{6,2},{7,3},{8,12},{9,13},{10,... | collective-permute-start | bytes 786440 | tf_op jit(solution)/shard_map/ppermute | solution.py:244
  19.0 33.9 %collective-permute-start.8 = (bf16[1,64,2048]{2,1,0:T(8,128)(2,1)S(1)}, bf16[1,64,2048]{2,1,0:T(8,128)(2,1)S(1)}, u32[]{:S(2)}, u32[]{:S(2)}) collective-permute-start(bf16[1,64,2048]{2,1,0:T(8,128)(2,1)S(1)} %get-tuple-element.32), channel_id=1, source_target_pairs={{0,5},{1,4},{2,7},{3,6},{4,1},{5,0},{6,3},{7,2},{8,13},{9,12},{10,... | collective-permute-start | bytes 786440 | tf_op jit(solution)/shard_map/ppermute | solution.py:244
  26.4 26.6 %collective-permute-start.9 = (bf16[1,64,2048]{2,1,0:T(8,128)(2,1)S(1)}, bf16[1,64,2048]{2,1,0:T(8,128)(2,1)S(1)}, u32[]{:S(2)}, u32[]{:S(2)}) collective-permute-start(bf16[1,64,2048]{2,1,0:T(8,128)(2,1)S(1)} %get-tuple-element.33), channel_id=1, source_target_pairs={{0,7},{1,6},{2,5},{3,4},{4,3},{5,2},{6,1},{7,0},{8,15},{9,14},{10,... | collective-permute-start | bytes 786440 | tf_op jit(solution)/shard_map/ppermute | solution.py:244
  53.9 1.6 %collective-permute-start.10 = (f32[8,32,256]{2,1,0:T(8,128)S(1)}, f32[8,32,256]{2,1,0:T(8,128)S(1)}, u32[]{:S(2)}, u32[]{:S(2)}) collective-permute-start(f32[8,32,256]{2,1,0:T(8,128)S(1)} %get-tuple-element.36), channel_id=1, source_target_pairs={{0,8},{8,0},{16,24},{24,16},{1,9},{9,1},{17,25},{25,17},{2,10},{10... | collective-permute-start | bytes 786440 | tf_op jit(solution)/shard_map/ppermute | solution.py:244
  72.7 4.0 %collective-permute-start.13 = (f32[32,256]{1,0:T(8,128)S(1)}, f32[32,256]{1,0:T(8,128)S(1)}, u32[]{:S(2)}, u32[]{:S(2)}) collective-permute-start(f32[32,256]{1,0:T(8,128)S(1)} %reduce_sum.9), channel_id=1, source_target_pairs={{0,16},{8,24},{16,0},{24,8},{1,17},{9,25},{17,1},{25,9},{2,18},{10... | collective-permute-start | bytes 98312 | tf_op jit(solution)/shard_map/ppermute | solution.py:244
  73.9 3.4 %collective-permute-start.12 = (f32[32,256]{1,0:T(8,128)S(1)}, f32[32,256]{1,0:T(8,128)S(1)}, u32[]{:S(2)}, u32[]{:S(2)}) collective-permute-start(f32[32,256]{1,0:T(8,128)S(1)} %reduce_sum.9), channel_id=1, source_target_pairs={{0,24},{8,16},{16,8},{24,0},{1,25},{9,17},{17,9},{25,1},{2,26},{10... | collective-permute-start | bytes 98312 | tf_op jit(solution)/shard_map/ppermute | solution.py:244
  73.9 3.4 %collective-permute-start.11 = (f32[32,256]{1,0:T(8,128)S(1)}, f32[32,256]{1,0:T(8,128)S(1)}, u32[]{:S(2)}, u32[]{:S(2)}) collective-permute-start(f32[32,256]{1,0:T(8,128)S(1)} %reduce_sum.9), channel_id=1, source_target_pairs={{0,8},{8,0},{16,24},{24,16},{1,9},{9,1},{17,25},{25,17},{2,10},{10... | collective-permute-start | bytes 98312 | tf_op jit(solution)/shard_map/ppermute | solution.py:244

commit v5 on v4

--- a/solution.py
+++ b/solution.py
@@ -244,6 +244,16 @@
     return lax.ppermute(x, axis, [(i, i ^ k) for i in range(lax.axis_size(axis))])
 
 
+def summed_blocks(blocks, axis):
+    rows = blocks.shape[1]
+    largest = jnp.max(jnp.abs(blocks), axis=1, keepdims=True)
+    exponent = jnp.ceil(jnp.log2(jnp.maximum(largest, 1e-30)))
+    scaled = (blocks * jnp.exp2(-exponent)).astype(jnp.float16)
+    tail = jnp.broadcast_to(exponent.astype(jnp.float16), (blocks.shape[0], 8, blocks.shape[2]))
+    got = lax.all_to_all(jnp.concatenate([scaled, tail], axis=1), axis, 0, 0, tiled=True).astype(jnp.float32)
+    return jnp.sum(got[:, :rows] * jnp.exp2(got[:, rows:rows + 1]), axis=0)
+
+
 def per_device(orbitals, tiles, tile_block, tile_count):
     rep_size = lax.axis_size("rep")
     grid_size = lax.axis_size("grid")
@@ -276,7 +286,7 @@
         def shapes(ks):
             return [(1, width, cols)] * len(ks)
 
-        waves, late_ks = [[6], [0, 1, 2, 3], [4, 5, 7]], [4, 5, 7]
+        waves, late_ks = [[6], [0, 1, 2, 3], [5, 4, 7]], [5, 4, 7]
         full, turned, made = contract_first(
             starts(waves[0]), own_output, shapes(waves[0]), block, inside, parts
         )
@@ -306,7 +316,7 @@
     fitted = fit(full, early, len(late), early_ids, late_ids)
     part_keep, part_send = action(fitted, early, late, all_ids, basis_rows, fit_scale, mix_scale)
     pair = part_keep + swapped(part_send, "rep", 1)
-    mine = jnp.sum(lax.all_to_all(pair, "grid", 0, 0, tiled=True), axis=0)
+    mine = summed_blocks(pair, "grid")
     if rep_size == 4:
         other, across = swapped(mine, "rep", 2), swapped(mine, "rep", 3)
         beside = swapped(mine, "rep", 1)

time: 78.2 us -> 76.9 us (0.983)
  waiting for transfers between devices: 31.3 us -> 29.9 us
    ppermute x14, waiting for transfers between devices: 31.3 us -> 29.9 us  [swapped(): lax.ppermute(x, axis, [(i, i ^ k) for i in range(lax.axis_size(axis))])]
where the time goes in v5:
time: 76.9 us; the launch traced here: 76.8 us
  waiting for transfers between devices  29.9 us (39%)
  starting transfers between devices  21.8 us (28%)
  blocking collectives  16.5 us (21%)
  Pallas kernels  6.88 us (9%)
  other arithmetic  0.85 us (1%)
  between operations  0.8 us (1%)
    ppermute x14, waiting for transfers between devices, swapped(): lax.ppermute(x, axis, [(i, i ^ k) for i in range(lax.axis_size(axis))])  29.9 us
    ppermute x14, starting transfers between devices, swapped(): lax.ppermute(x, axis, [(i, i ^ k) for i in range(lax.axis_size(axis))])  21.8 us
    all_to_all x1, blocking collectives, summed_blocks(): lax.all_to_all(jnp.concatenate([scaled, tail], axis=1), axis, 0, 0, tiled...  16.5 us
    pallas_call x2, Pallas kernels, contract_next(): pl.pallas_call(functools.partial(next_kernel, group_starts, place), out_s...  2.1 us
    pallas_call x1, Pallas kernels, load(): pl.pallas_call(load_kernel, out_shape=[jax.ShapeDtypeStruct(tiles.shape[2...  1.91 us
  transfers between devices with their start and end apart: 14, of which 8 were waited for; matrix products, arithmetic and copies ran while one was open for 0% of the time, Pallas kernels for 6%

profile of v5, /device:TPU:0, one launch (start us, length us, event | category | flops | bytes accessed | tf_op | source)
XLA Modules:
  0.0 76.8 jit_solution(270714309845391034)
XLA Ops:
  0.0 0.0 copy-start
  0.0 3.0 %collective-permute-start.1 = (bf16[128,256]{1,0:T(8,128)(2,1)}, bf16[128,256]{1,0:T(8,128)(2,1)S(1)}, u32[]{:S(2)}, u32[]{:S(2)}) collective-permute-start(bf16[128,256]{1,0:T(8,128)(2,1)} %refs_0_.1), channel_id=1, source_target_pairs={{0,16},{8,24},{16,0},{24,8},{1,17},{9,25},{17,1},{25,9},{2,18},{10... | collective-permute-start | bytes 196616 | tf_op jit(solution)/shard_map/ppermute | solution.py:244
  3.0 0.0 collective-permute-start
  3.0 0.2 collective-permute-start.2
  3.8 1.9 %shard_map.46 = (bf16[6,64,4096]{2,1,0:T(8,128)(2,1)S(1)}, s32[1,6]{1,0:T(1,128)S(1)}) custom-call(s32[1,1]{1,0:T(1,128)S(6)} %copy.8.count_ref, s32[1,1,6]{2,1,0:T(1,128)} %block_hbm.1, bf16[1,1,6,64,4096]{4,3,2,1,0:T(8,128)(2,1)} %tiles_hbm.1), custom_call_target="tpu_custom_call" | custom-call | bytes 3145728 | tf_op jit(solution)/shard_map/pallas_call | solution.py:41
  5.7 0.0 collective-permute-done.1.refs_2_
  5.7 0.0 collective-permute-done.refs_1_
  5.8 1.2 %collective-permute-done.2.refs_3_ = bf16[128,256]{1,0:T(8,128)(2,1)S(1)} collective-permute-done((bf16[128,256]{1,0:T(8,128)(2,1)}, bf16[128,256]{1,0:T(8,128)(2,1)S(1)}, u32[]{:S(2)}, u32[]{:S(2)}) %collective-permute-start.2) | collective-permute-done | bytes 65568 | tf_op jit(solution)/shard_map/ppermute | solution.py:244
  6.9 0.0 copy-done
  6.9 1.1 %shard_map.47 = (bf16[512,256]{1,0:T(8,128)(2,1)S(1)}, bf16[256,384]{1,0:T(8,128)(2,1)S(1)}, bf16[1,64,2048]{2,1,0:T(8,128)(2,1)S(1)}) custom-call(s32[1,6]{1,0:T(1,128)S(1)} %get-tuple-element.21.block_ref, bf16[6,64,4096]{2,1,0:T(8,128)(2,1)S(1)} %get-tuple-element.22.tiles_ref, bf16[128,256]{1,0:T(8,128)(2,1)S(1)} %copy-done, ...), custom_call_target="tpu_custom_call" | custom-call | flops 100663296 | bytes 3407872 | tf_op jit(solution)/shard_map/pallas_call | solution.py:136
  8.0 3.7 %collective-permute-start.3 = (bf16[1,64,2048]{2,1,0:T(8,128)(2,1)S(1)}, bf16[1,64,2048]{2,1,0:T(8,128)(2,1)S(1)}, u32[]{:S(2)}, u32[]{:S(2)}) collective-permute-start(bf16[1,64,2048]{2,1,0:T(8,128)(2,1)S(1)} %get-tuple-element.24.skipped), channel_id=1, source_target_pairs={{0,6},{1,7},{2,4},{3,5},{4,2},{5,3},{6,0},{7,1},{8,14},{9,15},{10,... | collective-permute-start | bytes 786440 | tf_op jit(solution)/shard_map/ppermute | solution.py:244
  11.7 1.1 %shard_map.48 = (bf16[1,64,2048]{2,1,0:T(8,128)(2,1)S(1)}, bf16[1,64,2048]{2,1,0:T(8,128)(2,1)S(1)}, bf16[1,64,2048]{2,1,0:T(8,128)(2,1)S(1)}, bf16[1,64,2048]{2,1,0:T(8,128)(2,1)S(1)}) custom-call(bf16[256,384]{1,0:T(8,128)(2,1)S(1)} %get-tuple-element.25.turned_ref, bf16[6,64,4096]{2,1,0:T(8,128)(2,1)S(1)} %get-tuple-element.22.tiles_ref, ...), custom_call_target="tpu_custom_call" | custom-call | flops 402653184 | bytes 4194304 | tf_op jit(solution)/shard_map/pallas_call | solution.py:149
  12.8 1.6 %collective-permute-start.4 = (bf16[1,64,2048]{2,1,0:T(8,128)(2,1)S(1)}, bf16[1,64,2048]{2,1,0:T(8,128)(2,1)S(1)}, u32[]{:S(2)}, u32[]{:S(2)}) collective-permute-start(bf16[1,64,2048]{2,1,0:T(8,128)(2,1)S(1)} %get-tuple-element.27), channel_id=1, source_target_pairs={{0,1},{1,0},{2,3},{3,2},{4,5},{5,4},{6,7},{7,6},{8,9},{9,8},{10,11... | collective-permute-start | bytes 786440 | tf_op jit(solution)/shard_map/ppermute | solution.py:244
  14.3 0.0 collective-permute-start.5
  14.3 2.0 %collective-permute-start.6 = (bf16[1,64,2048]{2,1,0:T(8,128)(2,1)S(1)}, bf16[1,64,2048]{2,1,0:T(8,128)(2,1)S(1)}, u32[]{:S(2)}, u32[]{:S(2)}) collective-permute-start(bf16[1,64,2048]{2,1,0:T(8,128)(2,1)S(1)} %get-tuple-element.29), channel_id=1, source_target_pairs={{0,3},{1,2},{2,1},{3,0},{4,7},{5,6},{6,5},{7,4},{8,11},{9,10},{10,... | collective-permute-start | bytes 786440 | tf_op jit(solution)/shard_map/ppermute | solution.py:244
  16.3 1.1 %shard_map.50 = (bf16[1,64,2048]{2,1,0:T(8,128)(2,1)S(1)}, bf16[1,64,2048]{2,1,0:T(8,128)(2,1)S(1)}, bf16[1,64,2048]{2,1,0:T(8,128)(2,1)S(1)}) custom-call(bf16[256,384]{1,0:T(8,128)(2,1)S(1)} %get-tuple-element.25.turned_ref, bf16[6,64,4096]{2,1,0:T(8,128)(2,1)S(1)} %get-tuple-element.22.tiles_ref, bf16[1,64,2048]{2,1,0:T(8,128)(2,1)S(1)} %get-tuple-element.26.refs_1_.skipped), custom_call_target="tpu_custom_call" | custom-call | flops 301989888 | bytes 3932160 | tf_op jit(solution)/shard_map/pallas_call | solution.py:149
  17.4 0.4 collective-permute-start.7
  17.8 1.2 %collective-permute-done.3.refs_0_ = bf16[1,64,2048]{2,1,0:T(8,128)(2,1)S(1)} collective-permute-done((bf16[1,64,2048]{2,1,0:T(8,128)(2,1)S(1)}, bf16[1,64,2048]{2,1,0:T(8,128)(2,1)S(1)}, u32[]{:S(2)}, u32[]{:S(2)}) %collective-permute-start.3) | collective-permute-done | bytes 262176 | tf_op jit(solution)/shard_map/ppermute | solution.py:244
  19.0 6.4 %collective-permute-start.8 = (bf16[1,64,2048]{2,1,0:T(8,128)(2,1)S(1)}, bf16[1,64,2048]{2,1,0:T(8,128)(2,1)S(1)}, u32[]{:S(2)}, u32[]{:S(2)}) collective-permute-start(bf16[1,64,2048]{2,1,0:T(8,128)(2,1)S(1)} %get-tuple-element.32), channel_id=1, source_target_pairs={{0,4},{1,5},{2,6},{3,7},{4,0},{5,1},{6,2},{7,3},{8,12},{9,13},{10,... | collective-permute-start | bytes 786440 | tf_op jit(solution)/shard_map/ppermute | solution.py:244
  25.4 0.0 collective-permute-done.4.refs_2_
  25.4 2.3 %collective-permute-start.9 = (bf16[1,64,2048]{2,1,0:T(8,128)(2,1)S(1)}, bf16[1,64,2048]{2,1,0:T(8,128)(2,1)S(1)}, u32[]{:S(2)}, u32[]{:S(2)}) collective-permute-start(bf16[1,64,2048]{2,1,0:T(8,128)(2,1)S(1)} %get-tuple-element.33), channel_id=1, source_target_pairs={{0,7},{1,6},{2,5},{3,4},{4,3},{5,2},{6,1},{7,0},{8,15},{9,14},{10,... | collective-permute-start | bytes 786440 | tf_op jit(solution)/shard_map/ppermute | solution.py:244
  27.7 3.3 %collective-permute-done.5.refs_3_ = bf16[1,64,2048]{2,1,0:T(8,128)(2,1)S(1)} collective-permute-done((bf16[1,64,2048]{2,1,0:T(8,128)(2,1)S(1)}, bf16[1,64,2048]{2,1,0:T(8,128)(2,1)S(1)}, u32[]{:S(2)}, u32[]{:S(2)}) %collective-permute-start.5) | collective-permute-done | bytes 262176 | tf_op jit(solution)/shard_map/ppermute | solution.py:244
  31.0 7.5 %collective-permute-done.6.refs_4_ = bf16[1,64,2048]{2,1,0:T(8,128)(2,1)S(1)} collective-permute-done((bf16[1,64,2048]{2,1,0:T(8,128)(2,1)S(1)}, bf16[1,64,2048]{2,1,0:T(8,128)(2,1)S(1)}, u32[]{:S(2)}, u32[]{:S(2)}) %collective-permute-start.6) | collective-permute-done | bytes 262176 | tf_op jit(solution)/shard_map/ppermute | solution.py:244
  38.5 0.7 shard_map.49
  39.2 0.0 collective-permute-done.7.refs_5_
  39.3 12.7 %collective-permute-done.8.refs_6_ = bf16[1,64,2048]{2,1,0:T(8,128)(2,1)S(1)} collective-permute-done((bf16[1,64,2048]{2,1,0:T(8,128)(2,1)S(1)}, bf16[1,64,2048]{2,1,0:T(8,128)(2,1)S(1)}, u32[]{:S(2)}, u32[]{:S(2)}) %collective-permute-start.8) | collective-permute-done | bytes 262176 | tf_op jit(solution)/shard_map/ppermute | solution.py:244
  52.0 0.0 collective-permute-done.9.refs_7_
  52.0 1.0 %shard_map.51 = (f32[8,32,256]{2,1,0:T(8,128)S(1)}, f32[8,32,256]{2,1,0:T(8,128)S(1)}) custom-call(f32[256,2048]{1,0:T(8,128)S(1)} %get-tuple-element.30.fitted_ref, bf16[1,64,2048]{2,1,0:T(8,128)(2,1)S(1)} %collective-permute-done.3.refs_0_, bf16[1,64,2048]{2,1,0:T(8,128)(2,1)S(1)} %get-tuple-element.26.refs_1_.skipped, ...), custom_call_target="tpu_custom_call" | custom-call | flops 1073741824 | bytes 2097152 | tf_op jit(solution)/shard_map/pallas_call | solution.py:228
  53.0 0.1 collective-permute-start.10
  53.1 1.5 %collective-permute-done.10 = f32[8,32,256]{2,1,0:T(8,128)S(1)} collective-permute-done((f32[8,32,256]{2,1,0:T(8,128)S(1)}, f32[8,32,256]{2,1,0:T(8,128)S(1)}, u32[]{:S(2)}, u32[]{:S(2)}) %collective-permute-start.10) | collective-permute-done | bytes 262176 | tf_op jit(solution)/shard_map/ppermute | solution.py:244
  54.6 0.1 abs_reduce_fusion
  54.8 16.5 %all_to_all.5 = f16[8,40,256]{2,1,0:T(8,128)(2,1)S(1)} all-to-all(f16[8,40,256]{2,1,0:T(8,128)(2,1)S(1)} %pad_maximum_fusion), channel_id=1, replica_groups=mesh['rep'=4,'grid'=8] {'grid'}, dimensions={0} | all-to-all | bytes 327680 | tf_op jit(solution)/shard_map/all_to_all | solution.py:253
  71.4 1.3 %collective-permute-start.13 = (f32[32,256]{1,0:T(8,128)S(1)}, f32[32,256]{1,0:T(8,128)S(1)}, u32[]{:S(2)}, u32[]{:S(2)}) collective-permute-start(f32[32,256]{1,0:T(8,128)S(1)} %fusion), channel_id=1, source_target_pairs={{0,16},{8,24},{16,0},{24,8},{1,17},{9,25},{17,1},{25,9},{2,18},{10... | collective-permute-start | bytes 98312 | tf_op jit(solution)/shard_map/ppermute | solution.py:244
  72.7 0.0 collective-permute-start.12
  72.7 0.9 %collective-permute-start.11 = (f32[32,256]{1,0:T(8,128)S(1)}, f32[32,256]{1,0:T(8,128)S(1)}, u32[]{:S(2)}, u32[]{:S(2)}) collective-permute-start(f32[32,256]{1,0:T(8,128)S(1)} %fusion), channel_id=1, source_target_pairs={{0,8},{8,0},{16,24},{24,16},{1,9},{9,1},{17,25},{25,17},{2,10},{10... | collective-permute-start | bytes 98312 | tf_op jit(solution)/shard_map/ppermute | solution.py:244
  73.6 1.8 %collective-permute-done.13 = f32[32,256]{1,0:T(8,128)S(1)} collective-permute-done((f32[32,256]{1,0:T(8,128)S(1)}, f32[32,256]{1,0:T(8,128)S(1)}, u32[]{:S(2)}, u32[]{:S(2)}) %collective-permute-start.13) | collective-permute-done | bytes 32800 | tf_op jit(solution)/shard_map/ppermute | solution.py:244
  75.4 0.7 collective-permute-done.12
  76.1 0.0 collective-permute-done.11
  76.1 0.6 pad_maximum_fusion.1
  (9 shorter events, 0.2 us)
Async XLA Ops:
  0.0 6.9 %copy-start = (bf16[128,256]{1,0:T(8,128)(2,1)S(1)}, bf16[128,256]{1,0:T(8,128)(2,1)}, u32[]{:S(2)}) copy-start(bf16[128,256]{1,0:T(8,128)(2,1)} %refs_0_.1) | copy-start | bytes 196612
  0.0 5.7 %collective-permute-start.1 = (bf16[128,256]{1,0:T(8,128)(2,1)}, bf16[128,256]{1,0:T(8,128)(2,1)S(1)}, u32[]{:S(2)}, u32[]{:S(2)}) collective-permute-start(bf16[128,256]{1,0:T(8,128)(2,1)} %refs_0_.1), channel_id=1, source_target_pairs={{0,16},{8,24},{16,0},{24,8},{1,17},{9,25},{17,1},{25,9},{2,18},{10... | collective-permute-start | bytes 196616 | tf_op jit(solution)/shard_map/ppermute | solution.py:244
  3.0 2.8 %collective-permute-start = (bf16[128,256]{1,0:T(8,128)(2,1)}, bf16[128,256]{1,0:T(8,128)(2,1)S(1)}, u32[]{:S(2)}, u32[]{:S(2)}) collective-permute-start(bf16[128,256]{1,0:T(8,128)(2,1)} %refs_0_.1), channel_id=1, source_target_pairs={{0,8},{8,0},{16,24},{24,16},{1,9},{9,1},{17,25},{25,17},{2,10},{10... | collective-permute-start | bytes 196616 | tf_op jit(solution)/shard_map/ppermute | solution.py:244
  3.0 4.0 %collective-permute-start.2 = (bf16[128,256]{1,0:T(8,128)(2,1)}, bf16[128,256]{1,0:T(8,128)(2,1)S(1)}, u32[]{:S(2)}, u32[]{:S(2)}) collective-permute-start(bf16[128,256]{1,0:T(8,128)(2,1)} %refs_0_.1), channel_id=1, source_target_pairs={{0,24},{8,16},{16,8},{24,0},{1,25},{9,17},{17,9},{25,1},{2,26},{10... | collective-permute-start | bytes 196616 | tf_op jit(solution)/shard_map/ppermute | solution.py:244
  8.0 11.0 %collective-permute-start.3 = (bf16[1,64,2048]{2,1,0:T(8,128)(2,1)S(1)}, bf16[1,64,2048]{2,1,0:T(8,128)(2,1)S(1)}, u32[]{:S(2)}, u32[]{:S(2)}) collective-permute-start(bf16[1,64,2048]{2,1,0:T(8,128)(2,1)S(1)} %get-tuple-element.24.skipped), channel_id=1, source_target_pairs={{0,6},{1,7},{2,4},{3,5},{4,2},{5,3},{6,0},{7,1},{8,14},{9,15},{10,... | collective-permute-start | bytes 786440 | tf_op jit(solution)/shard_map/ppermute | solution.py:244
  12.8 12.7 %collective-permute-start.4 = (bf16[1,64,2048]{2,1,0:T(8,128)(2,1)S(1)}, bf16[1,64,2048]{2,1,0:T(8,128)(2,1)S(1)}, u32[]{:S(2)}, u32[]{:S(2)}) collective-permute-start(bf16[1,64,2048]{2,1,0:T(8,128)(2,1)S(1)} %get-tuple-element.27), channel_id=1, source_target_pairs={{0,1},{1,0},{2,3},{3,2},{4,5},{5,4},{6,7},{7,6},{8,9},{9,8},{10,11... | collective-permute-start | bytes 786440 | tf_op jit(solution)/shard_map/ppermute | solution.py:244
  14.3 16.7 %collective-permute-start.5 = (bf16[1,64,2048]{2,1,0:T(8,128)(2,1)S(1)}, bf16[1,64,2048]{2,1,0:T(8,128)(2,1)S(1)}, u32[]{:S(2)}, u32[]{:S(2)}) collective-permute-start(bf16[1,64,2048]{2,1,0:T(8,128)(2,1)S(1)} %get-tuple-element.28), channel_id=1, source_target_pairs={{0,2},{1,3},{2,0},{3,1},{4,6},{5,7},{6,4},{7,5},{8,10},{9,11},{10,... | collective-permute-start | bytes 786440 | tf_op jit(solution)/shard_map/ppermute | solution.py:244
  14.3 24.2 %collective-permute-start.6 = (bf16[1,64,2048]{2,1,0:T(8,128)(2,1)S(1)}, bf16[1,64,2048]{2,1,0:T(8,128)(2,1)S(1)}, u32[]{:S(2)}, u32[]{:S(2)}) collective-permute-start(bf16[1,64,2048]{2,1,0:T(8,128)(2,1)S(1)} %get-tuple-element.29), channel_id=1, source_target_pairs={{0,3},{1,2},{2,1},{3,0},{4,7},{5,6},{6,5},{7,4},{8,11},{9,10},{10,... | collective-permute-start | bytes 786440 | tf_op jit(solution)/shard_map/ppermute | solution.py:244
  17.4 21.9 %collective-permute-start.7 = (bf16[1,64,2048]{2,1,0:T(8,128)(2,1)S(1)}, bf16[1,64,2048]{2,1,0:T(8,128)(2,1)S(1)}, u32[]{:S(2)}, u32[]{:S(2)}) collective-permute-start(bf16[1,64,2048]{2,1,0:T(8,128)(2,1)S(1)} %get-tuple-element.31), channel_id=1, source_target_pairs={{0,5},{1,4},{2,7},{3,6},{4,1},{5,0},{6,3},{7,2},{8,13},{9,12},{10,... | collective-permute-start | bytes 786440 | tf_op jit(solution)/shard_map/ppermute | solution.py:244
  19.0 32.9 %collective-permute-start.8 = (bf16[1,64,2048]{2,1,0:T(8,128)(2,1)S(1)}, bf16[1,64,2048]{2,1,0:T(8,128)(2,1)S(1)}, u32[]{:S(2)}, u32[]{:S(2)}) collective-permute-start(bf16[1,64,2048]{2,1,0:T(8,128)(2,1)S(1)} %get-tuple-element.32), channel_id=1, source_target_pairs={{0,4},{1,5},{2,6},{3,7},{4,0},{5,1},{6,2},{7,3},{8,12},{9,13},{10,... | collective-permute-start | bytes 786440 | tf_op jit(solution)/shard_map/ppermute | solution.py:244
  25.4 26.6 %collective-permute-start.9 = (bf16[1,64,2048]{2,1,0:T(8,128)(2,1)S(1)}, bf16[1,64,2048]{2,1,0:T(8,128)(2,1)S(1)}, u32[]{:S(2)}, u32[]{:S(2)}) collective-permute-start(bf16[1,64,2048]{2,1,0:T(8,128)(2,1)S(1)} %get-tuple-element.33), channel_id=1, source_target_pairs={{0,7},{1,6},{2,5},{3,4},{4,3},{5,2},{6,1},{7,0},{8,15},{9,14},{10,... | collective-permute-start | bytes 786440 | tf_op jit(solution)/shard_map/ppermute | solution.py:244
  53.0 1.6 %collective-permute-start.10 = (f32[8,32,256]{2,1,0:T(8,128)S(1)}, f32[8,32,256]{2,1,0:T(8,128)S(1)}, u32[]{:S(2)}, u32[]{:S(2)}) collective-permute-start(f32[8,32,256]{2,1,0:T(8,128)S(1)} %get-tuple-element.36), channel_id=1, source_target_pairs={{0,8},{8,0},{16,24},{24,16},{1,9},{9,1},{17,25},{25,17},{2,10},{10... | collective-permute-start | bytes 786440 | tf_op jit(solution)/shard_map/ppermute | solution.py:244
  71.4 4.0 %collective-permute-start.13 = (f32[32,256]{1,0:T(8,128)S(1)}, f32[32,256]{1,0:T(8,128)S(1)}, u32[]{:S(2)}, u32[]{:S(2)}) collective-permute-start(f32[32,256]{1,0:T(8,128)S(1)} %fusion), channel_id=1, source_target_pairs={{0,16},{8,24},{16,0},{24,8},{1,17},{9,25},{17,1},{25,9},{2,18},{10... | collective-permute-start | bytes 98312 | tf_op jit(solution)/shard_map/ppermute | solution.py:244
  72.7 3.4 %collective-permute-start.12 = (f32[32,256]{1,0:T(8,128)S(1)}, f32[32,256]{1,0:T(8,128)S(1)}, u32[]{:S(2)}, u32[]{:S(2)}) collective-permute-start(f32[32,256]{1,0:T(8,128)S(1)} %fusion), channel_id=1, source_target_pairs={{0,24},{8,16},{16,8},{24,0},{1,25},{9,17},{17,9},{25,1},{2,26},{10... | collective-permute-start | bytes 98312 | tf_op jit(solution)/shard_map/ppermute | solution.py:244
  72.7 3.4 %collective-permute-start.11 = (f32[32,256]{1,0:T(8,128)S(1)}, f32[32,256]{1,0:T(8,128)S(1)}, u32[]{:S(2)}, u32[]{:S(2)}) collective-permute-start(f32[32,256]{1,0:T(8,128)S(1)} %fusion), channel_id=1, source_target_pairs={{0,8},{8,0},{16,24},{24,16},{1,9},{9,1},{17,25},{25,17},{2,10},{10... | collective-permute-start | bytes 98312 | tf_op jit(solution)/shard_map/ppermute | solution.py:244

commit v6 on v5

--- a/solution.py
+++ b/solution.py
@@ -196,10 +196,20 @@
     )(orbitals, *early)
 
 
-def action_kernel(fit_scale, mix_scale, step, width, ids, n_early, n_late, fitted_ref, *refs):
-    early, late, (keep_ref, send_ref, fitted) = refs[:n_early], refs[n_early:n_early + n_late], refs[-3:]
-    norb, cols = fitted_ref.shape
-    upper = lax.axis_index("rep") % 2 == 1
+def action_half(rows, fitted, mix_scale, half, width, ids, out_ref):
+    offset = pl.multiple_of(half * (width // 2), width // 2)
+    lhs = jnp.concatenate(
+        [ref[b, pl.ds(offset, width // 2), :] for ref in rows for b in range(ref.shape[0])], axis=0
+    )
+    term = lax.dot_general(lhs, fitted, (((1,), (1,)), ((), ())), preferred_element_type=jnp.float32)
+    term = (-mix_scale * term).reshape((-1,) + out_ref.shape[1:])
+    for k, b in enumerate(ids):
+        out_ref[b] = term[k]
+
+
+def send_kernel(fit_scale, mix_scale, step, width, ids, n_early, n_late, fitted_ref, *refs):
+    rows, late, (send_ref, out_ref) = refs[:n_early + n_late], refs[n_early:n_early + n_late], refs[-2:]
+    cols = fitted_ref.shape[1]
     if late:
         turned = refs[n_early + n_late][...]
     for at in range(cols // step):
@@ -207,37 +217,45 @@
         total = fitted_ref[:, lanes]
         if late:
             total = total + jnp.dot(turned, joined(late, lanes), preferred_element_type=jnp.float32)
-        fitted[:, lanes] = (fit_scale * total).astype(jnp.bfloat16)
-    term = lax.dot_general(
-        joined(early + late), fitted[...], (((1,), (1,)), ((), ())), preferred_element_type=jnp.float32
-    )
-    blocks = ids()
-    term = (-mix_scale * term).reshape(len(blocks), 2, width // 2, norb)
-    keep = jnp.where(upper, term[:, 1], term[:, 0])
-    send = jnp.where(upper, term[:, 0], term[:, 1])
-    for k, b in enumerate(blocks):
-        keep_ref[b] = keep[k]
-        send_ref[b] = send[k]
+        out_ref[:, lanes] = (fit_scale * total).astype(jnp.bfloat16)
+    core = lax.axis_index("rep") % 2
+    action_half(rows, out_ref[...], mix_scale, 1 - core, width, ids(), send_ref)
+
+
+def keep_kernel(mix_scale, width, ids, fitted_ref, *refs):
+    core = lax.axis_index("rep") % 2
+    action_half(refs[:-1], fitted_ref[...], mix_scale, core, width, ids(), refs[-1])
 
 
 def action(fitted, early, late, ids, basis_rows, fit_scale, mix_scale):
     norb, cols = fitted[0].shape
     width = early[0].shape[1]
     blocks = basis_rows // width
-    shape = jax.ShapeDtypeStruct((blocks, width // 2, norb), jnp.float32)
-    return pl.pallas_call(
+    half = jax.ShapeDtypeStruct((blocks, width // 2, norb), jnp.float32)
+    rows = list(early) + list(late)
+    params = pltpu.CompilerParams(vmem_limit_bytes=VMEM_LIMIT)
+    cost = pl.CostEstimate(
+        flops=2 * blocks * width * cols * norb, bytes_accessed=2 * blocks * width * cols, transcendentals=0
+    )
+    send, columns = pl.pallas_call(
         functools.partial(
-            action_kernel, fit_scale, mix_scale, min(512, cols), width, ids, len(early), len(late)
+            send_kernel, fit_scale, mix_scale, min(512, cols), width, ids, len(early), len(late)
         ),
-        out_shape=[shape, shape],
-        in_specs=[pl.BlockSpec(memory_space=pltpu.VMEM)] * (len(fitted) + len(early) + len(late)),
+        out_shape=[half, jax.ShapeDtypeStruct((norb, cols), jnp.bfloat16)],
+        in_specs=[pl.BlockSpec(memory_space=pltpu.VMEM)] * (len(fitted) + len(rows)),
         out_specs=[pl.BlockSpec(memory_space=pltpu.VMEM)] * 2,
-        scratch_shapes=[pltpu.VMEM((norb, cols), jnp.bfloat16)],
-        compiler_params=pltpu.CompilerParams(vmem_limit_bytes=VMEM_LIMIT),
-        cost_estimate=pl.CostEstimate(
-            flops=4 * blocks * width * cols * norb, bytes_accessed=2 * blocks * width * cols, transcendentals=0
-        ),
-    )(fitted[0], *early, *late, *fitted[1:])
+        compiler_params=params,
+        cost_estimate=cost,
+    )(fitted[0], *rows, *fitted[1:])
+    keep = pl.pallas_call(
+        functools.partial(keep_kernel, mix_scale, width, ids),
+        out_shape=half,
+        in_specs=[pl.BlockSpec(memory_space=pltpu.VMEM)] * (1 + len(rows)),
+        out_specs=pl.BlockSpec(memory_space=pltpu.VMEM),
+        compiler_params=params,
+        cost_estimate=cost,
+    )(columns, *rows)
+    return keep, send
 
 
 def swapped(x, axis, k):
@@ -247,7 +265,7 @@
 def summed_blocks(blocks, axis):
     rows = blocks.shape[1]
     largest = jnp.max(jnp.abs(blocks), axis=1, keepdims=True)
-    exponent = jnp.ceil(jnp.log2(jnp.maximum(largest, 1e-30)))
+    exponent = jnp.ceil(jnp.log2(jnp.maximum(largest, 1e-30))) - 14
     scaled = (blocks * jnp.exp2(-exponent)).astype(jnp.float16)
     tail = jnp.broadcast_to(exponent.astype(jnp.float16), (blocks.shape[0], 8, blocks.shape[2]))
     got = lax.all_to_all(jnp.concatenate([scaled, tail], axis=1), axis, 0, 0, tiled=True).astype(jnp.float32)

time: 76.9 us -> 76.8 us (level)
  transfers between devices with their start and end apart: 14 -> 14, of which waited for: 8 -> 8; matrix products, arithmetic and copies ran while one was open for 0% -> 0% of each run, Pallas kernels for 6% -> 7%
where the time goes in v6:
time: 76.8 us; the launch traced here: 76.6 us
  waiting for transfers between devices  29.4 us (38%)
  starting transfers between devices  21.8 us (28%)
  blocking collectives  16.5 us (21%)
  Pallas kernels  7.21 us (9%)
  other arithmetic  0.84 us (1%)
  between operations  0.81 us (1%)
    ppermute x14, waiting for transfers between devices, swapped(): lax.ppermute(x, axis, [(i, i ^ k) for i in range(lax.axis_size(axis))])  29.4 us
    ppermute x14, starting transfers between devices, swapped(): lax.ppermute(x, axis, [(i, i ^ k) for i in range(lax.axis_size(axis))])  21.8 us
    all_to_all x1, blocking collectives, summed_blocks(): lax.all_to_all(jnp.concatenate([scaled, tail], axis=1), axis, 0, 0, tiled...  16.5 us
    pallas_call x2, Pallas kernels, contract_next(): pl.pallas_call(functools.partial(next_kernel, group_starts, place), out_s...  2.1 us
    pallas_call x1, Pallas kernels, load(): pl.pallas_call(load_kernel, out_shape=[jax.ShapeDtypeStruct(tiles.shape[2...  1.91 us
  transfers between devices with their start and end apart: 14, of which 8 were waited for; matrix products, arithmetic and copies ran while one was open for 0% of the time, Pallas kernels for 7%

profile of v6, /device:TPU:0, one launch (start us, length us, event | category | flops | bytes accessed | tf_op | source)
XLA Modules:
  0.0 76.6 jit_solution(1272056227811148449)
XLA Ops:
  0.0 0.0 copy-start
  0.0 3.0 %collective-permute-start.1 = (bf16[128,256]{1,0:T(8,128)(2,1)}, bf16[128,256]{1,0:T(8,128)(2,1)S(1)}, u32[]{:S(2)}, u32[]{:S(2)}) collective-permute-start(bf16[128,256]{1,0:T(8,128)(2,1)} %refs_0_.1), channel_id=1, source_target_pairs={{0,16},{8,24},{16,0},{24,8},{1,17},{9,25},{17,1},{25,9},{2,18},{10... | collective-permute-start | bytes 196616 | tf_op jit(solution)/shard_map/ppermute | solution.py:262
  3.0 0.0 collective-permute-start
  3.0 0.2 collective-permute-start.2
  3.8 1.9 %shard_map.46 = (bf16[6,64,4096]{2,1,0:T(8,128)(2,1)S(1)}, s32[1,6]{1,0:T(1,128)S(1)}) custom-call(s32[1,1]{1,0:T(1,128)S(6)} %copy.8.count_ref, s32[1,1,6]{2,1,0:T(1,128)} %block_hbm.1, bf16[1,1,6,64,4096]{4,3,2,1,0:T(8,128)(2,1)} %tiles_hbm.1), custom_call_target="tpu_custom_call" | custom-call | bytes 3145728 | tf_op jit(solution)/shard_map/pallas_call | solution.py:41
  5.7 0.0 collective-permute-done.1.refs_2_
  5.7 0.0 collective-permute-done.refs_1_
  5.8 1.2 %collective-permute-done.2.refs_3_ = bf16[128,256]{1,0:T(8,128)(2,1)S(1)} collective-permute-done((bf16[128,256]{1,0:T(8,128)(2,1)}, bf16[128,256]{1,0:T(8,128)(2,1)S(1)}, u32[]{:S(2)}, u32[]{:S(2)}) %collective-permute-start.2) | collective-permute-done | bytes 65568 | tf_op jit(solution)/shard_map/ppermute | solution.py:262
  6.9 0.0 copy-done
  6.9 1.1 %shard_map.47 = (bf16[512,256]{1,0:T(8,128)(2,1)S(1)}, bf16[256,384]{1,0:T(8,128)(2,1)S(1)}, bf16[1,64,2048]{2,1,0:T(8,128)(2,1)S(1)}) custom-call(s32[1,6]{1,0:T(1,128)S(1)} %get-tuple-element.21.block_ref, bf16[6,64,4096]{2,1,0:T(8,128)(2,1)S(1)} %get-tuple-element.22.tiles_ref, bf16[128,256]{1,0:T(8,128)(2,1)S(1)} %copy-done, ...), custom_call_target="tpu_custom_call" | custom-call | flops 100663296 | bytes 3407872 | tf_op jit(solution)/shard_map/pallas_call | solution.py:136
  8.0 3.7 %collective-permute-start.3 = (bf16[1,64,2048]{2,1,0:T(8,128)(2,1)S(1)}, bf16[1,64,2048]{2,1,0:T(8,128)(2,1)S(1)}, u32[]{:S(2)}, u32[]{:S(2)}) collective-permute-start(bf16[1,64,2048]{2,1,0:T(8,128)(2,1)S(1)} %get-tuple-element.24.skipped), channel_id=1, source_target_pairs={{0,6},{1,7},{2,4},{3,5},{4,2},{5,3},{6,0},{7,1},{8,14},{9,15},{10,... | collective-permute-start | bytes 786440 | tf_op jit(solution)/shard_map/ppermute | solution.py:262
  11.7 1.1 %shard_map.48 = (bf16[1,64,2048]{2,1,0:T(8,128)(2,1)S(1)}, bf16[1,64,2048]{2,1,0:T(8,128)(2,1)S(1)}, bf16[1,64,2048]{2,1,0:T(8,128)(2,1)S(1)}, bf16[1,64,2048]{2,1,0:T(8,128)(2,1)S(1)}) custom-call(bf16[256,384]{1,0:T(8,128)(2,1)S(1)} %get-tuple-element.25.turned_ref, bf16[6,64,4096]{2,1,0:T(8,128)(2,1)S(1)} %get-tuple-element.22.tiles_ref, ...), custom_call_target="tpu_custom_call" | custom-call | flops 402653184 | bytes 4194304 | tf_op jit(solution)/shard_map/pallas_call | solution.py:149
  12.8 1.6 %collective-permute-start.4 = (bf16[1,64,2048]{2,1,0:T(8,128)(2,1)S(1)}, bf16[1,64,2048]{2,1,0:T(8,128)(2,1)S(1)}, u32[]{:S(2)}, u32[]{:S(2)}) collective-permute-start(bf16[1,64,2048]{2,1,0:T(8,128)(2,1)S(1)} %get-tuple-element.27), channel_id=1, source_target_pairs={{0,1},{1,0},{2,3},{3,2},{4,5},{5,4},{6,7},{7,6},{8,9},{9,8},{10,11... | collective-permute-start | bytes 786440 | tf_op jit(solution)/shard_map/ppermute | solution.py:262
  14.3 0.0 collective-permute-start.5
  14.3 2.0 %collective-permute-start.6 = (bf16[1,64,2048]{2,1,0:T(8,128)(2,1)S(1)}, bf16[1,64,2048]{2,1,0:T(8,128)(2,1)S(1)}, u32[]{:S(2)}, u32[]{:S(2)}) collective-permute-start(bf16[1,64,2048]{2,1,0:T(8,128)(2,1)S(1)} %get-tuple-element.29), channel_id=1, source_target_pairs={{0,3},{1,2},{2,1},{3,0},{4,7},{5,6},{6,5},{7,4},{8,11},{9,10},{10,... | collective-permute-start | bytes 786440 | tf_op jit(solution)/shard_map/ppermute | solution.py:262
  16.3 1.1 %shard_map.50 = (bf16[1,64,2048]{2,1,0:T(8,128)(2,1)S(1)}, bf16[1,64,2048]{2,1,0:T(8,128)(2,1)S(1)}, bf16[1,64,2048]{2,1,0:T(8,128)(2,1)S(1)}) custom-call(bf16[256,384]{1,0:T(8,128)(2,1)S(1)} %get-tuple-element.25.turned_ref, bf16[6,64,4096]{2,1,0:T(8,128)(2,1)S(1)} %get-tuple-element.22.tiles_ref, bf16[1,64,2048]{2,1,0:T(8,128)(2,1)S(1)} %get-tuple-element.26.refs_1_.skipped), custom_call_target="tpu_custom_call" | custom-call | flops 301989888 | bytes 3932160 | tf_op jit(solution)/shard_map/pallas_call | solution.py:149
  17.4 0.4 collective-permute-start.7
  17.8 1.2 %collective-permute-done.3.refs_0_ = bf16[1,64,2048]{2,1,0:T(8,128)(2,1)S(1)} collective-permute-done((bf16[1,64,2048]{2,1,0:T(8,128)(2,1)S(1)}, bf16[1,64,2048]{2,1,0:T(8,128)(2,1)S(1)}, u32[]{:S(2)}, u32[]{:S(2)}) %collective-permute-start.3) | collective-permute-done | bytes 262176 | tf_op jit(solution)/shard_map/ppermute | solution.py:262
  19.0 6.4 %collective-permute-start.8 = (bf16[1,64,2048]{2,1,0:T(8,128)(2,1)S(1)}, bf16[1,64,2048]{2,1,0:T(8,128)(2,1)S(1)}, u32[]{:S(2)}, u32[]{:S(2)}) collective-permute-start(bf16[1,64,2048]{2,1,0:T(8,128)(2,1)S(1)} %get-tuple-element.32), channel_id=1, source_target_pairs={{0,4},{1,5},{2,6},{3,7},{4,0},{5,1},{6,2},{7,3},{8,12},{9,13},{10,... | collective-permute-start | bytes 786440 | tf_op jit(solution)/shard_map/ppermute | solution.py:262
  25.4 0.0 collective-permute-done.4.refs_2_
  25.4 2.3 %collective-permute-start.9 = (bf16[1,64,2048]{2,1,0:T(8,128)(2,1)S(1)}, bf16[1,64,2048]{2,1,0:T(8,128)(2,1)S(1)}, u32[]{:S(2)}, u32[]{:S(2)}) collective-permute-start(bf16[1,64,2048]{2,1,0:T(8,128)(2,1)S(1)} %get-tuple-element.33), channel_id=1, source_target_pairs={{0,7},{1,6},{2,5},{3,4},{4,3},{5,2},{6,1},{7,0},{8,15},{9,14},{10,... | collective-permute-start | bytes 786440 | tf_op jit(solution)/shard_map/ppermute | solution.py:262
  27.7 3.3 %collective-permute-done.5.refs_3_ = bf16[1,64,2048]{2,1,0:T(8,128)(2,1)S(1)} collective-permute-done((bf16[1,64,2048]{2,1,0:T(8,128)(2,1)S(1)}, bf16[1,64,2048]{2,1,0:T(8,128)(2,1)S(1)}, u32[]{:S(2)}, u32[]{:S(2)}) %collective-permute-start.5) | collective-permute-done | bytes 262176 | tf_op jit(solution)/shard_map/ppermute | solution.py:262
  31.0 7.5 %collective-permute-done.6.refs_4_ = bf16[1,64,2048]{2,1,0:T(8,128)(2,1)S(1)} collective-permute-done((bf16[1,64,2048]{2,1,0:T(8,128)(2,1)S(1)}, bf16[1,64,2048]{2,1,0:T(8,128)(2,1)S(1)}, u32[]{:S(2)}, u32[]{:S(2)}) %collective-permute-start.6) | collective-permute-done | bytes 262176 | tf_op jit(solution)/shard_map/ppermute | solution.py:262
  38.5 0.7 shard_map.49
  39.2 0.0 collective-permute-done.7.refs_5_
  39.3 12.7 %collective-permute-done.8.refs_6_ = bf16[1,64,2048]{2,1,0:T(8,128)(2,1)S(1)} collective-permute-done((bf16[1,64,2048]{2,1,0:T(8,128)(2,1)S(1)}, bf16[1,64,2048]{2,1,0:T(8,128)(2,1)S(1)}, u32[]{:S(2)}, u32[]{:S(2)}) %collective-permute-start.8) | collective-permute-done | bytes 262176 | tf_op jit(solution)/shard_map/ppermute | solution.py:262
  52.0 0.0 collective-permute-done.9.refs_7_
  52.0 0.9 %shard_map.51 = (f32[8,32,256]{2,1,0:T(8,128)S(1)}, bf16[256,2048]{1,0:T(8,128)(2,1)S(1)}) custom-call(f32[256,2048]{1,0:T(8,128)S(1)} %get-tuple-element.30.fitted_ref, bf16[1,64,2048]{2,1,0:T(8,128)(2,1)S(1)} %collective-permute-done.3.refs_0_, bf16[1,64,2048]{2,1,0:T(8,128)(2,1)S(1)} %get-tuple-element.26.refs_1_.skipped, ...), custom_call_target="tpu_custom_call" | custom-call | flops 536870912 | bytes 2097152 | tf_op jit(solution)/shard_map/pallas_call | solution.py:240
  52.9 0.1 collective-permute-start.10
  53.0 0.5 shard_map.52
  53.4 1.0 %collective-permute-done.10 = f32[8,32,256]{2,1,0:T(8,128)S(1)} collective-permute-done((f32[8,32,256]{2,1,0:T(8,128)S(1)}, f32[8,32,256]{2,1,0:T(8,128)S(1)}, u32[]{:S(2)}, u32[]{:S(2)}) %collective-permute-start.10) | collective-permute-done | bytes 262176 | tf_op jit(solution)/shard_map/ppermute | solution.py:262
  54.7 16.5 %all_to_all.5 = f16[8,40,256]{2,1,0:T(8,128)(2,1)S(1)} all-to-all(f16[8,40,256]{2,1,0:T(8,128)(2,1)S(1)} %pad_maximum_fusion), channel_id=1, replica_groups=mesh['rep'=4,'grid'=8] {'grid'}, dimensions={0} | all-to-all | bytes 327680 | tf_op jit(solution)/shard_map/all_to_all | solution.py:271
  71.3 1.3 %collective-permute-start.13 = (f32[32,256]{1,0:T(8,128)S(1)}, f32[32,256]{1,0:T(8,128)S(1)}, u32[]{:S(2)}, u32[]{:S(2)}) collective-permute-start(f32[32,256]{1,0:T(8,128)S(1)} %fusion), channel_id=1, source_target_pairs={{0,16},{8,24},{16,0},{24,8},{1,17},{9,25},{17,1},{25,9},{2,18},{10... | collective-permute-start | bytes 98312 | tf_op jit(solution)/shard_map/ppermute | solution.py:262
  72.6 0.0 collective-permute-start.12
  72.6 0.9 %collective-permute-start.11 = (f32[32,256]{1,0:T(8,128)S(1)}, f32[32,256]{1,0:T(8,128)S(1)}, u32[]{:S(2)}, u32[]{:S(2)}) collective-permute-start(f32[32,256]{1,0:T(8,128)S(1)} %fusion), channel_id=1, source_target_pairs={{0,8},{8,0},{16,24},{24,16},{1,9},{9,1},{17,25},{25,17},{2,10},{10... | collective-permute-start | bytes 98312 | tf_op jit(solution)/shard_map/ppermute | solution.py:262
  73.5 1.8 %collective-permute-done.13 = f32[32,256]{1,0:T(8,128)S(1)} collective-permute-done((f32[32,256]{1,0:T(8,128)S(1)}, f32[32,256]{1,0:T(8,128)S(1)}, u32[]{:S(2)}, u32[]{:S(2)}) %collective-permute-start.13) | collective-permute-done | bytes 32800 | tf_op jit(solution)/shard_map/ppermute | solution.py:262
  75.3 0.7 collective-permute-done.12
  76.0 0.0 collective-permute-done.11
  76.0 0.6 pad_maximum_fusion.1
  (10 shorter events, 0.2 us)
Async XLA Ops:
  0.0 6.9 %copy-start = (bf16[128,256]{1,0:T(8,128)(2,1)S(1)}, bf16[128,256]{1,0:T(8,128)(2,1)}, u32[]{:S(2)}) copy-start(bf16[128,256]{1,0:T(8,128)(2,1)} %refs_0_.1) | copy-start | bytes 196612
  0.0 5.7 %collective-permute-start.1 = (bf16[128,256]{1,0:T(8,128)(2,1)}, bf16[128,256]{1,0:T(8,128)(2,1)S(1)}, u32[]{:S(2)}, u32[]{:S(2)}) collective-permute-start(bf16[128,256]{1,0:T(8,128)(2,1)} %refs_0_.1), channel_id=1, source_target_pairs={{0,16},{8,24},{16,0},{24,8},{1,17},{9,25},{17,1},{25,9},{2,18},{10... | collective-permute-start | bytes 196616 | tf_op jit(solution)/shard_map/ppermute | solution.py:262
  3.0 2.8 %collective-permute-start = (bf16[128,256]{1,0:T(8,128)(2,1)}, bf16[128,256]{1,0:T(8,128)(2,1)S(1)}, u32[]{:S(2)}, u32[]{:S(2)}) collective-permute-start(bf16[128,256]{1,0:T(8,128)(2,1)} %refs_0_.1), channel_id=1, source_target_pairs={{0,8},{8,0},{16,24},{24,16},{1,9},{9,1},{17,25},{25,17},{2,10},{10... | collective-permute-start | bytes 196616 | tf_op jit(solution)/shard_map/ppermute | solution.py:262
  3.0 4.0 %collective-permute-start.2 = (bf16[128,256]{1,0:T(8,128)(2,1)}, bf16[128,256]{1,0:T(8,128)(2,1)S(1)}, u32[]{:S(2)}, u32[]{:S(2)}) collective-permute-start(bf16[128,256]{1,0:T(8,128)(2,1)} %refs_0_.1), channel_id=1, source_target_pairs={{0,24},{8,16},{16,8},{24,0},{1,25},{9,17},{17,9},{25,1},{2,26},{10... | collective-permute-start | bytes 196616 | tf_op jit(solution)/shard_map/ppermute | solution.py:262
  8.0 11.0 %collective-permute-start.3 = (bf16[1,64,2048]{2,1,0:T(8,128)(2,1)S(1)}, bf16[1,64,2048]{2,1,0:T(8,128)(2,1)S(1)}, u32[]{:S(2)}, u32[]{:S(2)}) collective-permute-start(bf16[1,64,2048]{2,1,0:T(8,128)(2,1)S(1)} %get-tuple-element.24.skipped), channel_id=1, source_target_pairs={{0,6},{1,7},{2,4},{3,5},{4,2},{5,3},{6,0},{7,1},{8,14},{9,15},{10,... | collective-permute-start | bytes 786440 | tf_op jit(solution)/shard_map/ppermute | solution.py:262
  12.8 12.7 %collective-permute-start.4 = (bf16[1,64,2048]{2,1,0:T(8,128)(2,1)S(1)}, bf16[1,64,2048]{2,1,0:T(8,128)(2,1)S(1)}, u32[]{:S(2)}, u32[]{:S(2)}) collective-permute-start(bf16[1,64,2048]{2,1,0:T(8,128)(2,1)S(1)} %get-tuple-element.27), channel_id=1, source_target_pairs={{0,1},{1,0},{2,3},{3,2},{4,5},{5,4},{6,7},{7,6},{8,9},{9,8},{10,11... | collective-permute-start | bytes 786440 | tf_op jit(solution)/shard_map/ppermute | solution.py:262
  14.3 16.7 %collective-permute-start.5 = (bf16[1,64,2048]{2,1,0:T(8,128)(2,1)S(1)}, bf16[1,64,2048]{2,1,0:T(8,128)(2,1)S(1)}, u32[]{:S(2)}, u32[]{:S(2)}) collective-permute-start(bf16[1,64,2048]{2,1,0:T(8,128)(2,1)S(1)} %get-tuple-element.28), channel_id=1, source_target_pairs={{0,2},{1,3},{2,0},{3,1},{4,6},{5,7},{6,4},{7,5},{8,10},{9,11},{10,... | collective-permute-start | bytes 786440 | tf_op jit(solution)/shard_map/ppermute | solution.py:262
  14.3 24.2 %collective-permute-start.6 = (bf16[1,64,2048]{2,1,0:T(8,128)(2,1)S(1)}, bf16[1,64,2048]{2,1,0:T(8,128)(2,1)S(1)}, u32[]{:S(2)}, u32[]{:S(2)}) collective-permute-start(bf16[1,64,2048]{2,1,0:T(8,128)(2,1)S(1)} %get-tuple-element.29), channel_id=1, source_target_pairs={{0,3},{1,2},{2,1},{3,0},{4,7},{5,6},{6,5},{7,4},{8,11},{9,10},{10,... | collective-permute-start | bytes 786440 | tf_op jit(solution)/shard_map/ppermute | solution.py:262
  17.4 21.9 %collective-permute-start.7 = (bf16[1,64,2048]{2,1,0:T(8,128)(2,1)S(1)}, bf16[1,64,2048]{2,1,0:T(8,128)(2,1)S(1)}, u32[]{:S(2)}, u32[]{:S(2)}) collective-permute-start(bf16[1,64,2048]{2,1,0:T(8,128)(2,1)S(1)} %get-tuple-element.31), channel_id=1, source_target_pairs={{0,5},{1,4},{2,7},{3,6},{4,1},{5,0},{6,3},{7,2},{8,13},{9,12},{10,... | collective-permute-start | bytes 786440 | tf_op jit(solution)/shard_map/ppermute | solution.py:262
  19.0 32.9 %collective-permute-start.8 = (bf16[1,64,2048]{2,1,0:T(8,128)(2,1)S(1)}, bf16[1,64,2048]{2,1,0:T(8,128)(2,1)S(1)}, u32[]{:S(2)}, u32[]{:S(2)}) collective-permute-start(bf16[1,64,2048]{2,1,0:T(8,128)(2,1)S(1)} %get-tuple-element.32), channel_id=1, source_target_pairs={{0,4},{1,5},{2,6},{3,7},{4,0},{5,1},{6,2},{7,3},{8,12},{9,13},{10,... | collective-permute-start | bytes 786440 | tf_op jit(solution)/shard_map/ppermute | solution.py:262
  25.4 26.6 %collective-permute-start.9 = (bf16[1,64,2048]{2,1,0:T(8,128)(2,1)S(1)}, bf16[1,64,2048]{2,1,0:T(8,128)(2,1)S(1)}, u32[]{:S(2)}, u32[]{:S(2)}) collective-permute-start(bf16[1,64,2048]{2,1,0:T(8,128)(2,1)S(1)} %get-tuple-element.33), channel_id=1, source_target_pairs={{0,7},{1,6},{2,5},{3,4},{4,3},{5,2},{6,1},{7,0},{8,15},{9,14},{10,... | collective-permute-start | bytes 786440 | tf_op jit(solution)/shard_map/ppermute | solution.py:262
  52.9 1.6 %collective-permute-start.10 = (f32[8,32,256]{2,1,0:T(8,128)S(1)}, f32[8,32,256]{2,1,0:T(8,128)S(1)}, u32[]{:S(2)}, u32[]{:S(2)}) collective-permute-start(f32[8,32,256]{2,1,0:T(8,128)S(1)} %get-tuple-element.36), channel_id=1, source_target_pairs={{0,8},{8,0},{16,24},{24,16},{1,9},{9,1},{17,25},{25,17},{2,10},{10... | collective-permute-start | bytes 786440 | tf_op jit(solution)/shard_map/ppermute | solution.py:262
  71.3 4.0 %collective-permute-start.13 = (f32[32,256]{1,0:T(8,128)S(1)}, f32[32,256]{1,0:T(8,128)S(1)}, u32[]{:S(2)}, u32[]{:S(2)}) collective-permute-start(f32[32,256]{1,0:T(8,128)S(1)} %fusion), channel_id=1, source_target_pairs={{0,16},{8,24},{16,0},{24,8},{1,17},{9,25},{17,1},{25,9},{2,18},{10... | collective-permute-start | bytes 98312 | tf_op jit(solution)/shard_map/ppermute | solution.py:262
  72.6 3.4 %collective-permute-start.12 = (f32[32,256]{1,0:T(8,128)S(1)}, f32[32,256]{1,0:T(8,128)S(1)}, u32[]{:S(2)}, u32[]{:S(2)}) collective-permute-start(f32[32,256]{1,0:T(8,128)S(1)} %fusion), channel_id=1, source_target_pairs={{0,24},{8,16},{16,8},{24,0},{1,25},{9,17},{17,9},{25,1},{2,26},{10... | collective-permute-start | bytes 98312 | tf_op jit(solution)/shard_map/ppermute | solution.py:262
  72.6 3.4 %collective-permute-start.11 = (f32[32,256]{1,0:T(8,128)S(1)}, f32[32,256]{1,0:T(8,128)S(1)}, u32[]{:S(2)}, u32[]{:S(2)}) collective-permute-start(f32[32,256]{1,0:T(8,128)S(1)} %fusion), channel_id=1, source_target_pairs={{0,8},{8,0},{16,24},{24,16},{1,9},{9,1},{17,25},{25,17},{2,10},{10... | collective-permute-start | bytes 98312 | tf_op jit(solution)/shard_map/ppermute | solution.py:262

commit v7 on v6

--- a/solution.py
+++ b/solution.py
@@ -60,16 +60,10 @@
     )(count, in_hbm(block), in_hbm(tiles))
 
 
-def multiply(turned_ref, tiles_ref, group_starts, place, outs):
+def products(turned_ref, tiles_ref, group_starts):
     slots, width, extent = tiles_ref.shape
     half = turned_ref.shape[0] // 2
     step = SUB * width
-    row_at = lax.broadcasted_iota(jnp.int32, (SUB * SUB, SUB * SUB), 0)
-    col_at = lax.broadcasted_iota(jnp.int32, (SUB * SUB, SUB * SUB), 1)
-    bits = SUB.bit_length() - 1
-    swap = (col_at == ((row_at & (SUB - 1)) << bits) + (row_at >> bits)).astype(jnp.bfloat16)
-    low = lax.broadcasted_iota(jnp.int32, (SUB, LANES), 1) < width
-    groups = len(group_starts)
     lhs = jnp.concatenate(
         [
             turned_ref[pl.ds(pl.multiple_of(first + at, SUB), SUB), :]
@@ -78,14 +72,22 @@
         ],
         axis=0,
     )
-    chunks = extent // step
+    for at in range(extent // step):
+        rhs = tiles_ref[:, :, at * step:(at + 1) * step].reshape(slots * width, step)
+        yield at, jnp.dot(lhs, rhs, preferred_element_type=jnp.float32)
+
+
+def arrange(chunks, groups, width, place, outs):
+    row_at = lax.broadcasted_iota(jnp.int32, (SUB * SUB, SUB * SUB), 0)
+    col_at = lax.broadcasted_iota(jnp.int32, (SUB * SUB, SUB * SUB), 1)
+    bits = SUB.bit_length() - 1
+    swap = (col_at == ((row_at & (SUB - 1)) << bits) + (row_at >> bits)).astype(jnp.bfloat16)
+    low = lax.broadcasted_iota(jnp.int32, (SUB, LANES), 1) < width
     sides = []
-    for at in range(chunks):
-        rhs = tiles_ref[:, :, at * step:(at + 1) * step].reshape(slots * width, step)
-        acc = jnp.dot(lhs, rhs, preferred_element_type=jnp.float32)
+    for at, acc in chunks:
         for s in range(groups):
             per_mu = []
-            for q in range(step // LANES):
+            for q in range(acc.shape[1] // LANES):
                 a = acc[s * SUB:(s + 1) * SUB, q * LANES:(q + 1) * LANES]
                 b = acc[(groups + s) * SUB:(groups + s + 1) * SUB, q * LANES:(q + 1) * LANES]
                 per_mu.append(jnp.where(low, a, pltpu.roll(b, width, 1)).astype(jnp.bfloat16))
@@ -102,7 +104,34 @@
             ]
 
 
-def first_kernel(group_starts, place, n_parts, block_ref, tiles_ref, *refs):
+def multiply(turned_ref, tiles_ref, group_starts, place, outs):
+    chunks = list(products(turned_ref, tiles_ref, group_starts))
+    arrange(chunks, len(group_starts), tiles_ref.shape[1], place, outs)
+
+
+def arrange_kernel(width, rows_ref, out_ref):
+    step = SUB * width
+    chunks = [
+        (at, rows_ref[:, at * step:(at + 1) * step].astype(jnp.float32)) for at in range(rows_ref.shape[1] // step)
+    ]
+    arrange(chunks, 1, width, lambda s, k: (0, 0, k), [out_ref])
+
+
+def arranged(rows, width):
+    made = rows.shape[0] * rows.shape[1] // width
+    return pl.pallas_call(
+        functools.partial(arrange_kernel, width),
+        out_shape=jax.ShapeDtypeStruct((1, width, made), rows.dtype),
+        in_specs=[pl.BlockSpec(memory_space=pltpu.VMEM)],
+        out_specs=pl.BlockSpec(memory_space=pltpu.VMEM),
+        compiler_params=pltpu.CompilerParams(vmem_limit_bytes=VMEM_LIMIT),
+        cost_estimate=pl.CostEstimate(
+            flops=2 * SUB * SUB * width * made, bytes_accessed=4 * width * made, transcendentals=0
+        ),
+    )(rows)
+
+
+def first_kernel(group_starts, place, n_parts, plain, block_ref, tiles_ref, *refs):
     parts, (full_ref, turned_ref, *outs), picked = refs[:n_parts], refs[n_parts:-1], refs[-1]
     slots, width, _ = tiles_ref.shape
     depth = parts[0].shape[0]
@@ -114,7 +143,12 @@
         rows = full_ref[pl.ds(row, width), :]
         picked[t * width:(t + 1) * width, :] = jnp.where(block_ref[0, t] >= 0, rows, jnp.zeros_like(rows))
     turned_ref[...] = picked[...].T
-    multiply(turned_ref, tiles_ref, group_starts(), place, outs)
+    if plain:
+        for at, acc in products(turned_ref, tiles_ref, group_starts()):
+            step = acc.shape[1]
+            outs[0][:, at * step:(at + 1) * step] = acc.astype(jnp.bfloat16)
+    else:
+        multiply(turned_ref, tiles_ref, group_starts(), place, outs)
 
 
 def next_kernel(group_starts, place, turned_ref, tiles_ref, skipped, *outs):
@@ -129,12 +163,12 @@
     )
 
 
-def contract_first(group_starts, place, out_shapes, block, tiles, parts):
+def contract_first(group_starts, place, out_shapes, block, tiles, parts, plain=False):
     slots, width, _ = tiles.shape
     depth, norb = parts[0].shape
     shapes = [(depth * len(parts), norb), (norb, slots * width)] + out_shapes
     full, turned, *made = pl.pallas_call(
-        functools.partial(first_kernel, group_starts, place, len(parts)),
+        functools.partial(first_kernel, group_starts, place, len(parts), plain),
         out_shape=[jax.ShapeDtypeStruct(shape, jnp.bfloat16) for shape in shapes],
         in_specs=[pl.BlockSpec(memory_space=pltpu.VMEM)] * (2 + len(parts)),
         out_specs=[pl.BlockSpec(memory_space=pltpu.VMEM)] * len(shapes),
@@ -304,15 +338,16 @@
         def shapes(ks):
             return [(1, width, cols)] * len(ks)
 
-        waves, late_ks = [[6], [0, 1, 2, 3], [5, 4, 7]], [5, 4, 7]
+        waves, late_ks = [[6], [0, 2, 3, 1], [5, 4, 7]], [5, 4, 7]
         full, turned, made = contract_first(
-            starts(waves[0]), own_output, shapes(waves[0]), block, inside, parts
+            starts(waves[0]), None, [(2 * SUB, tiles.shape[4])], block, inside, parts, plain=True
         )
         sent = dict(zip(waves[0], made))
         for wave in waves[1:]:
             made = contract_next(starts(wave), own_output, shapes(wave), turned, inside, made[0])
             sent.update(zip(wave, made))
         received = {k: swapped(sent[k], "grid", k) if k else sent[k] for wave in waves for k in wave}
+        received[waves[0][0]] = arranged(received[waves[0][0]], width)
         early_ks = [k for wave in waves for k in wave if k not in late_ks]
         early, late = [received[k] for k in early_ks], [received[k] for k in late_ks]
         early_ids, late_ids, all_ids = ids(early_ks), ids(late_ks), ids(early_ks + late_ks)

time: 76.8 us -> 76.5 us (level)
  waiting for transfers between devices: 29.4 us -> 26.1 us
  starting transfers between devices: 21.8 us -> 24.7 us
    ppermute x14, waiting for transfers between devices: 29.4 us -> 26.1 us  [swapped(): lax.ppermute(x, axis, [(i, i ^ k) for i in range(lax.axis_size(axis))])]
    ppermute x14, starting transfers between devices: 21.8 us -> 24.7 us  [swapped(): lax.ppermute(x, axis, [(i, i ^ k) for i in range(lax.axis_size(axis))])]
where the time goes in v7:
time: 76.5 us; the launch traced here: 76.3 us
  waiting for transfers between devices  26.1 us (34%)
  starting transfers between devices  24.7 us (32%)
  blocking collectives  16.5 us (22%)
  Pallas kernels  7.26 us (9%)
  other arithmetic  0.84 us (1%)
  between operations  0.82 us (1%)
    ppermute x14, waiting for transfers between devices, swapped(): lax.ppermute(x, axis, [(i, i ^ k) for i in range(lax.axis_size(axis))])  26.1 us
    ppermute x14, starting transfers between devices, swapped(): lax.ppermute(x, axis, [(i, i ^ k) for i in range(lax.axis_size(axis))])  24.7 us
    all_to_all x1, blocking collectives, summed_blocks(): lax.all_to_all(jnp.concatenate([scaled, tail], axis=1), axis, 0, 0, tiled...  16.5 us
    pallas_call x2, Pallas kernels, contract_next(): pl.pallas_call(functools.partial(next_kernel, group_starts, place), out_s...  2.1 us
    pallas_call x1, Pallas kernels, load(): pl.pallas_call(load_kernel, out_shape=[jax.ShapeDtypeStruct(tiles.shape[2...  1.91 us
  transfers between devices with their start and end apart: 14, of which 8 were waited for; matrix products, arithmetic and copies ran while one was open for 0% of the time, Pallas kernels for 7%

profile of v7, /device:TPU:0, one launch (start us, length us, event | category | flops | bytes accessed | tf_op | source)
XLA Modules:
  0.0 76.3 jit_solution(11026883878905389287)
XLA Ops:
  0.0 0.0 copy-start
  0.0 3.0 %collective-permute-start.1 = (bf16[128,256]{1,0:T(8,128)(2,1)}, bf16[128,256]{1,0:T(8,128)(2,1)S(1)}, u32[]{:S(2)}, u32[]{:S(2)}) collective-permute-start(bf16[128,256]{1,0:T(8,128)(2,1)} %refs_0_.1), channel_id=1, source_target_pairs={{0,16},{8,24},{16,0},{24,8},{1,17},{9,25},{17,1},{25,9},{2,18},{10... | collective-permute-start | bytes 196616 | tf_op jit(solution)/shard_map/ppermute | solution.py:296
  3.0 0.0 collective-permute-start
  3.0 0.2 collective-permute-start.2
  3.8 1.9 %shard_map.46 = (bf16[6,64,4096]{2,1,0:T(8,128)(2,1)S(1)}, s32[1,6]{1,0:T(1,128)S(1)}) custom-call(s32[1,1]{1,0:T(1,128)S(6)} %copy.8.count_ref, s32[1,1,6]{2,1,0:T(1,128)} %block_hbm.1, bf16[1,1,6,64,4096]{4,3,2,1,0:T(8,128)(2,1)} %tiles_hbm.1), custom_call_target="tpu_custom_call" | custom-call | bytes 3145728 | tf_op jit(solution)/shard_map/pallas_call | solution.py:41
  5.7 0.0 collective-permute-done.1.refs_2_
  5.7 0.0 collective-permute-done.refs_1_
  5.8 1.2 %collective-permute-done.2.refs_3_ = bf16[128,256]{1,0:T(8,128)(2,1)S(1)} collective-permute-done((bf16[128,256]{1,0:T(8,128)(2,1)}, bf16[128,256]{1,0:T(8,128)(2,1)S(1)}, u32[]{:S(2)}, u32[]{:S(2)}) %collective-permute-start.2) | collective-permute-done | bytes 65568 | tf_op jit(solution)/shard_map/ppermute | solution.py:296
  6.9 0.0 copy-done
  6.9 0.8 %shard_map.47 = (bf16[512,256]{1,0:T(8,128)(2,1)S(1)}, bf16[256,384]{1,0:T(8,128)(2,1)S(1)}, bf16[32,4096]{1,0:T(8,128)(2,1)S(1)}) custom-call(s32[1,6]{1,0:T(1,128)S(1)} %get-tuple-element.21.block_ref, bf16[6,64,4096]{2,1,0:T(8,128)(2,1)S(1)} %get-tuple-element.22.tiles_ref, bf16[128,256]{1,0:T(8,128)(2,1)S(1)} %copy-done, ...), custom_call_target="tpu_custom_call" | custom-call | flops 100663296 | bytes 3407872 | tf_op jit(solution)/shard_map/pallas_call | solution.py:170
  7.8 3.6 %collective-permute-start.3 = (bf16[32,4096]{1,0:T(8,128)(2,1)S(1)}, bf16[32,4096]{1,0:T(8,128)(2,1)S(1)}, u32[]{:S(2)}, u32[]{:S(2)}) collective-permute-start(bf16[32,4096]{1,0:T(8,128)(2,1)S(1)} %get-tuple-element.24.skipped), channel_id=1, source_target_pairs={{0,6},{1,7},{2,4},{3,5},{4,2},{5,3},{6,0},{7,1},{8,14},{9,15},{10,... | collective-permute-start | bytes 786440 | tf_op jit(solution)/shard_map/ppermute | solution.py:296
  11.4 1.1 %shard_map.49 = (bf16[1,64,2048]{2,1,0:T(8,128)(2,1)S(1)}, bf16[1,64,2048]{2,1,0:T(8,128)(2,1)S(1)}, bf16[1,64,2048]{2,1,0:T(8,128)(2,1)S(1)}, bf16[1,64,2048]{2,1,0:T(8,128)(2,1)S(1)}) custom-call(bf16[256,384]{1,0:T(8,128)(2,1)S(1)} %get-tuple-element.25.turned_ref, bf16[6,64,4096]{2,1,0:T(8,128)(2,1)S(1)} %get-tuple-element.22.tiles_ref, ...), custom_call_target="tpu_custom_call" | custom-call | flops 402653184 | bytes 4194304 | tf_op jit(solution)/shard_map/pallas_call | solution.py:183
  12.5 0.1 collective-permute-start.4
  12.5 2.9 %collective-permute-start.5 = (bf16[1,64,2048]{2,1,0:T(8,128)(2,1)S(1)}, bf16[1,64,2048]{2,1,0:T(8,128)(2,1)S(1)}, u32[]{:S(2)}, u32[]{:S(2)}) collective-permute-start(bf16[1,64,2048]{2,1,0:T(8,128)(2,1)S(1)} %get-tuple-element.28), channel_id=1, source_target_pairs={{0,3},{1,2},{2,1},{3,0},{4,7},{5,6},{6,5},{7,4},{8,11},{9,10},{10,... | collective-permute-start | bytes 786440 | tf_op jit(solution)/shard_map/ppermute | solution.py:296
  15.5 0.5 collective-permute-start.6
  16.0 1.0 %shard_map.51 = (bf16[1,64,2048]{2,1,0:T(8,128)(2,1)S(1)}, bf16[1,64,2048]{2,1,0:T(8,128)(2,1)S(1)}, bf16[1,64,2048]{2,1,0:T(8,128)(2,1)S(1)}) custom-call(bf16[256,384]{1,0:T(8,128)(2,1)S(1)} %get-tuple-element.25.turned_ref, bf16[6,64,4096]{2,1,0:T(8,128)(2,1)S(1)} %get-tuple-element.22.tiles_ref, bf16[1,64,2048]{2,1,0:T(8,128)(2,1)S(1)} %get-tuple-element.26.refs_1_.skipped), custom_call_target="tpu_custom_call" | custom-call | flops 301989888 | bytes 3932160 | tf_op jit(solution)/shard_map/pallas_call | solution.py:183
  17.1 0.4 collective-permute-start.7
  17.5 1.3 %collective-permute-done.3.rows_ref = bf16[32,4096]{1,0:T(8,128)(2,1)S(1)} collective-permute-done((bf16[32,4096]{1,0:T(8,128)(2,1)S(1)}, bf16[32,4096]{1,0:T(8,128)(2,1)S(1)}, u32[]{:S(2)}, u32[]{:S(2)}) %collective-permute-start.3) | collective-permute-done | bytes 262176 | tf_op jit(solution)/shard_map/ppermute | solution.py:296
  18.8 6.3 %collective-permute-start.8 = (bf16[1,64,2048]{2,1,0:T(8,128)(2,1)S(1)}, bf16[1,64,2048]{2,1,0:T(8,128)(2,1)S(1)}, u32[]{:S(2)}, u32[]{:S(2)}) collective-permute-start(bf16[1,64,2048]{2,1,0:T(8,128)(2,1)S(1)} %get-tuple-element.32), channel_id=1, source_target_pairs={{0,4},{1,5},{2,6},{3,7},{4,0},{5,1},{6,2},{7,3},{8,12},{9,13},{10,... | collective-permute-start | bytes 786440 | tf_op jit(solution)/shard_map/ppermute | solution.py:296
  25.1 5.6 %collective-permute-done.4.refs_2_ = bf16[1,64,2048]{2,1,0:T(8,128)(2,1)S(1)} collective-permute-done((bf16[1,64,2048]{2,1,0:T(8,128)(2,1)S(1)}, bf16[1,64,2048]{2,1,0:T(8,128)(2,1)S(1)}, u32[]{:S(2)}, u32[]{:S(2)}) %collective-permute-start.4) | collective-permute-done | bytes 262176 | tf_op jit(solution)/shard_map/ppermute | solution.py:296
  30.7 5.3 %collective-permute-start.9 = (bf16[1,64,2048]{2,1,0:T(8,128)(2,1)S(1)}, bf16[1,64,2048]{2,1,0:T(8,128)(2,1)S(1)}, u32[]{:S(2)}, u32[]{:S(2)}) collective-permute-start(bf16[1,64,2048]{2,1,0:T(8,128)(2,1)S(1)} %get-tuple-element.33), channel_id=1, source_target_pairs={{0,7},{1,6},{2,5},{3,4},{4,3},{5,2},{6,1},{7,0},{8,15},{9,14},{10,... | collective-permute-start | bytes 786440 | tf_op jit(solution)/shard_map/ppermute | solution.py:296
  36.0 0.3 shard_map.48.refs_0_
  36.4 1.8 %collective-permute-done.5.refs_3_ = bf16[1,64,2048]{2,1,0:T(8,128)(2,1)S(1)} collective-permute-done((bf16[1,64,2048]{2,1,0:T(8,128)(2,1)S(1)}, bf16[1,64,2048]{2,1,0:T(8,128)(2,1)S(1)}, u32[]{:S(2)}, u32[]{:S(2)}) %collective-permute-start.5) | collective-permute-done | bytes 262176 | tf_op jit(solution)/shard_map/ppermute | solution.py:296
  38.2 0.0 collective-permute-done.6.refs_4_
  38.2 0.7 shard_map.50
  38.9 0.0 collective-permute-done.7.refs_5_
  39.0 12.7 %collective-permute-done.8.refs_6_ = bf16[1,64,2048]{2,1,0:T(8,128)(2,1)S(1)} collective-permute-done((bf16[1,64,2048]{2,1,0:T(8,128)(2,1)S(1)}, bf16[1,64,2048]{2,1,0:T(8,128)(2,1)S(1)}, u32[]{:S(2)}, u32[]{:S(2)}) %collective-permute-start.8) | collective-permute-done | bytes 262176 | tf_op jit(solution)/shard_map/ppermute | solution.py:296
  51.7 0.0 collective-permute-done.9.refs_7_
  51.7 0.9 %shard_map.52 = (f32[8,32,256]{2,1,0:T(8,128)S(1)}, bf16[256,2048]{1,0:T(8,128)(2,1)S(1)}) custom-call(f32[256,2048]{1,0:T(8,128)S(1)} %get-tuple-element.30.fitted_ref, bf16[1,64,2048]{2,1,0:T(8,128)(2,1)S(1)} %shard_map.48.refs_0_, bf16[1,64,2048]{2,1,0:T(8,128)(2,1)S(1)} %get-tuple-element.26.refs_1_.skipped, ...), custom_call_target="tpu_custom_call" | custom-call | flops 536870912 | bytes 2097152 | tf_op jit(solution)/shard_map/pallas_call | solution.py:274
  52.6 0.1 collective-permute-start.10
  52.6 0.5 shard_map.53
  53.1 1.0 %collective-permute-done.10 = f32[8,32,256]{2,1,0:T(8,128)S(1)} collective-permute-done((f32[8,32,256]{2,1,0:T(8,128)S(1)}, f32[8,32,256]{2,1,0:T(8,128)S(1)}, u32[]{:S(2)}, u32[]{:S(2)}) %collective-permute-start.10) | collective-permute-done | bytes 262176 | tf_op jit(solution)/shard_map/ppermute | solution.py:296
  54.3 16.5 %all_to_all.5 = f16[8,40,256]{2,1,0:T(8,128)(2,1)S(1)} all-to-all(f16[8,40,256]{2,1,0:T(8,128)(2,1)S(1)} %pad_maximum_fusion), channel_id=1, replica_groups=mesh['rep'=4,'grid'=8] {'grid'}, dimensions={0} | all-to-all | bytes 327680 | tf_op jit(solution)/shard_map/all_to_all | solution.py:305
  71.0 1.3 %collective-permute-start.13 = (f32[32,256]{1,0:T(8,128)S(1)}, f32[32,256]{1,0:T(8,128)S(1)}, u32[]{:S(2)}, u32[]{:S(2)}) collective-permute-start(f32[32,256]{1,0:T(8,128)S(1)} %fusion), channel_id=1, source_target_pairs={{0,16},{8,24},{16,0},{24,8},{1,17},{9,25},{17,1},{25,9},{2,18},{10... | collective-permute-start | bytes 98312 | tf_op jit(solution)/shard_map/ppermute | solution.py:296
  72.2 0.0 collective-permute-start.12
  72.3 0.9 %collective-permute-start.11 = (f32[32,256]{1,0:T(8,128)S(1)}, f32[32,256]{1,0:T(8,128)S(1)}, u32[]{:S(2)}, u32[]{:S(2)}) collective-permute-start(f32[32,256]{1,0:T(8,128)S(1)} %fusion), channel_id=1, source_target_pairs={{0,8},{8,0},{16,24},{24,16},{1,9},{9,1},{17,25},{25,17},{2,10},{10... | collective-permute-start | bytes 98312 | tf_op jit(solution)/shard_map/ppermute | solution.py:296
  73.2 1.8 %collective-permute-done.13 = f32[32,256]{1,0:T(8,128)S(1)} collective-permute-done((f32[32,256]{1,0:T(8,128)S(1)}, f32[32,256]{1,0:T(8,128)S(1)}, u32[]{:S(2)}, u32[]{:S(2)}) %collective-permute-start.13) | collective-permute-done | bytes 32800 | tf_op jit(solution)/shard_map/ppermute | solution.py:296
  75.0 0.7 collective-permute-done.12
  75.7 0.0 collective-permute-done.11
  75.7 0.6 pad_maximum_fusion.1
  (10 shorter events, 0.2 us)
Async XLA Ops:
  0.0 6.9 %copy-start = (bf16[128,256]{1,0:T(8,128)(2,1)S(1)}, bf16[128,256]{1,0:T(8,128)(2,1)}, u32[]{:S(2)}) copy-start(bf16[128,256]{1,0:T(8,128)(2,1)} %refs_0_.1) | copy-start | bytes 196612
  0.0 5.7 %collective-permute-start.1 = (bf16[128,256]{1,0:T(8,128)(2,1)}, bf16[128,256]{1,0:T(8,128)(2,1)S(1)}, u32[]{:S(2)}, u32[]{:S(2)}) collective-permute-start(bf16[128,256]{1,0:T(8,128)(2,1)} %refs_0_.1), channel_id=1, source_target_pairs={{0,16},{8,24},{16,0},{24,8},{1,17},{9,25},{17,1},{25,9},{2,18},{10... | collective-permute-start | bytes 196616 | tf_op jit(solution)/shard_map/ppermute | solution.py:296
  3.0 2.8 %collective-permute-start = (bf16[128,256]{1,0:T(8,128)(2,1)}, bf16[128,256]{1,0:T(8,128)(2,1)S(1)}, u32[]{:S(2)}, u32[]{:S(2)}) collective-permute-start(bf16[128,256]{1,0:T(8,128)(2,1)} %refs_0_.1), channel_id=1, source_target_pairs={{0,8},{8,0},{16,24},{24,16},{1,9},{9,1},{17,25},{25,17},{2,10},{10... | collective-permute-start | bytes 196616 | tf_op jit(solution)/shard_map/ppermute | solution.py:296
  3.0 4.0 %collective-permute-start.2 = (bf16[128,256]{1,0:T(8,128)(2,1)}, bf16[128,256]{1,0:T(8,128)(2,1)S(1)}, u32[]{:S(2)}, u32[]{:S(2)}) collective-permute-start(bf16[128,256]{1,0:T(8,128)(2,1)} %refs_0_.1), channel_id=1, source_target_pairs={{0,24},{8,16},{16,8},{24,0},{1,25},{9,17},{17,9},{25,1},{2,26},{10... | collective-permute-start | bytes 196616 | tf_op jit(solution)/shard_map/ppermute | solution.py:296
  7.8 11.0 %collective-permute-start.3 = (bf16[32,4096]{1,0:T(8,128)(2,1)S(1)}, bf16[32,4096]{1,0:T(8,128)(2,1)S(1)}, u32[]{:S(2)}, u32[]{:S(2)}) collective-permute-start(bf16[32,4096]{1,0:T(8,128)(2,1)S(1)} %get-tuple-element.24.skipped), channel_id=1, source_target_pairs={{0,6},{1,7},{2,4},{3,5},{4,2},{5,3},{6,0},{7,1},{8,14},{9,15},{10,... | collective-permute-start | bytes 786440 | tf_op jit(solution)/shard_map/ppermute | solution.py:296
  12.5 18.3 %collective-permute-start.4 = (bf16[1,64,2048]{2,1,0:T(8,128)(2,1)S(1)}, bf16[1,64,2048]{2,1,0:T(8,128)(2,1)S(1)}, u32[]{:S(2)}, u32[]{:S(2)}) collective-permute-start(bf16[1,64,2048]{2,1,0:T(8,128)(2,1)S(1)} %get-tuple-element.27), channel_id=1, source_target_pairs={{0,2},{1,3},{2,0},{3,1},{4,6},{5,7},{6,4},{7,5},{8,10},{9,11},{10,... | collective-permute-start | bytes 786440 | tf_op jit(solution)/shard_map/ppermute | solution.py:296
  12.5 25.7 %collective-permute-start.5 = (bf16[1,64,2048]{2,1,0:T(8,128)(2,1)S(1)}, bf16[1,64,2048]{2,1,0:T(8,128)(2,1)S(1)}, u32[]{:S(2)}, u32[]{:S(2)}) collective-permute-start(bf16[1,64,2048]{2,1,0:T(8,128)(2,1)S(1)} %get-tuple-element.28), channel_id=1, source_target_pairs={{0,3},{1,2},{2,1},{3,0},{4,7},{5,6},{6,5},{7,4},{8,11},{9,10},{10,... | collective-permute-start | bytes 786440 | tf_op jit(solution)/shard_map/ppermute | solution.py:296
  15.5 22.7 %collective-permute-start.6 = (bf16[1,64,2048]{2,1,0:T(8,128)(2,1)S(1)}, bf16[1,64,2048]{2,1,0:T(8,128)(2,1)S(1)}, u32[]{:S(2)}, u32[]{:S(2)}) collective-permute-start(bf16[1,64,2048]{2,1,0:T(8,128)(2,1)S(1)} %get-tuple-element.29), channel_id=1, source_target_pairs={{0,1},{1,0},{2,3},{3,2},{4,5},{5,4},{6,7},{7,6},{8,9},{9,8},{10,11... | collective-permute-start | bytes 786440 | tf_op jit(solution)/shard_map/ppermute | solution.py:296
  17.1 21.9 %collective-permute-start.7 = (bf16[1,64,2048]{2,1,0:T(8,128)(2,1)S(1)}, bf16[1,64,2048]{2,1,0:T(8,128)(2,1)S(1)}, u32[]{:S(2)}, u32[]{:S(2)}) collective-permute-start(bf16[1,64,2048]{2,1,0:T(8,128)(2,1)S(1)} %get-tuple-element.31), channel_id=1, source_target_pairs={{0,5},{1,4},{2,7},{3,6},{4,1},{5,0},{6,3},{7,2},{8,13},{9,12},{10,... | collective-permute-start | bytes 786440 | tf_op jit(solution)/shard_map/ppermute | solution.py:296
  18.8 32.9 %collective-permute-start.8 = (bf16[1,64,2048]{2,1,0:T(8,128)(2,1)S(1)}, bf16[1,64,2048]{2,1,0:T(8,128)(2,1)S(1)}, u32[]{:S(2)}, u32[]{:S(2)}) collective-permute-start(bf16[1,64,2048]{2,1,0:T(8,128)(2,1)S(1)} %get-tuple-element.32), channel_id=1, source_target_pairs={{0,4},{1,5},{2,6},{3,7},{4,0},{5,1},{6,2},{7,3},{8,12},{9,13},{10,... | collective-permute-start | bytes 786440 | tf_op jit(solution)/shard_map/ppermute | solution.py:296
  30.7 20.9 %collective-permute-start.9 = (bf16[1,64,2048]{2,1,0:T(8,128)(2,1)S(1)}, bf16[1,64,2048]{2,1,0:T(8,128)(2,1)S(1)}, u32[]{:S(2)}, u32[]{:S(2)}) collective-permute-start(bf16[1,64,2048]{2,1,0:T(8,128)(2,1)S(1)} %get-tuple-element.33), channel_id=1, source_target_pairs={{0,7},{1,6},{2,5},{3,4},{4,3},{5,2},{6,1},{7,0},{8,15},{9,14},{10,... | collective-permute-start | bytes 786440 | tf_op jit(solution)/shard_map/ppermute | solution.py:296
  52.6 1.6 %collective-permute-start.10 = (f32[8,32,256]{2,1,0:T(8,128)S(1)}, f32[8,32,256]{2,1,0:T(8,128)S(1)}, u32[]{:S(2)}, u32[]{:S(2)}) collective-permute-start(f32[8,32,256]{2,1,0:T(8,128)S(1)} %get-tuple-element.36), channel_id=1, source_target_pairs={{0,8},{8,0},{16,24},{24,16},{1,9},{9,1},{17,25},{25,17},{2,10},{10... | collective-permute-start | bytes 786440 | tf_op jit(solution)/shard_map/ppermute | solution.py:296
  71.0 4.0 %collective-permute-start.13 = (f32[32,256]{1,0:T(8,128)S(1)}, f32[32,256]{1,0:T(8,128)S(1)}, u32[]{:S(2)}, u32[]{:S(2)}) collective-permute-start(f32[32,256]{1,0:T(8,128)S(1)} %fusion), channel_id=1, source_target_pairs={{0,16},{8,24},{16,0},{24,8},{1,17},{9,25},{17,1},{25,9},{2,18},{10... | collective-permute-start | bytes 98312 | tf_op jit(solution)/shard_map/ppermute | solution.py:296
  72.2 3.4 %collective-permute-start.12 = (f32[32,256]{1,0:T(8,128)S(1)}, f32[32,256]{1,0:T(8,128)S(1)}, u32[]{:S(2)}, u32[]{:S(2)}) collective-permute-start(f32[32,256]{1,0:T(8,128)S(1)} %fusion), channel_id=1, source_target_pairs={{0,24},{8,16},{16,8},{24,0},{1,25},{9,17},{17,9},{25,1},{2,26},{10... | collective-permute-start | bytes 98312 | tf_op jit(solution)/shard_map/ppermute | solution.py:296
  72.3 3.4 %collective-permute-start.11 = (f32[32,256]{1,0:T(8,128)S(1)}, f32[32,256]{1,0:T(8,128)S(1)}, u32[]{:S(2)}, u32[]{:S(2)}) collective-permute-start(f32[32,256]{1,0:T(8,128)S(1)} %fusion), channel_id=1, source_target_pairs={{0,8},{8,0},{16,24},{24,16},{1,9},{9,1},{17,25},{25,17},{2,10},{10... | collective-permute-start | bytes 98312 | tf_op jit(solution)/shard_map/ppermute | solution.py:296

commit v8 on v7

--- a/solution.py
+++ b/solution.py
@@ -273,7 +273,7 @@
     )
     send, columns = pl.pallas_call(
         functools.partial(
-            send_kernel, fit_scale, mix_scale, min(512, cols), width, ids, len(early), len(late)
+            send_kernel, fit_scale, mix_scale, cols, width, ids, len(early), len(late)
         ),
         out_shape=[half, jax.ShapeDtypeStruct((norb, cols), jnp.bfloat16)],
         in_specs=[pl.BlockSpec(memory_space=pltpu.VMEM)] * (len(fitted) + len(rows)),

time: 76.5 us -> 76.5 us (level)
  no operation moved by 1% of the time
where the time goes in v8:
time: 76.5 us; the launch traced here: 76.3 us
  waiting for transfers between devices  26.1 us (34%)
  starting transfers between devices  24.7 us (32%)
  blocking collectives  16.5 us (22%)
  Pallas kernels  7.26 us (9%)
  other arithmetic  0.84 us (1%)
  between operations  0.82 us (1%)
    ppermute x14, waiting for transfers between devices, swapped(): lax.ppermute(x, axis, [(i, i ^ k) for i in range(lax.axis_size(axis))])  26.1 us
    ppermute x14, starting transfers between devices, swapped(): lax.ppermute(x, axis, [(i, i ^ k) for i in range(lax.axis_size(axis))])  24.7 us
    all_to_all x1, blocking collectives, summed_blocks(): lax.all_to_all(jnp.concatenate([scaled, tail], axis=1), axis, 0, 0, tiled...  16.5 us
    pallas_call x2, Pallas kernels, contract_next(): pl.pallas_call(functools.partial(next_kernel, group_starts, place), out_s...  2.1 us
    pallas_call x1, Pallas kernels, load(): pl.pallas_call(load_kernel, out_shape=[jax.ShapeDtypeStruct(tiles.shape[2...  1.91 us
  transfers between devices with their start and end apart: 14, of which 8 were waited for; matrix products, arithmetic and copies ran while one was open for 0% of the time, Pallas kernels for 7%

profile of v8, /device:TPU:0, one launch (start us, length us, event | category | flops | bytes accessed | tf_op | source)
XLA Modules:
  0.0 76.3 jit_solution(11026883878905389287)
XLA Ops:
  0.0 0.0 copy-start
  0.0 3.0 %collective-permute-start.1 = (bf16[128,256]{1,0:T(8,128)(2,1)}, bf16[128,256]{1,0:T(8,128)(2,1)S(1)}, u32[]{:S(2)}, u32[]{:S(2)}) collective-permute-start(bf16[128,256]{1,0:T(8,128)(2,1)} %refs_0_.1), channel_id=1, source_target_pairs={{0,16},{8,24},{16,0},{24,8},{1,17},{9,25},{17,1},{25,9},{2,18},{10... | collective-permute-start | bytes 196616 | tf_op jit(solution)/shard_map/ppermute | solution.py:296
  3.0 0.0 collective-permute-start
  3.0 0.2 collective-permute-start.2
  3.8 1.9 %shard_map.46 = (bf16[6,64,4096]{2,1,0:T(8,128)(2,1)S(1)}, s32[1,6]{1,0:T(1,128)S(1)}) custom-call(s32[1,1]{1,0:T(1,128)S(6)} %copy.8.count_ref, s32[1,1,6]{2,1,0:T(1,128)} %block_hbm.1, bf16[1,1,6,64,4096]{4,3,2,1,0:T(8,128)(2,1)} %tiles_hbm.1), custom_call_target="tpu_custom_call" | custom-call | bytes 3145728 | tf_op jit(solution)/shard_map/pallas_call | solution.py:41
  5.7 0.0 collective-permute-done.1.refs_2_
  5.7 0.0 collective-permute-done.refs_1_
  5.8 1.2 %collective-permute-done.2.refs_3_ = bf16[128,256]{1,0:T(8,128)(2,1)S(1)} collective-permute-done((bf16[128,256]{1,0:T(8,128)(2,1)}, bf16[128,256]{1,0:T(8,128)(2,1)S(1)}, u32[]{:S(2)}, u32[]{:S(2)}) %collective-permute-start.2) | collective-permute-done | bytes 65568 | tf_op jit(solution)/shard_map/ppermute | solution.py:296
  6.9 0.0 copy-done
  6.9 0.8 %shard_map.47 = (bf16[512,256]{1,0:T(8,128)(2,1)S(1)}, bf16[256,384]{1,0:T(8,128)(2,1)S(1)}, bf16[32,4096]{1,0:T(8,128)(2,1)S(1)}) custom-call(s32[1,6]{1,0:T(1,128)S(1)} %get-tuple-element.21.block_ref, bf16[6,64,4096]{2,1,0:T(8,128)(2,1)S(1)} %get-tuple-element.22.tiles_ref, bf16[128,256]{1,0:T(8,128)(2,1)S(1)} %copy-done, ...), custom_call_target="tpu_custom_call" | custom-call | flops 100663296 | bytes 3407872 | tf_op jit(solution)/shard_map/pallas_call | solution.py:170
  7.8 3.6 %collective-permute-start.3 = (bf16[32,4096]{1,0:T(8,128)(2,1)S(1)}, bf16[32,4096]{1,0:T(8,128)(2,1)S(1)}, u32[]{:S(2)}, u32[]{:S(2)}) collective-permute-start(bf16[32,4096]{1,0:T(8,128)(2,1)S(1)} %get-tuple-element.24.skipped), channel_id=1, source_target_pairs={{0,6},{1,7},{2,4},{3,5},{4,2},{5,3},{6,0},{7,1},{8,14},{9,15},{10,... | collective-permute-start | bytes 786440 | tf_op jit(solution)/shard_map/ppermute | solution.py:296
  11.4 1.1 %shard_map.49 = (bf16[1,64,2048]{2,1,0:T(8,128)(2,1)S(1)}, bf16[1,64,2048]{2,1,0:T(8,128)(2,1)S(1)}, bf16[1,64,2048]{2,1,0:T(8,128)(2,1)S(1)}, bf16[1,64,2048]{2,1,0:T(8,128)(2,1)S(1)}) custom-call(bf16[256,384]{1,0:T(8,128)(2,1)S(1)} %get-tuple-element.25.turned_ref, bf16[6,64,4096]{2,1,0:T(8,128)(2,1)S(1)} %get-tuple-element.22.tiles_ref, ...), custom_call_target="tpu_custom_call" | custom-call | flops 402653184 | bytes 4194304 | tf_op jit(solution)/shard_map/pallas_call | solution.py:183
  12.5 0.1 collective-permute-start.4
  12.5 2.9 %collective-permute-start.5 = (bf16[1,64,2048]{2,1,0:T(8,128)(2,1)S(1)}, bf16[1,64,2048]{2,1,0:T(8,128)(2,1)S(1)}, u32[]{:S(2)}, u32[]{:S(2)}) collective-permute-start(bf16[1,64,2048]{2,1,0:T(8,128)(2,1)S(1)} %get-tuple-element.28), channel_id=1, source_target_pairs={{0,3},{1,2},{2,1},{3,0},{4,7},{5,6},{6,5},{7,4},{8,11},{9,10},{10,... | collective-permute-start | bytes 786440 | tf_op jit(solution)/shard_map/ppermute | solution.py:296
  15.5 0.5 collective-permute-start.6
  16.0 1.0 %shard_map.51 = (bf16[1,64,2048]{2,1,0:T(8,128)(2,1)S(1)}, bf16[1,64,2048]{2,1,0:T(8,128)(2,1)S(1)}, bf16[1,64,2048]{2,1,0:T(8,128)(2,1)S(1)}) custom-call(bf16[256,384]{1,0:T(8,128)(2,1)S(1)} %get-tuple-element.25.turned_ref, bf16[6,64,4096]{2,1,0:T(8,128)(2,1)S(1)} %get-tuple-element.22.tiles_ref, bf16[1,64,2048]{2,1,0:T(8,128)(2,1)S(1)} %get-tuple-element.26.refs_1_.skipped), custom_call_target="tpu_custom_call" | custom-call | flops 301989888 | bytes 3932160 | tf_op jit(solution)/shard_map/pallas_call | solution.py:183
  17.1 0.4 collective-permute-start.7
  17.5 1.3 %collective-permute-done.3.rows_ref = bf16[32,4096]{1,0:T(8,128)(2,1)S(1)} collective-permute-done((bf16[32,4096]{1,0:T(8,128)(2,1)S(1)}, bf16[32,4096]{1,0:T(8,128)(2,1)S(1)}, u32[]{:S(2)}, u32[]{:S(2)}) %collective-permute-start.3) | collective-permute-done | bytes 262176 | tf_op jit(solution)/shard_map/ppermute | solution.py:296
  18.8 6.3 %collective-permute-start.8 = (bf16[1,64,2048]{2,1,0:T(8,128)(2,1)S(1)}, bf16[1,64,2048]{2,1,0:T(8,128)(2,1)S(1)}, u32[]{:S(2)}, u32[]{:S(2)}) collective-permute-start(bf16[1,64,2048]{2,1,0:T(8,128)(2,1)S(1)} %get-tuple-element.32), channel_id=1, source_target_pairs={{0,4},{1,5},{2,6},{3,7},{4,0},{5,1},{6,2},{7,3},{8,12},{9,13},{10,... | collective-permute-start | bytes 786440 | tf_op jit(solution)/shard_map/ppermute | solution.py:296
  25.1 5.6 %collective-permute-done.4.refs_2_ = bf16[1,64,2048]{2,1,0:T(8,128)(2,1)S(1)} collective-permute-done((bf16[1,64,2048]{2,1,0:T(8,128)(2,1)S(1)}, bf16[1,64,2048]{2,1,0:T(8,128)(2,1)S(1)}, u32[]{:S(2)}, u32[]{:S(2)}) %collective-permute-start.4) | collective-permute-done | bytes 262176 | tf_op jit(solution)/shard_map/ppermute | solution.py:296
  30.7 5.3 %collective-permute-start.9 = (bf16[1,64,2048]{2,1,0:T(8,128)(2,1)S(1)}, bf16[1,64,2048]{2,1,0:T(8,128)(2,1)S(1)}, u32[]{:S(2)}, u32[]{:S(2)}) collective-permute-start(bf16[1,64,2048]{2,1,0:T(8,128)(2,1)S(1)} %get-tuple-element.33), channel_id=1, source_target_pairs={{0,7},{1,6},{2,5},{3,4},{4,3},{5,2},{6,1},{7,0},{8,15},{9,14},{10,... | collective-permute-start | bytes 786440 | tf_op jit(solution)/shard_map/ppermute | solution.py:296
  36.0 0.3 shard_map.48.refs_0_
  36.4 1.8 %collective-permute-done.5.refs_3_ = bf16[1,64,2048]{2,1,0:T(8,128)(2,1)S(1)} collective-permute-done((bf16[1,64,2048]{2,1,0:T(8,128)(2,1)S(1)}, bf16[1,64,2048]{2,1,0:T(8,128)(2,1)S(1)}, u32[]{:S(2)}, u32[]{:S(2)}) %collective-permute-start.5) | collective-permute-done | bytes 262176 | tf_op jit(solution)/shard_map/ppermute | solution.py:296
  38.2 0.0 collective-permute-done.6.refs_4_
  38.2 0.7 shard_map.50
  38.9 0.0 collective-permute-done.7.refs_5_
  39.0 12.7 %collective-permute-done.8.refs_6_ = bf16[1,64,2048]{2,1,0:T(8,128)(2,1)S(1)} collective-permute-done((bf16[1,64,2048]{2,1,0:T(8,128)(2,1)S(1)}, bf16[1,64,2048]{2,1,0:T(8,128)(2,1)S(1)}, u32[]{:S(2)}, u32[]{:S(2)}) %collective-permute-start.8) | collective-permute-done | bytes 262176 | tf_op jit(solution)/shard_map/ppermute | solution.py:296
  51.7 0.0 collective-permute-done.9.refs_7_
  51.7 0.9 %shard_map.52 = (f32[8,32,256]{2,1,0:T(8,128)S(1)}, bf16[256,2048]{1,0:T(8,128)(2,1)S(1)}) custom-call(f32[256,2048]{1,0:T(8,128)S(1)} %get-tuple-element.30.fitted_ref, bf16[1,64,2048]{2,1,0:T(8,128)(2,1)S(1)} %shard_map.48.refs_0_, bf16[1,64,2048]{2,1,0:T(8,128)(2,1)S(1)} %get-tuple-element.26.refs_1_.skipped, ...), custom_call_target="tpu_custom_call" | custom-call | flops 536870912 | bytes 2097152 | tf_op jit(solution)/shard_map/pallas_call | solution.py:274
  52.6 0.1 collective-permute-start.10
  52.6 0.5 shard_map.53
  53.1 1.0 %collective-permute-done.10 = f32[8,32,256]{2,1,0:T(8,128)S(1)} collective-permute-done((f32[8,32,256]{2,1,0:T(8,128)S(1)}, f32[8,32,256]{2,1,0:T(8,128)S(1)}, u32[]{:S(2)}, u32[]{:S(2)}) %collective-permute-start.10) | collective-permute-done | bytes 262176 | tf_op jit(solution)/shard_map/ppermute | solution.py:296
  54.3 16.5 %all_to_all.5 = f16[8,40,256]{2,1,0:T(8,128)(2,1)S(1)} all-to-all(f16[8,40,256]{2,1,0:T(8,128)(2,1)S(1)} %pad_maximum_fusion), channel_id=1, replica_groups=mesh['rep'=4,'grid'=8] {'grid'}, dimensions={0} | all-to-all | bytes 327680 | tf_op jit(solution)/shard_map/all_to_all | solution.py:305
  71.0 1.3 %collective-permute-start.13 = (f32[32,256]{1,0:T(8,128)S(1)}, f32[32,256]{1,0:T(8,128)S(1)}, u32[]{:S(2)}, u32[]{:S(2)}) collective-permute-start(f32[32,256]{1,0:T(8,128)S(1)} %fusion), channel_id=1, source_target_pairs={{0,16},{8,24},{16,0},{24,8},{1,17},{9,25},{17,1},{25,9},{2,18},{10... | collective-permute-start | bytes 98312 | tf_op jit(solution)/shard_map/ppermute | solution.py:296
  72.2 0.0 collective-permute-start.12
  72.3 0.9 %collective-permute-start.11 = (f32[32,256]{1,0:T(8,128)S(1)}, f32[32,256]{1,0:T(8,128)S(1)}, u32[]{:S(2)}, u32[]{:S(2)}) collective-permute-start(f32[32,256]{1,0:T(8,128)S(1)} %fusion), channel_id=1, source_target_pairs={{0,8},{8,0},{16,24},{24,16},{1,9},{9,1},{17,25},{25,17},{2,10},{10... | collective-permute-start | bytes 98312 | tf_op jit(solution)/shard_map/ppermute | solution.py:296
  73.2 1.8 %collective-permute-done.13 = f32[32,256]{1,0:T(8,128)S(1)} collective-permute-done((f32[32,256]{1,0:T(8,128)S(1)}, f32[32,256]{1,0:T(8,128)S(1)}, u32[]{:S(2)}, u32[]{:S(2)}) %collective-permute-start.13) | collective-permute-done | bytes 32800 | tf_op jit(solution)/shard_map/ppermute | solution.py:296
  75.0 0.7 collective-permute-done.12
  75.7 0.0 collective-permute-done.11
  75.7 0.6 pad_maximum_fusion.1
  (10 shorter events, 0.2 us)
Async XLA Ops:
  0.0 6.9 %copy-start = (bf16[128,256]{1,0:T(8,128)(2,1)S(1)}, bf16[128,256]{1,0:T(8,128)(2,1)}, u32[]{:S(2)}) copy-start(bf16[128,256]{1,0:T(8,128)(2,1)} %refs_0_.1) | copy-start | bytes 196612
  0.0 5.7 %collective-permute-start.1 = (bf16[128,256]{1,0:T(8,128)(2,1)}, bf16[128,256]{1,0:T(8,128)(2,1)S(1)}, u32[]{:S(2)}, u32[]{:S(2)}) collective-permute-start(bf16[128,256]{1,0:T(8,128)(2,1)} %refs_0_.1), channel_id=1, source_target_pairs={{0,16},{8,24},{16,0},{24,8},{1,17},{9,25},{17,1},{25,9},{2,18},{10... | collective-permute-start | bytes 196616 | tf_op jit(solution)/shard_map/ppermute | solution.py:296
  3.0 2.8 %collective-permute-start = (bf16[128,256]{1,0:T(8,128)(2,1)}, bf16[128,256]{1,0:T(8,128)(2,1)S(1)}, u32[]{:S(2)}, u32[]{:S(2)}) collective-permute-start(bf16[128,256]{1,0:T(8,128)(2,1)} %refs_0_.1), channel_id=1, source_target_pairs={{0,8},{8,0},{16,24},{24,16},{1,9},{9,1},{17,25},{25,17},{2,10},{10... | collective-permute-start | bytes 196616 | tf_op jit(solution)/shard_map/ppermute | solution.py:296
  3.0 4.0 %collective-permute-start.2 = (bf16[128,256]{1,0:T(8,128)(2,1)}, bf16[128,256]{1,0:T(8,128)(2,1)S(1)}, u32[]{:S(2)}, u32[]{:S(2)}) collective-permute-start(bf16[128,256]{1,0:T(8,128)(2,1)} %refs_0_.1), channel_id=1, source_target_pairs={{0,24},{8,16},{16,8},{24,0},{1,25},{9,17},{17,9},{25,1},{2,26},{10... | collective-permute-start | bytes 196616 | tf_op jit(solution)/shard_map/ppermute | solution.py:296
  7.8 11.0 %collective-permute-start.3 = (bf16[32,4096]{1,0:T(8,128)(2,1)S(1)}, bf16[32,4096]{1,0:T(8,128)(2,1)S(1)}, u32[]{:S(2)}, u32[]{:S(2)}) collective-permute-start(bf16[32,4096]{1,0:T(8,128)(2,1)S(1)} %get-tuple-element.24.skipped), channel_id=1, source_target_pairs={{0,6},{1,7},{2,4},{3,5},{4,2},{5,3},{6,0},{7,1},{8,14},{9,15},{10,... | collective-permute-start | bytes 786440 | tf_op jit(solution)/shard_map/ppermute | solution.py:296
  12.5 18.3 %collective-permute-start.4 = (bf16[1,64,2048]{2,1,0:T(8,128)(2,1)S(1)}, bf16[1,64,2048]{2,1,0:T(8,128)(2,1)S(1)}, u32[]{:S(2)}, u32[]{:S(2)}) collective-permute-start(bf16[1,64,2048]{2,1,0:T(8,128)(2,1)S(1)} %get-tuple-element.27), channel_id=1, source_target_pairs={{0,2},{1,3},{2,0},{3,1},{4,6},{5,7},{6,4},{7,5},{8,10},{9,11},{10,... | collective-permute-start | bytes 786440 | tf_op jit(solution)/shard_map/ppermute | solution.py:296
  12.5 25.7 %collective-permute-start.5 = (bf16[1,64,2048]{2,1,0:T(8,128)(2,1)S(1)}, bf16[1,64,2048]{2,1,0:T(8,128)(2,1)S(1)}, u32[]{:S(2)}, u32[]{:S(2)}) collective-permute-start(bf16[1,64,2048]{2,1,0:T(8,128)(2,1)S(1)} %get-tuple-element.28), channel_id=1, source_target_pairs={{0,3},{1,2},{2,1},{3,0},{4,7},{5,6},{6,5},{7,4},{8,11},{9,10},{10,... | collective-permute-start | bytes 786440 | tf_op jit(solution)/shard_map/ppermute | solution.py:296
  15.5 22.7 %collective-permute-start.6 = (bf16[1,64,2048]{2,1,0:T(8,128)(2,1)S(1)}, bf16[1,64,2048]{2,1,0:T(8,128)(2,1)S(1)}, u32[]{:S(2)}, u32[]{:S(2)}) collective-permute-start(bf16[1,64,2048]{2,1,0:T(8,128)(2,1)S(1)} %get-tuple-element.29), channel_id=1, source_target_pairs={{0,1},{1,0},{2,3},{3,2},{4,5},{5,4},{6,7},{7,6},{8,9},{9,8},{10,11... | collective-permute-start | bytes 786440 | tf_op jit(solution)/shard_map/ppermute | solution.py:296
  17.1 21.9 %collective-permute-start.7 = (bf16[1,64,2048]{2,1,0:T(8,128)(2,1)S(1)}, bf16[1,64,2048]{2,1,0:T(8,128)(2,1)S(1)}, u32[]{:S(2)}, u32[]{:S(2)}) collective-permute-start(bf16[1,64,2048]{2,1,0:T(8,128)(2,1)S(1)} %get-tuple-element.31), channel_id=1, source_target_pairs={{0,5},{1,4},{2,7},{3,6},{4,1},{5,0},{6,3},{7,2},{8,13},{9,12},{10,... | collective-permute-start | bytes 786440 | tf_op jit(solution)/shard_map/ppermute | solution.py:296
  18.8 32.9 %collective-permute-start.8 = (bf16[1,64,2048]{2,1,0:T(8,128)(2,1)S(1)}, bf16[1,64,2048]{2,1,0:T(8,128)(2,1)S(1)}, u32[]{:S(2)}, u32[]{:S(2)}) collective-permute-start(bf16[1,64,2048]{2,1,0:T(8,128)(2,1)S(1)} %get-tuple-element.32), channel_id=1, source_target_pairs={{0,4},{1,5},{2,6},{3,7},{4,0},{5,1},{6,2},{7,3},{8,12},{9,13},{10,... | collective-permute-start | bytes 786440 | tf_op jit(solution)/shard_map/ppermute | solution.py:296
  30.7 20.9 %collective-permute-start.9 = (bf16[1,64,2048]{2,1,0:T(8,128)(2,1)S(1)}, bf16[1,64,2048]{2,1,0:T(8,128)(2,1)S(1)}, u32[]{:S(2)}, u32[]{:S(2)}) collective-permute-start(bf16[1,64,2048]{2,1,0:T(8,128)(2,1)S(1)} %get-tuple-element.33), channel_id=1, source_target_pairs={{0,7},{1,6},{2,5},{3,4},{4,3},{5,2},{6,1},{7,0},{8,15},{9,14},{10,... | collective-permute-start | bytes 786440 | tf_op jit(solution)/shard_map/ppermute | solution.py:296
  52.6 1.6 %collective-permute-start.10 = (f32[8,32,256]{2,1,0:T(8,128)S(1)}, f32[8,32,256]{2,1,0:T(8,128)S(1)}, u32[]{:S(2)}, u32[]{:S(2)}) collective-permute-start(f32[8,32,256]{2,1,0:T(8,128)S(1)} %get-tuple-element.36), channel_id=1, source_target_pairs={{0,8},{8,0},{16,24},{24,16},{1,9},{9,1},{17,25},{25,17},{2,10},{10... | collective-permute-start | bytes 786440 | tf_op jit(solution)/shard_map/ppermute | solution.py:296
  71.0 4.0 %collective-permute-start.13 = (f32[32,256]{1,0:T(8,128)S(1)}, f32[32,256]{1,0:T(8,128)S(1)}, u32[]{:S(2)}, u32[]{:S(2)}) collective-permute-start(f32[32,256]{1,0:T(8,128)S(1)} %fusion), channel_id=1, source_target_pairs={{0,16},{8,24},{16,0},{24,8},{1,17},{9,25},{17,1},{25,9},{2,18},{10... | collective-permute-start | bytes 98312 | tf_op jit(solution)/shard_map/ppermute | solution.py:296
  72.2 3.4 %collective-permute-start.12 = (f32[32,256]{1,0:T(8,128)S(1)}, f32[32,256]{1,0:T(8,128)S(1)}, u32[]{:S(2)}, u32[]{:S(2)}) collective-permute-start(f32[32,256]{1,0:T(8,128)S(1)} %fusion), channel_id=1, source_target_pairs={{0,24},{8,16},{16,8},{24,0},{1,25},{9,17},{17,9},{25,1},{2,26},{10... | collective-permute-start | bytes 98312 | tf_op jit(solution)/shard_map/ppermute | solution.py:296
  72.3 3.4 %collective-permute-start.11 = (f32[32,256]{1,0:T(8,128)S(1)}, f32[32,256]{1,0:T(8,128)S(1)}, u32[]{:S(2)}, u32[]{:S(2)}) collective-permute-start(f32[32,256]{1,0:T(8,128)S(1)} %fusion), channel_id=1, source_target_pairs={{0,8},{8,0},{16,24},{24,16},{1,9},{9,1},{17,25},{25,17},{2,10},{10... | collective-permute-start | bytes 98312 | tf_op jit(solution)/shard_map/ppermute | solution.py:296

commit v9 on v7

--- a/solution.py
+++ b/solution.py
@@ -319,26 +319,34 @@
     inside, block = load(tiles, tile_count, tile_block)
     per_part = half // grid_size
     if per_part == SUB and grid_size == 8 and rep_size == 4:
-        near_size = grid_size // 2
         parts = [orbitals] + [swapped(orbitals, "rep", k) for k in range(1, rep_size)]
-
-        def ids(ks):
+        layers = grid_size // 2
+
+        def target(at, move, sign=1):
+            return (at // 2 + sign * move[0] + layers) % layers * 2 + (at % 2 ^ move[1])
+
+        def ids(moves, sign):
             def blocks():
                 me = lax.axis_index("grid")
-                return [me ^ k for k in ks]
+                return [target(me, move, sign) for move in moves]
 
             return blocks
 
-        def starts(ks):
-            return lambda: [b * SUB for b in ids(ks)()]
+        def starts(moves):
+            return lambda: [b * SUB for b in ids(moves, 1)()]
 
         def own_output(s, k):
             return s, 0, k
 
-        def shapes(ks):
-            return [(1, width, cols)] * len(ks)
-
-        waves, late_ks = [[6], [0, 2, 3, 1], [5, 4, 7]], [5, 4, 7]
+        def shapes(moves):
+            return [(1, width, cols)] * len(moves)
+
+        def moved(x, move):
+            if move == (0, 0):
+                return x
+            return lax.ppermute(x, "grid", [(i, target(i, move)) for i in range(grid_size)])
+
+        waves, late_moves = [[(1, 0)], [(0, 0), (0, 1), (3, 0), (2, 1)], [(2, 0), (1, 1), (3, 1)]], [(2, 0), (1, 1), (3, 1)]
         full, turned, made = contract_first(
             starts(waves[0]), None, [(2 * SUB, tiles.shape[4])], block, inside, parts, plain=True
         )
@@ -346,11 +354,11 @@
         for wave in waves[1:]:
             made = contract_next(starts(wave), own_output, shapes(wave), turned, inside, made[0])
             sent.update(zip(wave, made))
-        received = {k: swapped(sent[k], "grid", k) if k else sent[k] for wave in waves for k in wave}
+        received = {move: moved(sent[move], move) for move in sent}
         received[waves[0][0]] = arranged(received[waves[0][0]], width)
-        early_ks = [k for wave in waves for k in wave if k not in late_ks]
-        early, late = [received[k] for k in early_ks], [received[k] for k in late_ks]
-        early_ids, late_ids, all_ids = ids(early_ks), ids(late_ks), ids(early_ks + late_ks)
+        early_moves = [move for move in received if move not in late_moves]
+        early, late = [received[move] for move in early_moves], [received[move] for move in late_moves]
+        early_ids, late_ids, all_ids = ids(early_moves, -1), ids(late_moves, -1), ids(early_moves + late_moves, -1)
     else:
         def place(s, k):
             part, col = divmod(s * SUB + k, per_part)

time: 76.5 us -> 76.5 us (level)
  starting transfers between devices: 24.7 us -> 30 us
  blocking collectives: 16.5 us -> 12.4 us
  waiting for transfers between devices: 26.1 us -> 24.9 us
    ppermute x0 -> x7, starting transfers between devices: none -> 24.6 us  [moved(): lax.ppermute(x, 'grid', [(i, target(i, move)) for i in range(grid_size)])]
    ppermute x14 -> x7, waiting for transfers between devices: 26.1 us -> 4.7 us  [swapped(): lax.ppermute(x, axis, [(i, i ^ k) for i in range(lax.axis_size(axis))])]
    ppermute x0 -> x7, waiting for transfers between devices: none -> 20.2 us  [moved(): lax.ppermute(x, 'grid', [(i, target(i, move)) for i in range(grid_size)])]
    ppermute x14 -> x7, starting transfers between devices: 24.7 us -> 5.44 us  [swapped(): lax.ppermute(x, axis, [(i, i ^ k) for i in range(lax.axis_size(axis))])]
    all_to_all x1, blocking collectives: 16.5 us -> 12.4 us  [summed_blocks(): lax.all_to_all(jnp.concatenate([scaled, tail], axis=1), axis, 0, 0, tiled...]
where the time goes in v9:
time: 76.5 us; the launch traced here: 76.3 us
  starting transfers between devices  30 us (39%)
  waiting for transfers between devices  24.9 us (33%)
  blocking collectives  12.4 us (16%)
  Pallas kernels  7.27 us (10%)
  other arithmetic  0.84 us (1%)
  between operations  0.81 us (1%)
    ppermute x7, starting transfers between devices, moved(): lax.ppermute(x, 'grid', [(i, target(i, move)) for i in range(grid_size)])  24.6 us
    ppermute x7, waiting for transfers between devices, moved(): lax.ppermute(x, 'grid', [(i, target(i, move)) for i in range(grid_size)])  20.2 us
    all_to_all x1, blocking collectives, summed_blocks(): lax.all_to_all(jnp.concatenate([scaled, tail], axis=1), axis, 0, 0, tiled...  12.4 us
    ppermute x7, starting transfers between devices, swapped(): lax.ppermute(x, axis, [(i, i ^ k) for i in range(lax.axis_size(axis))])  5.44 us
    ppermute x7, waiting for transfers between devices, swapped(): lax.ppermute(x, axis, [(i, i ^ k) for i in range(lax.axis_size(axis))])  4.7 us
    pallas_call x2, Pallas kernels, contract_next(): pl.pallas_call(functools.partial(next_kernel, group_starts, place), out_s...  2.1 us
    pallas_call x1, Pallas kernels, load(): pl.pallas_call(load_kernel, out_shape=[jax.ShapeDtypeStruct(tiles.shape[2...  1.91 us
  transfers between devices with their start and end apart: 14, of which 8 were waited for; matrix products, arithmetic and copies ran while one was open for 0% of the time, Pallas kernels for 7%

profile of v9, /device:TPU:0, one launch (start us, length us, event | category | flops | bytes accessed | tf_op | source)
XLA Modules:
  0.0 76.3 jit_solution(14551391315585829951)
XLA Ops:
  0.0 0.0 copy-start
  0.0 3.0 %collective-permute-start.1 = (bf16[128,256]{1,0:T(8,128)(2,1)}, bf16[128,256]{1,0:T(8,128)(2,1)S(1)}, u32[]{:S(2)}, u32[]{:S(2)}) collective-permute-start(bf16[128,256]{1,0:T(8,128)(2,1)} %refs_0_.1), channel_id=1, source_target_pairs={{0,16},{8,24},{16,0},{24,8},{1,17},{9,25},{17,1},{25,9},{2,18},{10... | collective-permute-start | bytes 196616 | tf_op jit(solution)/shard_map/ppermute | solution.py:296
  3.0 0.0 collective-permute-start
  3.0 0.2 collective-permute-start.2
  3.8 1.9 %shard_map.46 = (bf16[6,64,4096]{2,1,0:T(8,128)(2,1)S(1)}, s32[1,6]{1,0:T(1,128)S(1)}) custom-call(s32[1,1]{1,0:T(1,128)S(6)} %copy.8.count_ref, s32[1,1,6]{2,1,0:T(1,128)} %block_hbm.1, bf16[1,1,6,64,4096]{4,3,2,1,0:T(8,128)(2,1)} %tiles_hbm.1), custom_call_target="tpu_custom_call" | custom-call | bytes 3145728 | tf_op jit(solution)/shard_map/pallas_call | solution.py:41
  5.7 0.0 collective-permute-done.1.refs_2_
  5.7 0.0 collective-permute-done.refs_1_
  5.8 1.2 %collective-permute-done.2.refs_3_ = bf16[128,256]{1,0:T(8,128)(2,1)S(1)} collective-permute-done((bf16[128,256]{1,0:T(8,128)(2,1)}, bf16[128,256]{1,0:T(8,128)(2,1)S(1)}, u32[]{:S(2)}, u32[]{:S(2)}) %collective-permute-start.2) | collective-permute-done | bytes 65568 | tf_op jit(solution)/shard_map/ppermute | solution.py:296
  6.9 0.0 copy-done
  6.9 0.8 %shard_map.47 = (bf16[512,256]{1,0:T(8,128)(2,1)S(1)}, bf16[256,384]{1,0:T(8,128)(2,1)S(1)}, bf16[32,4096]{1,0:T(8,128)(2,1)S(1)}) custom-call(s32[1,6]{1,0:T(1,128)S(1)} %get-tuple-element.21.block_ref, bf16[6,64,4096]{2,1,0:T(8,128)(2,1)S(1)} %get-tuple-element.22.tiles_ref, bf16[128,256]{1,0:T(8,128)(2,1)S(1)} %copy-done, ...), custom_call_target="tpu_custom_call" | custom-call | flops 100663296 | bytes 3407872 | tf_op jit(solution)/shard_map/pallas_call | solution.py:170
  7.8 1.6 %collective-permute-start.3 = (bf16[32,4096]{1,0:T(8,128)(2,1)S(1)}, bf16[32,4096]{1,0:T(8,128)(2,1)S(1)}, u32[]{:S(2)}, u32[]{:S(2)}) collective-permute-start(bf16[32,4096]{1,0:T(8,128)(2,1)S(1)} %get-tuple-element.24.skipped), channel_id=1, source_target_pairs={{0,2},{1,3},{2,4},{3,5},{4,6},{5,7},{6,0},{7,1},{8,10},{9,11},{10,... | collective-permute-start | bytes 786440 | tf_op jit(solution)/shard_map/ppermute | solution.py:347
  9.4 1.0 %shard_map.49 = (bf16[1,64,2048]{2,1,0:T(8,128)(2,1)S(1)}, bf16[1,64,2048]{2,1,0:T(8,128)(2,1)S(1)}, bf16[1,64,2048]{2,1,0:T(8,128)(2,1)S(1)}, bf16[1,64,2048]{2,1,0:T(8,128)(2,1)S(1)}) custom-call(bf16[256,384]{1,0:T(8,128)(2,1)S(1)} %get-tuple-element.25.turned_ref, bf16[6,64,4096]{2,1,0:T(8,128)(2,1)S(1)} %get-tuple-element.22.tiles_ref, ...), custom_call_target="tpu_custom_call" | custom-call | flops 402653184 | bytes 4194304 | tf_op jit(solution)/shard_map/pallas_call | solution.py:183
  10.4 1.5 %collective-permute-start.4 = (bf16[1,64,2048]{2,1,0:T(8,128)(2,1)S(1)}, bf16[1,64,2048]{2,1,0:T(8,128)(2,1)S(1)}, u32[]{:S(2)}, u32[]{:S(2)}) collective-permute-start(bf16[1,64,2048]{2,1,0:T(8,128)(2,1)S(1)} %get-tuple-element.27), channel_id=1, source_target_pairs={{0,1},{1,0},{2,3},{3,2},{4,5},{5,4},{6,7},{7,6},{8,9},{9,8},{10,11... | collective-permute-start | bytes 786440 | tf_op jit(solution)/shard_map/ppermute | solution.py:347
  12.0 2.3 %collective-permute-start.5 = (bf16[1,64,2048]{2,1,0:T(8,128)(2,1)S(1)}, bf16[1,64,2048]{2,1,0:T(8,128)(2,1)S(1)}, u32[]{:S(2)}, u32[]{:S(2)}) collective-permute-start(bf16[1,64,2048]{2,1,0:T(8,128)(2,1)S(1)} %get-tuple-element.28), channel_id=1, source_target_pairs={{0,6},{1,7},{2,0},{3,1},{4,2},{5,3},{6,4},{7,5},{8,14},{9,15},{10,... | collective-permute-start | bytes 786440 | tf_op jit(solution)/shard_map/ppermute | solution.py:347
  14.2 0.7 collective-permute-start.6
  15.0 1.0 %shard_map.51 = (bf16[1,64,2048]{2,1,0:T(8,128)(2,1)S(1)}, bf16[1,64,2048]{2,1,0:T(8,128)(2,1)S(1)}, bf16[1,64,2048]{2,1,0:T(8,128)(2,1)S(1)}) custom-call(bf16[256,384]{1,0:T(8,128)(2,1)S(1)} %get-tuple-element.25.turned_ref, bf16[6,64,4096]{2,1,0:T(8,128)(2,1)S(1)} %get-tuple-element.22.tiles_ref, bf16[1,64,2048]{2,1,0:T(8,128)(2,1)S(1)} %get-tuple-element.26.refs_1_.skipped), custom_call_target="tpu_custom_call" | custom-call | flops 301989888 | bytes 3932160 | tf_op jit(solution)/shard_map/pallas_call | solution.py:183
  16.0 2.2 %collective-permute-start.7 = (bf16[1,64,2048]{2,1,0:T(8,128)(2,1)S(1)}, bf16[1,64,2048]{2,1,0:T(8,128)(2,1)S(1)}, u32[]{:S(2)}, u32[]{:S(2)}) collective-permute-start(bf16[1,64,2048]{2,1,0:T(8,128)(2,1)S(1)} %get-tuple-element.31), channel_id=1, source_target_pairs={{0,4},{1,5},{2,6},{3,7},{4,0},{5,1},{6,2},{7,3},{8,12},{9,13},{10,... | collective-permute-start | bytes 786440 | tf_op jit(solution)/shard_map/ppermute | solution.py:347
  18.2 0.5 collective-permute-done.3.rows_ref
  18.7 16.2 %collective-permute-start.8 = (bf16[1,64,2048]{2,1,0:T(8,128)(2,1)S(1)}, bf16[1,64,2048]{2,1,0:T(8,128)(2,1)S(1)}, u32[]{:S(2)}, u32[]{:S(2)}) collective-permute-start(bf16[1,64,2048]{2,1,0:T(8,128)(2,1)S(1)} %get-tuple-element.32), channel_id=1, source_target_pairs={{0,3},{1,2},{2,5},{3,4},{4,7},{5,6},{6,1},{7,0},{8,11},{9,10},{10,... | collective-permute-start | bytes 786440 | tf_op jit(solution)/shard_map/ppermute | solution.py:347
  34.9 0.0 collective-permute-done.4.refs_2_
  34.9 0.0 collective-permute-start.9
  34.9 0.3 shard_map.48.refs_0_
  35.3 0.0 collective-permute-done.5.refs_3_
  35.3 12.3 %collective-permute-done.6.refs_4_ = bf16[1,64,2048]{2,1,0:T(8,128)(2,1)S(1)} collective-permute-done((bf16[1,64,2048]{2,1,0:T(8,128)(2,1)S(1)}, bf16[1,64,2048]{2,1,0:T(8,128)(2,1)S(1)}, u32[]{:S(2)}, u32[]{:S(2)}) %collective-permute-start.6) | collective-permute-done | bytes 262176 | tf_op jit(solution)/shard_map/ppermute | solution.py:347
  47.5 0.7 shard_map.50
  48.3 3.9 %collective-permute-done.7.refs_5_ = bf16[1,64,2048]{2,1,0:T(8,128)(2,1)S(1)} collective-permute-done((bf16[1,64,2048]{2,1,0:T(8,128)(2,1)S(1)}, bf16[1,64,2048]{2,1,0:T(8,128)(2,1)S(1)}, u32[]{:S(2)}, u32[]{:S(2)}) %collective-permute-start.7) | collective-permute-done | bytes 262176 | tf_op jit(solution)/shard_map/ppermute | solution.py:347
  52.2 0.0 collective-permute-done.8.refs_6_
  52.2 3.6 %collective-permute-done.9.refs_7_ = bf16[1,64,2048]{2,1,0:T(8,128)(2,1)S(1)} collective-permute-done((bf16[1,64,2048]{2,1,0:T(8,128)(2,1)S(1)}, bf16[1,64,2048]{2,1,0:T(8,128)(2,1)S(1)}, u32[]{:S(2)}, u32[]{:S(2)}) %collective-permute-start.9) | collective-permute-done | bytes 262176 | tf_op jit(solution)/shard_map/ppermute | solution.py:347
  55.8 0.9 %shard_map.52 = (f32[8,32,256]{2,1,0:T(8,128)S(1)}, bf16[256,2048]{1,0:T(8,128)(2,1)S(1)}) custom-call(f32[256,2048]{1,0:T(8,128)S(1)} %get-tuple-element.30.fitted_ref, bf16[1,64,2048]{2,1,0:T(8,128)(2,1)S(1)} %shard_map.48.refs_0_, bf16[1,64,2048]{2,1,0:T(8,128)(2,1)S(1)} %get-tuple-element.26.refs_1_.skipped, ...), custom_call_target="tpu_custom_call" | custom-call | flops 536870912 | bytes 2097152 | tf_op jit(solution)/shard_map/pallas_call | solution.py:274
  56.7 0.1 collective-permute-start.10
  56.7 0.5 shard_map.53
  57.2 1.0 %collective-permute-done.10 = f32[8,32,256]{2,1,0:T(8,128)S(1)} collective-permute-done((f32[8,32,256]{2,1,0:T(8,128)S(1)}, f32[8,32,256]{2,1,0:T(8,128)S(1)}, u32[]{:S(2)}, u32[]{:S(2)}) %collective-permute-start.10) | collective-permute-done | bytes 262176 | tf_op jit(solution)/shard_map/ppermute | solution.py:296
  58.4 12.4 %all_to_all.5 = f16[8,40,256]{2,1,0:T(8,128)(2,1)S(1)} all-to-all(f16[8,40,256]{2,1,0:T(8,128)(2,1)S(1)} %pad_maximum_fusion), channel_id=1, replica_groups=mesh['rep'=4,'grid'=8] {'grid'}, dimensions={0} | all-to-all | bytes 327680 | tf_op jit(solution)/shard_map/all_to_all | solution.py:305
  71.0 1.3 %collective-permute-start.13 = (f32[32,256]{1,0:T(8,128)S(1)}, f32[32,256]{1,0:T(8,128)S(1)}, u32[]{:S(2)}, u32[]{:S(2)}) collective-permute-start(f32[32,256]{1,0:T(8,128)S(1)} %fusion), channel_id=1, source_target_pairs={{0,16},{8,24},{16,0},{24,8},{1,17},{9,25},{17,1},{25,9},{2,18},{10... | collective-permute-start | bytes 98312 | tf_op jit(solution)/shard_map/ppermute | solution.py:296
  72.2 0.0 collective-permute-start.12
  72.2 0.9 %collective-permute-start.11 = (f32[32,256]{1,0:T(8,128)S(1)}, f32[32,256]{1,0:T(8,128)S(1)}, u32[]{:S(2)}, u32[]{:S(2)}) collective-permute-start(f32[32,256]{1,0:T(8,128)S(1)} %fusion), channel_id=1, source_target_pairs={{0,8},{8,0},{16,24},{24,16},{1,9},{9,1},{17,25},{25,17},{2,10},{10... | collective-permute-start | bytes 98312 | tf_op jit(solution)/shard_map/ppermute | solution.py:296
  73.2 1.8 %collective-permute-done.13 = f32[32,256]{1,0:T(8,128)S(1)} collective-permute-done((f32[32,256]{1,0:T(8,128)S(1)}, f32[32,256]{1,0:T(8,128)S(1)}, u32[]{:S(2)}, u32[]{:S(2)}) %collective-permute-start.13) | collective-permute-done | bytes 32800 | tf_op jit(solution)/shard_map/ppermute | solution.py:296
  74.9 0.7 collective-permute-done.12
  75.6 0.0 collective-permute-done.11
  75.7 0.6 pad_maximum_fusion.1
  (10 shorter events, 0.2 us)
Async XLA Ops:
  0.0 6.9 %copy-start = (bf16[128,256]{1,0:T(8,128)(2,1)S(1)}, bf16[128,256]{1,0:T(8,128)(2,1)}, u32[]{:S(2)}) copy-start(bf16[128,256]{1,0:T(8,128)(2,1)} %refs_0_.1) | copy-start | bytes 196612
  0.0 5.7 %collective-permute-start.1 = (bf16[128,256]{1,0:T(8,128)(2,1)}, bf16[128,256]{1,0:T(8,128)(2,1)S(1)}, u32[]{:S(2)}, u32[]{:S(2)}) collective-permute-start(bf16[128,256]{1,0:T(8,128)(2,1)} %refs_0_.1), channel_id=1, source_target_pairs={{0,16},{8,24},{16,0},{24,8},{1,17},{9,25},{17,1},{25,9},{2,18},{10... | collective-permute-start | bytes 196616 | tf_op jit(solution)/shard_map/ppermute | solution.py:296
  3.0 2.8 %collective-permute-start = (bf16[128,256]{1,0:T(8,128)(2,1)}, bf16[128,256]{1,0:T(8,128)(2,1)S(1)}, u32[]{:S(2)}, u32[]{:S(2)}) collective-permute-start(bf16[128,256]{1,0:T(8,128)(2,1)} %refs_0_.1), channel_id=1, source_target_pairs={{0,8},{8,0},{16,24},{24,16},{1,9},{9,1},{17,25},{25,17},{2,10},{10... | collective-permute-start | bytes 196616 | tf_op jit(solution)/shard_map/ppermute | solution.py:296
  3.0 4.0 %collective-permute-start.2 = (bf16[128,256]{1,0:T(8,128)(2,1)}, bf16[128,256]{1,0:T(8,128)(2,1)S(1)}, u32[]{:S(2)}, u32[]{:S(2)}) collective-permute-start(bf16[128,256]{1,0:T(8,128)(2,1)} %refs_0_.1), channel_id=1, source_target_pairs={{0,24},{8,16},{16,8},{24,0},{1,25},{9,17},{17,9},{25,1},{2,26},{10... | collective-permute-start | bytes 196616 | tf_op jit(solution)/shard_map/ppermute | solution.py:296
  7.8 11.0 %collective-permute-start.3 = (bf16[32,4096]{1,0:T(8,128)(2,1)S(1)}, bf16[32,4096]{1,0:T(8,128)(2,1)S(1)}, u32[]{:S(2)}, u32[]{:S(2)}) collective-permute-start(bf16[32,4096]{1,0:T(8,128)(2,1)S(1)} %get-tuple-element.24.skipped), channel_id=1, source_target_pairs={{0,2},{1,3},{2,4},{3,5},{4,6},{5,7},{6,0},{7,1},{8,10},{9,11},{10,... | collective-permute-start | bytes 786440 | tf_op jit(solution)/shard_map/ppermute | solution.py:347
  10.4 24.5 %collective-permute-start.4 = (bf16[1,64,2048]{2,1,0:T(8,128)(2,1)S(1)}, bf16[1,64,2048]{2,1,0:T(8,128)(2,1)S(1)}, u32[]{:S(2)}, u32[]{:S(2)}) collective-permute-start(bf16[1,64,2048]{2,1,0:T(8,128)(2,1)S(1)} %get-tuple-element.27), channel_id=1, source_target_pairs={{0,1},{1,0},{2,3},{3,2},{4,5},{5,4},{6,7},{7,6},{8,9},{9,8},{10,11... | collective-permute-start | bytes 786440 | tf_op jit(solution)/shard_map/ppermute | solution.py:347
  12.0 23.3 %collective-permute-start.5 = (bf16[1,64,2048]{2,1,0:T(8,128)(2,1)S(1)}, bf16[1,64,2048]{2,1,0:T(8,128)(2,1)S(1)}, u32[]{:S(2)}, u32[]{:S(2)}) collective-permute-start(bf16[1,64,2048]{2,1,0:T(8,128)(2,1)S(1)} %get-tuple-element.28), channel_id=1, source_target_pairs={{0,6},{1,7},{2,0},{3,1},{4,2},{5,3},{6,4},{7,5},{8,14},{9,15},{10,... | collective-permute-start | bytes 786440 | tf_op jit(solution)/shard_map/ppermute | solution.py:347
  14.2 33.3 %collective-permute-start.6 = (bf16[1,64,2048]{2,1,0:T(8,128)(2,1)S(1)}, bf16[1,64,2048]{2,1,0:T(8,128)(2,1)S(1)}, u32[]{:S(2)}, u32[]{:S(2)}) collective-permute-start(bf16[1,64,2048]{2,1,0:T(8,128)(2,1)S(1)} %get-tuple-element.29), channel_id=1, source_target_pairs={{0,5},{1,4},{2,7},{3,6},{4,1},{5,0},{6,3},{7,2},{8,13},{9,12},{10,... | collective-permute-start | bytes 786440 | tf_op jit(solution)/shard_map/ppermute | solution.py:347
  16.0 36.1 %collective-permute-start.7 = (bf16[1,64,2048]{2,1,0:T(8,128)(2,1)S(1)}, bf16[1,64,2048]{2,1,0:T(8,128)(2,1)S(1)}, u32[]{:S(2)}, u32[]{:S(2)}) collective-permute-start(bf16[1,64,2048]{2,1,0:T(8,128)(2,1)S(1)} %get-tuple-element.31), channel_id=1, source_target_pairs={{0,4},{1,5},{2,6},{3,7},{4,0},{5,1},{6,2},{7,3},{8,12},{9,13},{10,... | collective-permute-start | bytes 786440 | tf_op jit(solution)/shard_map/ppermute | solution.py:347
  18.7 33.5 %collective-permute-start.8 = (bf16[1,64,2048]{2,1,0:T(8,128)(2,1)S(1)}, bf16[1,64,2048]{2,1,0:T(8,128)(2,1)S(1)}, u32[]{:S(2)}, u32[]{:S(2)}) collective-permute-start(bf16[1,64,2048]{2,1,0:T(8,128)(2,1)S(1)} %get-tuple-element.32), channel_id=1, source_target_pairs={{0,3},{1,2},{2,5},{3,4},{4,7},{5,6},{6,1},{7,0},{8,11},{9,10},{10,... | collective-permute-start | bytes 786440 | tf_op jit(solution)/shard_map/ppermute | solution.py:347
  34.9 20.9 %collective-permute-start.9 = (bf16[1,64,2048]{2,1,0:T(8,128)(2,1)S(1)}, bf16[1,64,2048]{2,1,0:T(8,128)(2,1)S(1)}, u32[]{:S(2)}, u32[]{:S(2)}) collective-permute-start(bf16[1,64,2048]{2,1,0:T(8,128)(2,1)S(1)} %get-tuple-element.33), channel_id=1, source_target_pairs={{0,7},{1,6},{2,1},{3,0},{4,3},{5,2},{6,5},{7,4},{8,15},{9,14},{10,... | collective-permute-start | bytes 786440 | tf_op jit(solution)/shard_map/ppermute | solution.py:347
  56.7 1.6 %collective-permute-start.10 = (f32[8,32,256]{2,1,0:T(8,128)S(1)}, f32[8,32,256]{2,1,0:T(8,128)S(1)}, u32[]{:S(2)}, u32[]{:S(2)}) collective-permute-start(f32[8,32,256]{2,1,0:T(8,128)S(1)} %get-tuple-element.36), channel_id=1, source_target_pairs={{0,8},{8,0},{16,24},{24,16},{1,9},{9,1},{17,25},{25,17},{2,10},{10... | collective-permute-start | bytes 786440 | tf_op jit(solution)/shard_map/ppermute | solution.py:296
  71.0 4.0 %collective-permute-start.13 = (f32[32,256]{1,0:T(8,128)S(1)}, f32[32,256]{1,0:T(8,128)S(1)}, u32[]{:S(2)}, u32[]{:S(2)}) collective-permute-start(f32[32,256]{1,0:T(8,128)S(1)} %fusion), channel_id=1, source_target_pairs={{0,16},{8,24},{16,0},{24,8},{1,17},{9,25},{17,1},{25,9},{2,18},{10... | collective-permute-start | bytes 98312 | tf_op jit(solution)/shard_map/ppermute | solution.py:296
  72.2 3.4 %collective-permute-start.12 = (f32[32,256]{1,0:T(8,128)S(1)}, f32[32,256]{1,0:T(8,128)S(1)}, u32[]{:S(2)}, u32[]{:S(2)}) collective-permute-start(f32[32,256]{1,0:T(8,128)S(1)} %fusion), channel_id=1, source_target_pairs={{0,24},{8,16},{16,8},{24,0},{1,25},{9,17},{17,9},{25,1},{2,26},{10... | collective-permute-start | bytes 98312 | tf_op jit(solution)/shard_map/ppermute | solution.py:296
  72.2 3.4 %collective-permute-start.11 = (f32[32,256]{1,0:T(8,128)S(1)}, f32[32,256]{1,0:T(8,128)S(1)}, u32[]{:S(2)}, u32[]{:S(2)}) collective-permute-start(f32[32,256]{1,0:T(8,128)S(1)} %fusion), channel_id=1, source_target_pairs={{0,8},{8,0},{16,24},{24,16},{1,9},{9,1},{17,25},{25,17},{2,10},{10... | collective-permute-start | bytes 98312 | tf_op jit(solution)/shard_map/ppermute | solution.py:296

commit v10 on v9

--- a/solution.py
+++ b/solution.py
@@ -273,7 +273,7 @@
     )
     send, columns = pl.pallas_call(
         functools.partial(
-            send_kernel, fit_scale, mix_scale, min(512, cols), width, ids, len(early), len(late)
+            send_kernel, fit_scale, mix_scale, cols, width, ids, len(early), len(late)
         ),
         out_shape=[half, jax.ShapeDtypeStruct((norb, cols), jnp.bfloat16)],
         in_specs=[pl.BlockSpec(memory_space=pltpu.VMEM)] * (len(fitted) + len(rows)),
@@ -346,7 +346,7 @@
                 return x
             return lax.ppermute(x, "grid", [(i, target(i, move)) for i in range(grid_size)])
 
-        waves, late_moves = [[(1, 0)], [(0, 0), (0, 1), (3, 0), (2, 1)], [(2, 0), (1, 1), (3, 1)]], [(2, 0), (1, 1), (3, 1)]
+        waves, late_moves = [[(1, 0)], [(0, 0), (3, 0), (2, 0)], [(2, 1), (3, 1), (1, 1), (0, 1)]], [(2, 1), (3, 1), (1, 1), (0, 1)]
         full, turned, made = contract_first(
             starts(waves[0]), None, [(2 * SUB, tiles.shape[4])], block, inside, parts, plain=True
         )

time: 76.5 us -> 76.5 us (level)
  starting transfers between devices: 30 us -> 36.6 us
  waiting for transfers between devices: 24.9 us -> 18.6 us
    ppermute x7, starting transfers between devices: 24.6 us -> 31.2 us  [moved(): lax.ppermute(x, 'grid', [(i, target(i, move)) for i in range(grid_size)])]
    ppermute x7, waiting for transfers between devices: 20.2 us -> 13.9 us  [moved(): lax.ppermute(x, 'grid', [(i, target(i, move)) for i in range(grid_size)])]
  transfers between devices with their start and end apart: 14 -> 14, of which waited for: 8 -> 6; matrix products, arithmetic and copies ran while one was open for 0% -> 0% of each run, Pallas kernels for 7% -> 7%
where the time goes in v10:
time: 76.5 us; the launch traced here: 76.3 us
  starting transfers between devices  36.6 us (48%)
  waiting for transfers between devices  18.6 us (24%)
  blocking collectives  12.4 us (16%)
  Pallas kernels  6.99 us (9%)
  other arithmetic  0.84 us (1%)
  between operations  0.81 us (1%)
    ppermute x7, starting transfers between devices, moved(): lax.ppermute(x, 'grid', [(i, target(i, move)) for i in range(grid_size)])  31.2 us
    ppermute x7, waiting for transfers between devices, moved(): lax.ppermute(x, 'grid', [(i, target(i, move)) for i in range(grid_size)])  13.9 us
    all_to_all x1, blocking collectives, summed_blocks(): lax.all_to_all(jnp.concatenate([scaled, tail], axis=1), axis, 0, 0, tiled...  12.4 us
    ppermute x7, starting transfers between devices, swapped(): lax.ppermute(x, axis, [(i, i ^ k) for i in range(lax.axis_size(axis))])  5.44 us
    ppermute x7, waiting for transfers between devices, swapped(): lax.ppermute(x, axis, [(i, i ^ k) for i in range(lax.axis_size(axis))])  4.7 us
    pallas_call x2, Pallas kernels, contract_next(): pl.pallas_call(functools.partial(next_kernel, group_starts, place), out_s...  2.08 us
    pallas_call x1, Pallas kernels, load(): pl.pallas_call(load_kernel, out_shape=[jax.ShapeDtypeStruct(tiles.shape[2...  1.91 us
  transfers between devices with their start and end apart: 14, of which 6 were waited for; matrix products, arithmetic and copies ran while one was open for 0% of the time, Pallas kernels for 7%

profile of v10, /device:TPU:0, one launch (start us, length us, event | category | flops | bytes accessed | tf_op | source)
XLA Modules:
  0.0 76.3 jit_solution(5703634904742563121)
XLA Ops:
  0.0 0.0 copy-start
  0.0 3.0 %collective-permute-start.1 = (bf16[128,256]{1,0:T(8,128)(2,1)}, bf16[128,256]{1,0:T(8,128)(2,1)S(1)}, u32[]{:S(2)}, u32[]{:S(2)}) collective-permute-start(bf16[128,256]{1,0:T(8,128)(2,1)} %refs_0_.1), channel_id=1, source_target_pairs={{0,16},{8,24},{16,0},{24,8},{1,17},{9,25},{17,1},{25,9},{2,18},{10... | collective-permute-start | bytes 196616 | tf_op jit(solution)/shard_map/ppermute | solution.py:296
  3.0 0.0 collective-permute-start
  3.0 0.2 collective-permute-start.2
  3.8 1.9 %shard_map.46 = (bf16[6,64,4096]{2,1,0:T(8,128)(2,1)S(1)}, s32[1,6]{1,0:T(1,128)S(1)}) custom-call(s32[1,1]{1,0:T(1,128)S(6)} %copy.8.count_ref, s32[1,1,6]{2,1,0:T(1,128)} %block_hbm.1, bf16[1,1,6,64,4096]{4,3,2,1,0:T(8,128)(2,1)} %tiles_hbm.1), custom_call_target="tpu_custom_call" | custom-call | bytes 3145728 | tf_op jit(solution)/shard_map/pallas_call | solution.py:41
  5.7 0.0 collective-permute-done.1.refs_2_
  5.7 0.0 collective-permute-done.refs_1_
  5.8 1.2 %collective-permute-done.2.refs_3_ = bf16[128,256]{1,0:T(8,128)(2,1)S(1)} collective-permute-done((bf16[128,256]{1,0:T(8,128)(2,1)}, bf16[128,256]{1,0:T(8,128)(2,1)S(1)}, u32[]{:S(2)}, u32[]{:S(2)}) %collective-permute-start.2) | collective-permute-done | bytes 65568 | tf_op jit(solution)/shard_map/ppermute | solution.py:296
  6.9 0.0 copy-done
  6.9 0.8 %shard_map.47 = (bf16[512,256]{1,0:T(8,128)(2,1)S(1)}, bf16[256,384]{1,0:T(8,128)(2,1)S(1)}, bf16[32,4096]{1,0:T(8,128)(2,1)S(1)}) custom-call(s32[1,6]{1,0:T(1,128)S(1)} %get-tuple-element.21.block_ref, bf16[6,64,4096]{2,1,0:T(8,128)(2,1)S(1)} %get-tuple-element.22.tiles_ref, bf16[128,256]{1,0:T(8,128)(2,1)S(1)} %copy-done, ...), custom_call_target="tpu_custom_call" | custom-call | flops 100663296 | bytes 3407872 | tf_op jit(solution)/shard_map/pallas_call | solution.py:170
  7.8 1.6 %collective-permute-start.3 = (bf16[32,4096]{1,0:T(8,128)(2,1)S(1)}, bf16[32,4096]{1,0:T(8,128)(2,1)S(1)}, u32[]{:S(2)}, u32[]{:S(2)}) collective-permute-start(bf16[32,4096]{1,0:T(8,128)(2,1)S(1)} %get-tuple-element.24.skipped), channel_id=1, source_target_pairs={{0,2},{1,3},{2,4},{3,5},{4,6},{5,7},{6,0},{7,1},{8,10},{9,11},{10,... | collective-permute-start | bytes 786440 | tf_op jit(solution)/shard_map/ppermute | solution.py:347
  9.4 1.0 %shard_map.49 = (bf16[1,64,2048]{2,1,0:T(8,128)(2,1)S(1)}, bf16[1,64,2048]{2,1,0:T(8,128)(2,1)S(1)}, bf16[1,64,2048]{2,1,0:T(8,128)(2,1)S(1)}) custom-call(bf16[256,384]{1,0:T(8,128)(2,1)S(1)} %get-tuple-element.25.turned_ref, bf16[6,64,4096]{2,1,0:T(8,128)(2,1)S(1)} %get-tuple-element.22.tiles_ref, bf16[32,4096]{1,0:T(8,128)(2,1)S(1)} %get-tuple-element.24.skipped), custom_call_target="tpu_custom_call" | custom-call | flops 301989888 | bytes 3932160 | tf_op jit(solution)/shard_map/pallas_call | solution.py:183
  10.4 2.3 %collective-permute-start.4 = (bf16[1,64,2048]{2,1,0:T(8,128)(2,1)S(1)}, bf16[1,64,2048]{2,1,0:T(8,128)(2,1)S(1)}, u32[]{:S(2)}, u32[]{:S(2)}) collective-permute-start(bf16[1,64,2048]{2,1,0:T(8,128)(2,1)S(1)} %get-tuple-element.27), channel_id=1, source_target_pairs={{0,6},{1,7},{2,0},{3,1},{4,2},{5,3},{6,4},{7,5},{8,14},{9,15},{10,... | collective-permute-start | bytes 786440 | tf_op jit(solution)/shard_map/ppermute | solution.py:347
  12.7 0.8 %collective-permute-start.5 = (bf16[1,64,2048]{2,1,0:T(8,128)(2,1)S(1)}, bf16[1,64,2048]{2,1,0:T(8,128)(2,1)S(1)}, u32[]{:S(2)}, u32[]{:S(2)}) collective-permute-start(bf16[1,64,2048]{2,1,0:T(8,128)(2,1)S(1)} %get-tuple-element.28), channel_id=1, source_target_pairs={{0,4},{1,5},{2,6},{3,7},{4,0},{5,1},{6,2},{7,3},{8,12},{9,13},{10,... | collective-permute-start | bytes 786440 | tf_op jit(solution)/shard_map/ppermute | solution.py:347
  13.5 1.0 %shard_map.51 = (bf16[1,64,2048]{2,1,0:T(8,128)(2,1)S(1)}, bf16[1,64,2048]{2,1,0:T(8,128)(2,1)S(1)}, bf16[1,64,2048]{2,1,0:T(8,128)(2,1)S(1)}, bf16[1,64,2048]{2,1,0:T(8,128)(2,1)S(1)}) custom-call(bf16[256,384]{1,0:T(8,128)(2,1)S(1)} %get-tuple-element.25.turned_ref, bf16[6,64,4096]{2,1,0:T(8,128)(2,1)S(1)} %get-tuple-element.22.tiles_ref, ...), custom_call_target="tpu_custom_call" | custom-call | flops 402653184 | bytes 4194304 | tf_op jit(solution)/shard_map/pallas_call | solution.py:183
  14.5 3.1 %collective-permute-start.6 = (bf16[1,64,2048]{2,1,0:T(8,128)(2,1)S(1)}, bf16[1,64,2048]{2,1,0:T(8,128)(2,1)S(1)}, u32[]{:S(2)}, u32[]{:S(2)}) collective-permute-start(bf16[1,64,2048]{2,1,0:T(8,128)(2,1)S(1)} %get-tuple-element.30), channel_id=1, source_target_pairs={{0,5},{1,4},{2,7},{3,6},{4,1},{5,0},{6,3},{7,2},{8,13},{9,12},{10,... | collective-permute-start | bytes 786440 | tf_op jit(solution)/shard_map/ppermute | solution.py:347
  17.7 1.8 %collective-permute-start.7 = (bf16[1,64,2048]{2,1,0:T(8,128)(2,1)S(1)}, bf16[1,64,2048]{2,1,0:T(8,128)(2,1)S(1)}, u32[]{:S(2)}, u32[]{:S(2)}) collective-permute-start(bf16[1,64,2048]{2,1,0:T(8,128)(2,1)S(1)} %get-tuple-element.31), channel_id=1, source_target_pairs={{0,7},{1,6},{2,1},{3,0},{4,3},{5,2},{6,5},{7,4},{8,15},{9,14},{10,... | collective-permute-start | bytes 786440 | tf_op jit(solution)/shard_map/ppermute | solution.py:347
  19.4 0.0 collective-permute-done.3.rows_ref
  19.4 21.1 %collective-permute-start.8 = (bf16[1,64,2048]{2,1,0:T(8,128)(2,1)S(1)}, bf16[1,64,2048]{2,1,0:T(8,128)(2,1)S(1)}, u32[]{:S(2)}, u32[]{:S(2)}) collective-permute-start(bf16[1,64,2048]{2,1,0:T(8,128)(2,1)S(1)} %get-tuple-element.32), channel_id=1, source_target_pairs={{0,3},{1,2},{2,5},{3,4},{4,7},{5,6},{6,1},{7,0},{8,11},{9,10},{10,... | collective-permute-start | bytes 786440 | tf_op jit(solution)/shard_map/ppermute | solution.py:347
  40.5 0.0 collective-permute-done.4.refs_2_
  40.5 0.5 collective-permute-start.9
  41.1 0.3 shard_map.48.refs_0_
  41.4 0.0 collective-permute-done.5.refs_3_
  41.4 0.5 shard_map.50
  41.9 11.2 %collective-permute-done.6.refs_4_ = bf16[1,64,2048]{2,1,0:T(8,128)(2,1)S(1)} collective-permute-done((bf16[1,64,2048]{2,1,0:T(8,128)(2,1)S(1)}, bf16[1,64,2048]{2,1,0:T(8,128)(2,1)S(1)}, u32[]{:S(2)}, u32[]{:S(2)}) %collective-permute-start.6) | collective-permute-done | bytes 262176 | tf_op jit(solution)/shard_map/ppermute | solution.py:347
  53.1 0.0 collective-permute-done.7.refs_5_
  53.1 0.0 collective-permute-done.8.refs_6_
  53.1 2.7 %collective-permute-done.9.refs_7_ = bf16[1,64,2048]{2,1,0:T(8,128)(2,1)S(1)} collective-permute-done((bf16[1,64,2048]{2,1,0:T(8,128)(2,1)S(1)}, bf16[1,64,2048]{2,1,0:T(8,128)(2,1)S(1)}, u32[]{:S(2)}, u32[]{:S(2)}) %collective-permute-start.9) | collective-permute-done | bytes 262176 | tf_op jit(solution)/shard_map/ppermute | solution.py:347
  55.8 0.9 %shard_map.52 = (f32[8,32,256]{2,1,0:T(8,128)S(1)}, bf16[256,2048]{1,0:T(8,128)(2,1)S(1)}) custom-call(f32[256,2048]{1,0:T(8,128)S(1)} %get-tuple-element.29.fitted_ref, bf16[1,64,2048]{2,1,0:T(8,128)(2,1)S(1)} %shard_map.48.refs_0_, bf16[1,64,2048]{2,1,0:T(8,128)(2,1)S(1)} %get-tuple-element.26.refs_1_.skipped, ...), custom_call_target="tpu_custom_call" | custom-call | flops 536870912 | bytes 2097152 | tf_op jit(solution)/shard_map/pallas_call | solution.py:274
  56.7 0.1 collective-permute-start.10
  56.8 0.5 shard_map.53
  57.2 1.0 %collective-permute-done.10 = f32[8,32,256]{2,1,0:T(8,128)S(1)} collective-permute-done((f32[8,32,256]{2,1,0:T(8,128)S(1)}, f32[8,32,256]{2,1,0:T(8,128)S(1)}, u32[]{:S(2)}, u32[]{:S(2)}) %collective-permute-start.10) | collective-permute-done | bytes 262176 | tf_op jit(solution)/shard_map/ppermute | solution.py:296
  58.5 12.4 %all_to_all.5 = f16[8,40,256]{2,1,0:T(8,128)(2,1)S(1)} all-to-all(f16[8,40,256]{2,1,0:T(8,128)(2,1)S(1)} %pad_maximum_fusion), channel_id=1, replica_groups=mesh['rep'=4,'grid'=8] {'grid'}, dimensions={0} | all-to-all | bytes 327680 | tf_op jit(solution)/shard_map/all_to_all | solution.py:305
  71.0 1.3 %collective-permute-start.13 = (f32[32,256]{1,0:T(8,128)S(1)}, f32[32,256]{1,0:T(8,128)S(1)}, u32[]{:S(2)}, u32[]{:S(2)}) collective-permute-start(f32[32,256]{1,0:T(8,128)S(1)} %fusion), channel_id=1, source_target_pairs={{0,16},{8,24},{16,0},{24,8},{1,17},{9,25},{17,1},{25,9},{2,18},{10... | collective-permute-start | bytes 98312 | tf_op jit(solution)/shard_map/ppermute | solution.py:296
  72.2 0.0 collective-permute-start.12
  72.2 0.9 %collective-permute-start.11 = (f32[32,256]{1,0:T(8,128)S(1)}, f32[32,256]{1,0:T(8,128)S(1)}, u32[]{:S(2)}, u32[]{:S(2)}) collective-permute-start(f32[32,256]{1,0:T(8,128)S(1)} %fusion), channel_id=1, source_target_pairs={{0,8},{8,0},{16,24},{24,16},{1,9},{9,1},{17,25},{25,17},{2,10},{10... | collective-permute-start | bytes 98312 | tf_op jit(solution)/shard_map/ppermute | solution.py:296
  73.2 1.8 %collective-permute-done.13 = f32[32,256]{1,0:T(8,128)S(1)} collective-permute-done((f32[32,256]{1,0:T(8,128)S(1)}, f32[32,256]{1,0:T(8,128)S(1)}, u32[]{:S(2)}, u32[]{:S(2)}) %collective-permute-start.13) | collective-permute-done | bytes 32800 | tf_op jit(solution)/shard_map/ppermute | solution.py:296
  75.0 0.7 collective-permute-done.12
  75.7 0.0 collective-permute-done.11
  75.7 0.6 pad_maximum_fusion.1
  (10 shorter events, 0.2 us)
Async XLA Ops:
  0.0 6.9 %copy-start = (bf16[128,256]{1,0:T(8,128)(2,1)S(1)}, bf16[128,256]{1,0:T(8,128)(2,1)}, u32[]{:S(2)}) copy-start(bf16[128,256]{1,0:T(8,128)(2,1)} %refs_0_.1) | copy-start | bytes 196612
  0.0 5.7 %collective-permute-start.1 = (bf16[128,256]{1,0:T(8,128)(2,1)}, bf16[128,256]{1,0:T(8,128)(2,1)S(1)}, u32[]{:S(2)}, u32[]{:S(2)}) collective-permute-start(bf16[128,256]{1,0:T(8,128)(2,1)} %refs_0_.1), channel_id=1, source_target_pairs={{0,16},{8,24},{16,0},{24,8},{1,17},{9,25},{17,1},{25,9},{2,18},{10... | collective-permute-start | bytes 196616 | tf_op jit(solution)/shard_map/ppermute | solution.py:296
  3.0 2.8 %collective-permute-start = (bf16[128,256]{1,0:T(8,128)(2,1)}, bf16[128,256]{1,0:T(8,128)(2,1)S(1)}, u32[]{:S(2)}, u32[]{:S(2)}) collective-permute-start(bf16[128,256]{1,0:T(8,128)(2,1)} %refs_0_.1), channel_id=1, source_target_pairs={{0,8},{8,0},{16,24},{24,16},{1,9},{9,1},{17,25},{25,17},{2,10},{10... | collective-permute-start | bytes 196616 | tf_op jit(solution)/shard_map/ppermute | solution.py:296
  3.0 4.0 %collective-permute-start.2 = (bf16[128,256]{1,0:T(8,128)(2,1)}, bf16[128,256]{1,0:T(8,128)(2,1)S(1)}, u32[]{:S(2)}, u32[]{:S(2)}) collective-permute-start(bf16[128,256]{1,0:T(8,128)(2,1)} %refs_0_.1), channel_id=1, source_target_pairs={{0,24},{8,16},{16,8},{24,0},{1,25},{9,17},{17,9},{25,1},{2,26},{10... | collective-permute-start | bytes 196616 | tf_op jit(solution)/shard_map/ppermute | solution.py:296
  7.8 11.7 %collective-permute-start.3 = (bf16[32,4096]{1,0:T(8,128)(2,1)S(1)}, bf16[32,4096]{1,0:T(8,128)(2,1)S(1)}, u32[]{:S(2)}, u32[]{:S(2)}) collective-permute-start(bf16[32,4096]{1,0:T(8,128)(2,1)S(1)} %get-tuple-element.24.skipped), channel_id=1, source_target_pairs={{0,2},{1,3},{2,4},{3,5},{4,6},{5,7},{6,0},{7,1},{8,10},{9,11},{10,... | collective-permute-start | bytes 786440 | tf_op jit(solution)/shard_map/ppermute | solution.py:347
  10.4 30.1 %collective-permute-start.4 = (bf16[1,64,2048]{2,1,0:T(8,128)(2,1)S(1)}, bf16[1,64,2048]{2,1,0:T(8,128)(2,1)S(1)}, u32[]{:S(2)}, u32[]{:S(2)}) collective-permute-start(bf16[1,64,2048]{2,1,0:T(8,128)(2,1)S(1)} %get-tuple-element.27), channel_id=1, source_target_pairs={{0,6},{1,7},{2,0},{3,1},{4,2},{5,3},{6,4},{7,5},{8,14},{9,15},{10,... | collective-permute-start | bytes 786440 | tf_op jit(solution)/shard_map/ppermute | solution.py:347
  12.7 28.7 %collective-permute-start.5 = (bf16[1,64,2048]{2,1,0:T(8,128)(2,1)S(1)}, bf16[1,64,2048]{2,1,0:T(8,128)(2,1)S(1)}, u32[]{:S(2)}, u32[]{:S(2)}) collective-permute-start(bf16[1,64,2048]{2,1,0:T(8,128)(2,1)S(1)} %get-tuple-element.28), channel_id=1, source_target_pairs={{0,4},{1,5},{2,6},{3,7},{4,0},{5,1},{6,2},{7,3},{8,12},{9,13},{10,... | collective-permute-start | bytes 786440 | tf_op jit(solution)/shard_map/ppermute | solution.py:347
  14.5 38.5 %collective-permute-start.6 = (bf16[1,64,2048]{2,1,0:T(8,128)(2,1)S(1)}, bf16[1,64,2048]{2,1,0:T(8,128)(2,1)S(1)}, u32[]{:S(2)}, u32[]{:S(2)}) collective-permute-start(bf16[1,64,2048]{2,1,0:T(8,128)(2,1)S(1)} %get-tuple-element.30), channel_id=1, source_target_pairs={{0,5},{1,4},{2,7},{3,6},{4,1},{5,0},{6,3},{7,2},{8,13},{9,12},{10,... | collective-permute-start | bytes 786440 | tf_op jit(solution)/shard_map/ppermute | solution.py:347
  17.7 35.4 %collective-permute-start.7 = (bf16[1,64,2048]{2,1,0:T(8,128)(2,1)S(1)}, bf16[1,64,2048]{2,1,0:T(8,128)(2,1)S(1)}, u32[]{:S(2)}, u32[]{:S(2)}) collective-permute-start(bf16[1,64,2048]{2,1,0:T(8,128)(2,1)S(1)} %get-tuple-element.31), channel_id=1, source_target_pairs={{0,7},{1,6},{2,1},{3,0},{4,3},{5,2},{6,5},{7,4},{8,15},{9,14},{10,... | collective-permute-start | bytes 786440 | tf_op jit(solution)/shard_map/ppermute | solution.py:347
  19.4 33.6 %collective-permute-start.8 = (bf16[1,64,2048]{2,1,0:T(8,128)(2,1)S(1)}, bf16[1,64,2048]{2,1,0:T(8,128)(2,1)S(1)}, u32[]{:S(2)}, u32[]{:S(2)}) collective-permute-start(bf16[1,64,2048]{2,1,0:T(8,128)(2,1)S(1)} %get-tuple-element.32), channel_id=1, source_target_pairs={{0,3},{1,2},{2,5},{3,4},{4,7},{5,6},{6,1},{7,0},{8,11},{9,10},{10,... | collective-permute-start | bytes 786440 | tf_op jit(solution)/shard_map/ppermute | solution.py:347
  40.5 15.2 %collective-permute-start.9 = (bf16[1,64,2048]{2,1,0:T(8,128)(2,1)S(1)}, bf16[1,64,2048]{2,1,0:T(8,128)(2,1)S(1)}, u32[]{:S(2)}, u32[]{:S(2)}) collective-permute-start(bf16[1,64,2048]{2,1,0:T(8,128)(2,1)S(1)} %get-tuple-element.33), channel_id=1, source_target_pairs={{0,1},{1,0},{2,3},{3,2},{4,5},{5,4},{6,7},{7,6},{8,9},{9,8},{10,11... | collective-permute-start | bytes 786440 | tf_op jit(solution)/shard_map/ppermute | solution.py:347
  56.7 1.6 %collective-permute-start.10 = (f32[8,32,256]{2,1,0:T(8,128)S(1)}, f32[8,32,256]{2,1,0:T(8,128)S(1)}, u32[]{:S(2)}, u32[]{:S(2)}) collective-permute-start(f32[8,32,256]{2,1,0:T(8,128)S(1)} %get-tuple-element.36), channel_id=1, source_target_pairs={{0,8},{8,0},{16,24},{24,16},{1,9},{9,1},{17,25},{25,17},{2,10},{10... | collective-permute-start | bytes 786440 | tf_op jit(solution)/shard_map/ppermute | solution.py:296
  71.0 4.0 %collective-permute-start.13 = (f32[32,256]{1,0:T(8,128)S(1)}, f32[32,256]{1,0:T(8,128)S(1)}, u32[]{:S(2)}, u32[]{:S(2)}) collective-permute-start(f32[32,256]{1,0:T(8,128)S(1)} %fusion), channel_id=1, source_target_pairs={{0,16},{8,24},{16,0},{24,8},{1,17},{9,25},{17,1},{25,9},{2,18},{10... | collective-permute-start | bytes 98312 | tf_op jit(solution)/shard_map/ppermute | solution.py:296
  72.2 3.4 %collective-permute-start.12 = (f32[32,256]{1,0:T(8,128)S(1)}, f32[32,256]{1,0:T(8,128)S(1)}, u32[]{:S(2)}, u32[]{:S(2)}) collective-permute-start(f32[32,256]{1,0:T(8,128)S(1)} %fusion), channel_id=1, source_target_pairs={{0,24},{8,16},{16,8},{24,0},{1,25},{9,17},{17,9},{25,1},{2,26},{10... | collective-permute-start | bytes 98312 | tf_op jit(solution)/shard_map/ppermute | solution.py:296
  72.2 3.4 %collective-permute-start.11 = (f32[32,256]{1,0:T(8,128)S(1)}, f32[32,256]{1,0:T(8,128)S(1)}, u32[]{:S(2)}, u32[]{:S(2)}) collective-permute-start(f32[32,256]{1,0:T(8,128)S(1)} %fusion), channel_id=1, source_target_pairs={{0,8},{8,0},{16,24},{24,16},{1,9},{9,1},{17,25},{25,17},{2,10},{10... | collective-permute-start | bytes 98312 | tf_op jit(solution)/shard_map/ppermute | solution.py:296
